TPU v7x, 256 devices: a whole 4x4x8 slice. The times are simulated.
256 devices in a mesh: ctx: 16 (over x, y), head: 8 (over z), fsdp: 2 (over core).
Axes of the slice: x: 4, y: 4, z: 8, core: 2. Of those that a mesh axis runs over, the one named last changes fastest.
Arguments:
- layer_input: bfloat16 [16384, 4096], P(('ctx', 'fsdp')), may hold values from -6 to 6
- query_act: bfloat16 [16384, 4096], P(('ctx', 'fsdp'), 'head'), may hold values from -6 to 6
- key_act: bfloat16 [16384, 4096], P(('ctx', 'fsdp'), 'head'), may hold values from -6 to 6
- out_grad: bfloat16 [16384, 4096], P(('ctx', 'fsdp'), 'head'), may hold values from -6 to 6
- value_weight: bfloat16 [4096, 4096], P('fsdp', 'head'), may hold values from -0.09375 to 0.09375
Outputs:
- query_grad: bfloat16 [16384, 4096], P(('ctx', 'fsdp'), 'head')
- key_grad: bfloat16 [16384, 4096], P(('ctx', 'fsdp'), 'head')
- input_grad: bfloat16 [16384, 4096], P(('ctx', 'fsdp'), 'head')
- weight_grad: float32 [4096, 4096], P(('ctx', 'fsdp'), 'head')
All inputs are finite; a program needn't handle non-finite values.
Results may differ from a plain program's by a relative error of at most 0.018.
Values may be sent and summed in bfloat16 or wider, within the bound.
No kernel may reach another device: no remote copies, remote signals or barrier semaphores. Data moves between devices by JAX's collectives and lax.ppermute only.
A program may use at most 64 MiB of HBM per device.

v0:
```python
import math

import jax
import jax.numpy as jnp
from jax import lax
from jax.experimental import pallas as pl
from jax.experimental.pallas import tpu as pltpu
from jax.sharding import PartitionSpec as P

HDIM = 128
SIDE = 4
RING = 8
F32 = jnp.float32
BF16 = jnp.bfloat16
NT = (((1,), (1,)), ((), ()))
TN = (((0,), (0,)), ((), ()))
NN = (((1,), (0,)), ((), ()))

VMEM = pl.BlockSpec(memory_space=pltpu.VMEM)
ANY = pl.BlockSpec(memory_space=pl.ANY)
HBM = pl.BlockSpec(memory_space=pltpu.HBM)


def dot(a, b, dims=NN):
    return lax.dot_general(a, b, dims, preferred_element_type=F32)


def sds(shape, dtype=BF16):
    return jax.ShapeDtypeStruct(shape, dtype)


def core():
    return lax.axis_index("fsdp")


def place():
    at = lax.axis_index("ctx")
    return at // SIDE, lax.rem(at, SIDE)


def dest(which):
    i = which - 1
    hop = jnp.where(i % 2 == 0, 3 - i // 2, 5 + i // 2)
    return lax.rem(lax.axis_index("head") + hop, RING)


def wide(ref):
    return ref[...].astype(F32)


def call(body, specs, ins, outs, name, scratch=(), limit=16):
    return pl.pallas_call(
        body,
        out_shape=tuple(outs),
        in_specs=specs,
        out_specs=tuple([VMEM] * len(outs)),
        scratch_shapes=list(scratch),
        compiler_params=pltpu.CompilerParams(vmem_limit_bytes=limit * 2**20),
        cost_estimate=pl.CostEstimate(
            flops=1000,
            bytes_accessed=sum(a.size * a.dtype.itemsize for a in ins)
            + sum(math.prod(o.shape) * o.dtype.itemsize for o in outs),
            transcendentals=0,
        ),
        name=name,
    )(*ins)


def in_hbm(a):
    return pltpu.with_memory_space_constraint(a, pltpu.HBM)


def heads_of(ref):
    return [slice(h, h + HDIM) for h in range(0, ref.shape[1], HDIM)]


def each_head(ref, body):
    @pl.loop(0, ref.shape[1] // HDIM)
    def _(h):
        at = pl.multiple_of(h * HDIM, HDIM)
        body(pl.ds(at, HDIM))


def tril(scores):
    rows = lax.broadcasted_iota(jnp.int32, scores.shape, 0)
    cols = lax.broadcasted_iota(jnp.int32, scores.shape, 1)
    return jnp.where(rows >= cols, scores, 0.0).astype(BF16)


def value_own_kernel(x_hbm, w_hbm, x_ref, part_ref, w_ref, sems):
    step = 512
    n = x_hbm.shape[1] // step
    half = n // 2

    def x_cols(j):
        return pl.ds(pl.multiple_of(lax.rem(core() * half + j, n) * step, step), step)

    xs = [
        pltpu.make_async_copy(x_hbm.at[:, x_cols(j)], x_ref.at[:, x_cols(j)], sems.at[j])
        for j in range(n)
    ]
    ws = [
        pltpu.make_async_copy(
            w_hbm.at[pl.ds(j * step, step), :], w_ref.at[pl.ds(j * step, step), :], sems.at[n + j]
        )
        for j in range(half)
    ]
    for j in range(half):
        ws[j].start()
        xs[j].start()
    for j in range(half, n):
        xs[j].start()
    part_ref[...] = jnp.zeros_like(part_ref)

    @pl.loop(0, half)
    def _(j):
        rows = pl.ds(pl.multiple_of(j * step, step), step)
        pltpu.make_async_copy(w_hbm.at[rows, :], w_ref.at[rows, :], sems.at[n + j]).wait()
        pltpu.make_async_copy(
            x_hbm.at[:, x_cols(j)], x_ref.at[:, x_cols(j)], sems.at[j]
        ).wait()
        part_ref[...] += dot(x_ref[:, x_cols(j)], w_ref[rows, :])

    for j in range(half, n):
        xs[j].wait()


def split(rows, keep_ref, give_ref):
    half = keep_ref.shape[0]
    for h, state in enumerate(rows):
        to = (h * HDIM) // half

        @pl.when(core() == to)
        def _():
            keep_ref[h * HDIM - to * half : (h + 1) * HDIM - to * half, :] = state

        @pl.when(core() != to)
        def _():
            give_ref[h * HDIM - to * half : (h + 1) * HDIM - to * half, :] = state


def join(near_ref, far_ref, state_ref):
    half = near_ref.shape[0]
    mine = pl.ds(pl.multiple_of(core() * half, half), half)
    other = pl.ds(pl.multiple_of((1 - core()) * half, half), half)
    state_ref[mine, :] = near_ref[...].astype(BF16)
    state_ref[other, :] = far_ref[...]


def value_rest_kernel(x_ref, w_ref, part_ref, k_ref, v_ref, keep_ref, give_ref):
    rows = w_ref.shape[0]
    cols = pl.ds(pl.multiple_of((1 - core()) * rows, rows), rows)
    v = (part_ref[...] + dot(x_ref[:, cols], w_ref[...])).astype(BF16)
    v_ref[...] = v
    pairs = [dot(k_ref[:, c], v[:, c], TN).astype(BF16) for c in heads_of(v_ref)]
    split(pairs, keep_ref, give_ref)


def inside_kernel(q_ref, k_ref, v_ref, a_ref):
    def head(c):
        a_ref[:, c] = dot(tril(dot(q_ref[:, c], k_ref[:, c], NT)), v_ref[:, c])

    each_head(q_ref, head)


def norm_kernel(q_ref, g_ref, a_ref, near_ref, far_ref, low_ref, state_ref, keep_ref, give_ref):
    join(near_ref, far_ref, state_ref)
    local = []
    for c in heads_of(q_ref):
        att = a_ref[:, c] + dot(q_ref[:, c], state_ref[c, :])
        inv = lax.rsqrt(jnp.mean(att * att, axis=-1, keepdims=True) + 1e-05)
        normed = att * inv
        g = g_ref[:, c].astype(F32)
        low = (inv * (g - normed * jnp.mean(g * normed, axis=-1, keepdims=True))).astype(BF16)
        low_ref[:, c] = low
        local.append(dot(q_ref[:, c], low, TN).astype(BF16))
    split(local, keep_ref, give_ref)


def cross_kernel(q_ref, k_ref, v_ref, low_ref, state_ref, vp_ref, kp_ref, qg_ref):
    def head(c):
        q, k, low = q_ref[:, c], k_ref[:, c], low_ref[:, c]
        cross = tril(dot(low, v_ref[:, c], NT))
        qg_ref[:, c] = (dot(cross, k) + dot(low, state_ref[c, :], NT)).astype(BF16)
        kp_ref[:, c] = dot(cross, q, TN)
        vp_ref[:, c] = dot(tril(dot(q, k, NT)), low, TN)

    each_head(q_ref, head)


def chip_sum_kernel(keep_ref, got_ref, _, t_ref):
    t_ref[...] = (wide(keep_ref) + wide(got_ref)).astype(BF16)


def pair_sum_kernel(a_ref, b_ref, _, t_ref):
    t_ref[...] = (wide(a_ref) + wide(b_ref)).astype(BF16)


def part_before(sign, at, beside, across):
    if sign == -1:
        at = SIDE - 1 - at
    return jnp.where(at % 2 == 1, beside, 0.0) + jnp.where(at >= SIDE // 2, across, 0.0)


def last_sum_kernel(sign, keep_ref, got_ref, y1, y2, x1, x2, near_ref, far_ref):
    x, y = place()
    before = part_before(sign, y, wide(y1), wide(y2)) + part_before(sign, x, wide(x1), wide(x2))
    lead = core() == (0 if sign == 1 else 1)
    near_ref[...] = jnp.where(lead, before, before + wide(got_ref))
    far_ref[...] = jnp.where(lead, before + wide(keep_ref), before).astype(BF16)


def along(a, axis, beside):
    def other(i):
        x, y = i // SIDE, i % SIDE
        if axis == "x":
            x = x ^ 1 if beside else SIDE - 1 - x
        else:
            y = y ^ 1 if beside else SIDE - 1 - y
        return x * SIDE + y

    return lax.ppermute(a, "ctx", [(i, other(i)) for i in range(SIDE * SIDE)])


def along_x_ring(a, k):
    return lax.ppermute(a, "ctx", [(i, (i + SIDE * k) % 16) for i in range(16)])


def along_y_ring(a, k):
    return lax.ppermute(
        a, "ctx", [(i, i // SIDE * SIDE + (i + k) % SIDE) for i in range(16)]
    )


def along_z(a, k):
    return lax.ppermute(a, "head", [(i, (i + k) % RING) for i in range(RING)])


def swap(a):
    return lax.ppermute(a, "fsdp", [(0, 1), (1, 0)])


def exclusive(keep, give, sign, work):
    shape = sds(keep.shape)

    def fold(kernel, *arrays):
        (t,) = call(kernel, [VMEM] * len(arrays), arrays, [shape], "fold")
        return t

    got = swap(give)
    t = fold(chip_sum_kernel, keep, got, keep)
    y1 = along(t, "y", True)
    done = work()
    t = fold(pair_sum_kernel, t, y1, done[0])
    y2 = along(t, "y", False)
    t = fold(pair_sum_kernel, t, y2, done[0])
    x1 = along(t, "x", True)
    t = fold(pair_sum_kernel, t, x1, done[0])
    x2 = along(t, "x", False)
    near, far = call(
        lambda *refs: last_sum_kernel(sign, *refs),
        [VMEM] * 6,
        [keep, got, y1, y2, x1, x2],
        [sds(keep.shape, F32), shape],
        "last_sum",
    )
    return near, swap(far), done


def chunk_product(which, vg, own_ref, other_ref, use):
    rows = pl.ds(pl.multiple_of(lax.rem(dest(which), RING // 2) * 512, 512), 512)
    mine = dest(which) // (RING // 2) == core()

    @pl.when(mine)
    def _():
        use(dot(vg, own_ref[rows, :], NT).astype(BF16))

    @pl.when(jnp.logical_not(mine))
    def _():
        use(dot(vg, other_ref[rows, :], NT).astype(BF16))


def first_kernel(scale, k_ref, vp_ref, near_ref, far_ref, own_ref, other_ref, x_ref, vg_ref, state_ref, right_ref, left_ref, piece_ref):
    join(near_ref, far_ref, state_ref)
    for c in heads_of(k_ref):
        vg_ref[:, c] = (vp_ref[:, c] + dot(k_ref[:, c], state_ref[c, :])).astype(BF16)
    half = right_ref.shape[0]

    def use(p):
        right_ref[...] = p[:half]
        left_ref[...] = p[half:]

    chunk_product(0, vg_ref[...], own_ref, other_ref, use)
    weight_pieces(scale, 1 - core(), vg_ref, x_ref, piece_ref)


def work_kernel(scale, vg_ref, own_ref, other_ref, x_ref, p_ref, piece_ref):
    @pl.loop(0, p_ref.shape[0])
    def _(i):
        def use(p):
            p_ref[i] = p

        chunk_product(1 + i, vg_ref[...], own_ref, other_ref, use)
    weight_pieces(scale, core(), vg_ref, x_ref, piece_ref)


def open_turn_kernel(r_ref, l_ref, p_ref, ro_ref, lo_ref):
    half = r_ref.shape[0]
    ro_ref[:half] = (wide(r_ref) + p_ref[0, :half].astype(F32)).astype(BF16)
    ro_ref[half:] = p_ref[0, half:]
    lo_ref[:half] = p_ref[1, :half]
    lo_ref[half:] = (wide(l_ref) + p_ref[1, half:].astype(F32)).astype(BF16)


def turn(first, r_ref, l_ref, p_ref, ro_ref, lo_ref):
    ro_ref[...] = (wide(r_ref) + p_ref[first].astype(F32)).astype(BF16)
    lo_ref[...] = (wide(l_ref) + p_ref[first + 1].astype(F32)).astype(BF16)


def last_turn_kernel(r_ref, l_ref, p_ref, o_ref):
    o_ref[...] = (p_ref[p_ref.shape[0] - 1].astype(F32) + wide(r_ref) + wide(l_ref)).astype(BF16)


def key_grad_kernel(v_ref, kp_ref, state_ref, _, kg_ref):
    def head(c):
        kg_ref[:, c] = (kp_ref[:, c] + dot(v_ref[:, c], state_ref[c, :], NT)).astype(BF16)

    each_head(v_ref, head)


def weight_pieces(scale, side, vg_ref, x_ref, o_ref):
    turned = vg_ref[...].T
    shift = side * 128

    @pl.loop(0, o_ref.shape[0] // 4)
    def _(group):
        first = group * 4
        x = jnp.concatenate(
            [
                x_ref[:, pl.ds(pl.multiple_of((first + p) * 256 + shift, 128), 128)]
                for p in range(4)
            ],
            axis=1,
        )
        res = (dot(turned, x) * scale).astype(BF16)
        for p in range(4):
            o_ref[first + p] = res[:, p * 128 : p * 128 + 128]


def chip_kernel(a_ref, b_ref, _, ru2, lv2, rv1, lu1, cu1, cv1, own):
    half = own.shape[1] // 2

    x, _ = place()

    def s(hop):
        i = lax.rem(x + hop, SIDE)
        return (a_ref[i].astype(F32) + b_ref[i].astype(F32)).astype(BF16)

    t = s(2)
    ru2[...] = t[:, :half]
    lv2[...] = t[:, half:]
    t = s(1)
    cu1[...] = t[:, :half]
    rv1[...] = t[:, half:]
    t = s(3)
    lu1[...] = t[:, :half]
    cv1[...] = t[:, half:]
    own[...] = s(0)


def pair_kernel(r_ref, l_ref, p_ref, a_ref, b_ref, c_ref, d_ref, _, ro_ref, lo_ref, o_ref, q_ref):
    turn(2, r_ref, l_ref, p_ref, ro_ref, lo_ref)
    o_ref[...] = (wide(a_ref) + wide(b_ref)).astype(BF16)
    q_ref[...] = (wide(c_ref) + wide(d_ref)).astype(BF16)


def line_kernel(r_ref, l_ref, p_ref, own_ref, ru_ref, lu_ref, rv_ref, lv_ref, ro_ref, lo_ref, m1, m2, m3, keep):
    turn(4, r_ref, l_ref, p_ref, ro_ref, lo_ref)
    half = ru_ref.shape[1]
    _, y = place()
    for hop, ref in ((1, m1), (2, m2), (3, m3), (0, keep)):
        i = lax.rem(y + hop, SIDE)
        own = own_ref[i].astype(F32)
        u = own[:half] + ru_ref[i].astype(F32) + lu_ref[i].astype(F32)
        v = own[half:] + rv_ref[i].astype(F32) + lv_ref[i].astype(F32)
        ref[:half] = u.astype(ref.dtype)
        ref[half:] = v.astype(ref.dtype)


def owner_kernel(keep_ref, a_ref, b_ref, c_ref, o_ref):
    o_ref[...] = (keep_ref[...] + wide(a_ref) + wide(b_ref) + wide(c_ref)).T


def local(layer_input, query_act, key_act, out_grad, value_weight):
    tok, width = layer_input.shape
    rows, cols = value_weight.shape
    square = sds((tok, cols))
    square_f32 = sds((tok, cols), F32)
    states = sds((cols, HDIM))

    w_other = swap(value_weight)
    x_near, part = call(
        value_own_kernel,
        [HBM, HBM],
        [in_hbm(layer_input), in_hbm(value_weight)],
        [sds((tok, width)), square_f32],
        "value_own",
        scratch=[pltpu.VMEM((rows, cols), BF16), pltpu.SemaphoreType.DMA((width // 512 + rows // 512,))],
    )
    halves = sds((cols // 2, HDIM))
    value, keep, give = call(
        value_rest_kernel,
        [VMEM] * 4,
        [x_near, w_other, part, key_act],
        [square, halves, halves],
        "value_rest",
    )
    near, far, (attended,) = exclusive(
        keep,
        give,
        1,
        lambda: call(
            inside_kernel,
            [VMEM] * 3,
            [query_act, key_act, value],
            [square_f32],
            "inside",
        ),
    )
    low, state, keep, give = call(
        norm_kernel,
        [VMEM] * 5,
        [query_act, out_grad, attended, near, far],
        [square, states, halves, halves],
        "norm_grad",
    )
    near, far, (value_part, key_part, query_grad) = exclusive(
        keep,
        give,
        -1,
        lambda: call(
            cross_kernel,
            [VMEM] * 5,
            [query_act, key_act, value, low, state],
            [square_f32, square_f32, square],
            "cross",
        ),
    )

    scale = 1.0 / math.sqrt(tok * lax.axis_size(("ctx", "fsdp")))
    half = sds((tok // 2, 512))
    full = sds((tok, 512))
    pieces = sds((width // 256, cols, 128))
    value_grad, state_grad, r, l, other = call(
        lambda *refs: first_kernel(scale, *refs),
        [VMEM] * 7,
        [key_act, value_part, near, far, value_weight, w_other, x_near],
        [square, states, half, half, pieces],
        "value_grad",
    )
    r, l = along_z(r, 1), along_z(l, -1)
    got = swap(other)
    parts, mine = call(
        lambda *refs: work_kernel(scale, *refs),
        [VMEM] * 4,
        [value_grad, value_weight, w_other, x_near],
        [sds((RING - 1, tok, 512)), pieces],
        "work",
    )
    r, l = call(open_turn_kernel, [VMEM] * 3, [r, l, parts], [full] * 2, "turn")
    after = r
    r, l = along_z(r, 1), along_z(l, -1)

    square4 = (SIDE, SIDE) + mine.shape[1:]
    piece = sds((SIDE, cols // 2, 128))
    ru2, lv2, rv1, lu1, cu1, cv1, own = call(
        chip_kernel,
        [VMEM] * 2 + [ANY],
        [mine.reshape(square4), got.reshape(square4), after],
        [piece] * 6 + [sds((SIDE, cols, 128))],
        "chip",
    )
    ru2, lv2 = along_x_ring(ru2, 1), along_x_ring(lv2, -1)
    rv1, lu1 = along_x_ring(rv1, 1), along_x_ring(lu1, -1)
    (key_grad,) = call(
        key_grad_kernel,
        [VMEM] * 3 + [ANY],
        [value, key_part, state_grad, own],
        [square],
        "key_grad",
    )
    r, l, ru1, lv1 = call(
        pair_kernel,
        [VMEM] * 7 + [HBM],
        [r, l, parts, cu1, ru2, cv1, lv2, in_hbm(key_grad)],
        [full] * 2 + [piece] * 2,
        "pair",
    )
    r, l = along_z(r, 1), along_z(l, -1)
    ru1, lv1 = along_x_ring(ru1, 1), along_x_ring(lv1, -1)
    r, l, m1, m2, m3, keep = call(
        line_kernel,
        [VMEM] * 8,
        [r, l, parts, own, ru1, lu1, rv1, lv1],
        [full] * 2 + [sds((cols, 128))] * 3 + [sds((cols, 128), F32)],
        "line",
    )
    r, l = along_z(r, 1), along_z(l, -1)
    got = [along_y_ring(m, k) for m, k in zip((m1, m2, m3), (1, 2, 3))]
    (weight_grad,) = call(
        owner_kernel, [VMEM] * 4, [keep, *got], [sds((128, cols), F32)], "owner"
    )
    (input_grad,) = call(last_turn_kernel, [VMEM] * 3, [r, l, parts], [full], "last_turn")
    return (query_grad, key_grad, input_grad, weight_grad)


def solution(mesh):
    in_specs = (
        P(("ctx", "fsdp"), None),
        P(("ctx", "fsdp"), "head"),
        P(("ctx", "fsdp"), "head"),
        P(("ctx", "fsdp"), "head"),
        P("fsdp", "head"),
    )
    out_specs = (
        P(("ctx", "fsdp"), "head"),
        P(("ctx", "fsdp"), "head"),
        P(("ctx", "fsdp"), "head"),
        P(("ctx", "fsdp"), "head"),
    )
    return jax.shard_map(local, mesh=mesh, in_specs=in_specs, out_specs=out_specs, check_vma=False)
```

profile of v0, /device:TPU:24, one launch (start us, length us, event | category | flops | bytes accessed | tf_op | source)
XLA Modules:
  0.0 118.5 jit_solution(1265716091143680838)
XLA Ops:
  0.7 3.1 %value_own.1 = (bf16[512,4096]{1,0:T(8,128)(2,1)S(1)}, f32[512,512]{1,0:T(8,128)S(1)}) custom-call(bf16[512,4096]{1,0:T(8,128)(2,1)} %x_hbm.1, bf16[2048,512]{1,0:T(8,128)(2,1)} %refs_1_.1), custom_call_target="tpu_custom_call" | custom-call | flops 1000 | bytes 11534336 | tf_op jit(solution)/shard_map/value_own/pallas_call | solution.py:52
  8.8 2.1 %inside.1._.a_ref = f32[512,512]{1,0:T(8,128)S(1)} custom-call(bf16[512,512]{1,0:T(8,128)(2,1)S(1)} %copy-done.2, bf16[512,512]{1,0:T(8,128)(2,1)S(1)} %copy-done.1, bf16[512,512]{1,0:T(8,128)(2,1)S(1)} %get-tuple-element.48.v_ref), custom_call_target="tpu_custom_call" | custom-call | flops 1000 | bytes 2621440 | tf_op jit(solution)/shard_map/inside/pallas_call | solution.py:52
  14.4 3.5 %collective-permute-done.3.b_ref.refs_3_ = bf16[256,128]{1,0:T(8,128)(2,1)S(1)} collective-permute-done((bf16[256,128]{1,0:T(8,128)(2,1)S(1)}, bf16[256,128]{1,0:T(8,128)(2,1)S(1)}, u32[]{:S(2)}, u32[]{:S(2)}) %collective-permute-start.3) | collective-permute-done | bytes 65568 | tf_op jit(solution)/shard_map/ppermute | solution.py:222
  19.5 2.8 %collective-permute-done.4.b_ref.refs_4_ = bf16[256,128]{1,0:T(8,128)(2,1)S(1)} collective-permute-done((bf16[256,128]{1,0:T(8,128)(2,1)S(1)}, bf16[256,128]{1,0:T(8,128)(2,1)S(1)}, u32[]{:S(2)}, u32[]{:S(2)}) %collective-permute-start.4) | collective-permute-done | bytes 65568 | tf_op jit(solution)/shard_map/ppermute | solution.py:222
  22.3 2.8 %collective-permute-start.5 = (bf16[256,128]{1,0:T(8,128)(2,1)S(1)}, bf16[256,128]{1,0:T(8,128)(2,1)S(1)}, u32[]{:S(2)}, u32[]{:S(2)}) collective-permute-start(bf16[256,128]{1,0:T(8,128)(2,1)S(1)} %fold.11), channel_id=1, source_target_pairs={{0,192},{16,208},{32,224},{48,240},{64,128},{80,144},{96,160},{112... | collective-permute-start | bytes 196616 | tf_op jit(solution)/shard_map/ppermute | solution.py:222
  25.2 2.7 %collective-permute-done.5.refs_5_ = bf16[256,128]{1,0:T(8,128)(2,1)S(1)} collective-permute-done((bf16[256,128]{1,0:T(8,128)(2,1)S(1)}, bf16[256,128]{1,0:T(8,128)(2,1)S(1)}, u32[]{:S(2)}, u32[]{:S(2)}) %collective-permute-start.5) | collective-permute-done | bytes 65568 | tf_op jit(solution)/shard_map/ppermute | solution.py:222
  32.0 4.9 %cross.1 = (f32[512,512]{1,0:T(8,128)S(1)}, f32[512,512]{1,0:T(8,128)S(1)}, bf16[512,512]{1,0:T(8,128)(2,1)}) custom-call(bf16[512,512]{1,0:T(8,128)(2,1)S(1)} %copy-done.2, bf16[512,512]{1,0:T(8,128)(2,1)S(1)} %copy-done.1, bf16[512,512]{1,0:T(8,128)(2,1)S(1)} %get-tuple-element.48.v_ref, bf16[512,512]{1,0:T(8,128)(2,1)S(1)} %get-tuple-element.53.low_ref, ...), custom_call_target="tpu_custom_call" | custom-call | flops 1000 | bytes 4849664 | tf_op jit(solution)/shard_map/cross/pallas_call | solution.py:52
  38.9 3.5 %collective-permute-done.9.b_ref.refs_3_ = bf16[256,128]{1,0:T(8,128)(2,1)S(1)} collective-permute-done((bf16[256,128]{1,0:T(8,128)(2,1)S(1)}, bf16[256,128]{1,0:T(8,128)(2,1)S(1)}, u32[]{:S(2)}, u32[]{:S(2)}) %collective-permute-start.9) | collective-permute-done | bytes 65568 | tf_op jit(solution)/shard_map/ppermute | solution.py:222
  42.8 4.0 %collective-permute-done.10.b_ref.refs_4_ = bf16[256,128]{1,0:T(8,128)(2,1)S(1)} collective-permute-done((bf16[256,128]{1,0:T(8,128)(2,1)S(1)}, bf16[256,128]{1,0:T(8,128)(2,1)S(1)}, u32[]{:S(2)}, u32[]{:S(2)}) %collective-permute-start.10) | collective-permute-done | bytes 65568 | tf_op jit(solution)/shard_map/ppermute | solution.py:222
  46.8 2.8 %collective-permute-start.11 = (bf16[256,128]{1,0:T(8,128)(2,1)S(1)}, bf16[256,128]{1,0:T(8,128)(2,1)S(1)}, u32[]{:S(2)}, u32[]{:S(2)}) collective-permute-start(bf16[256,128]{1,0:T(8,128)(2,1)S(1)} %fold.15), channel_id=1, source_target_pairs={{0,192},{16,208},{32,224},{48,240},{64,128},{80,144},{96,160},{112... | collective-permute-start | bytes 196616 | tf_op jit(solution)/shard_map/ppermute | solution.py:222
  49.7 2.7 %collective-permute-done.11.refs_5_ = bf16[256,128]{1,0:T(8,128)(2,1)S(1)} collective-permute-done((bf16[256,128]{1,0:T(8,128)(2,1)S(1)}, bf16[256,128]{1,0:T(8,128)(2,1)S(1)}, u32[]{:S(2)}, u32[]{:S(2)}) %collective-permute-start.11) | collective-permute-done | bytes 65568 | tf_op jit(solution)/shard_map/ppermute | solution.py:222
  53.8 3.2 %value_grad.1 = (bf16[512,512]{1,0:T(8,128)(2,1)S(1)}, bf16[512,128]{1,0:T(8,128)(2,1)S(1)}, bf16[256,512]{1,0:T(8,128)(2,1)S(1)}, bf16[256,512]{1,0:T(8,128)(2,1)S(1)}, bf16[16,512,128]{2,1,0:T(8,128)(2,1)S(1)}) custom-call(bf16[512,512]{1,0:T(8,128)(2,1)S(1)} %copy-done.1, f32[512,512]{1,0:T(8,128)S(1)} %get-tuple-element.57._.refs_1_, ...), custom_call_target="tpu_custom_call" | custom-call | flops 1000 | bytes 13434880 | tf_op jit(solution)/shard_map/value_grad/pallas_call | solution.py:52
  59.2 4.0 %collective-permute-start.15 = (bf16[256,512]{1,0:T(8,128)(2,1)S(1)}, bf16[256,512]{1,0:T(8,128)(2,1)S(1)}, u32[]{:S(2)}, u32[]{:S(2)}) collective-permute-start(bf16[256,512]{1,0:T(8,128)(2,1)S(1)} %get-tuple-element.67), channel_id=1, source_target_pairs={{0,14},{2,0},{4,2},{6,4},{8,6},{10,8},{12,10},{14,12},{1,15},{3,1}... | collective-permute-start | bytes 786440 | tf_op jit(solution)/shard_map/ppermute | solution.py:236
  63.1 5.6 %work.1 = (bf16[7,512,512]{2,1,0:T(8,128)(2,1)S(1)}, bf16[16,512,128]{2,1,0:T(8,128)(2,1)S(1)}) custom-call(bf16[512,512]{1,0:T(8,128)(2,1)S(1)} %get-tuple-element.63.refs_0_, bf16[2048,512]{1,0:T(8,128)(2,1)S(1)} %copy-done, bf16[2048,512]{1,0:T(8,128)(2,1)S(1)} %collective-permute-done.w_ref.refs_5_.refs_2_, ...), custom_call_target="tpu_custom_call" | custom-call | flops 1000 | bytes 14680064 | tf_op jit(solution)/shard_map/work/pallas_call | solution.py:52
  70.1 3.0 %collective-permute-start.17 = (bf16[512,512]{1,0:T(8,128)(2,1)S(1)}, bf16[512,512]{1,0:T(8,128)(2,1)S(1)}, u32[]{:S(2)}, u32[]{:S(2)}) collective-permute-start(bf16[512,512]{1,0:T(8,128)(2,1)S(1)} %get-tuple-element.71), channel_id=1, source_target_pairs={{0,14},{2,0},{4,2},{6,4},{8,6},{10,8},{12,10},{14,12},{1,15},{3,1}... | collective-permute-start | bytes 1572872 | tf_op jit(solution)/shard_map/ppermute | solution.py:236
  73.7 3.2 %collective-permute-start.19 = (bf16[4,256,128]{2,1,0:T(8,128)(2,1)S(1)}, bf16[4,256,128]{2,1,0:T(8,128)(2,1)S(1)}, u32[]{:S(2)}, u32[]{:S(2)}) collective-permute-start(bf16[4,256,128]{2,1,0:T(8,128)(2,1)S(1)} %get-tuple-element.75), channel_id=1, source_target_pairs={{0,192},{16,208},{32,224},{48,240},{64,0},{80,16},{96,32},{112,48}... | collective-permute-start | bytes 786440 | tf_op jit(solution)/shard_map/ppermute | solution.py:226
  80.0 4.0 %collective-permute-done.17.l_ref = bf16[512,512]{1,0:T(8,128)(2,1)S(1)} collective-permute-done((bf16[512,512]{1,0:T(8,128)(2,1)S(1)}, bf16[512,512]{1,0:T(8,128)(2,1)S(1)}, u32[]{:S(2)}, u32[]{:S(2)}) %collective-permute-start.17) | collective-permute-done | bytes 524320 | tf_op jit(solution)/shard_map/ppermute | solution.py:236
  84.0 3.4 %collective-permute-done.16.r_ref = bf16[512,512]{1,0:T(8,128)(2,1)S(1)} collective-permute-done((bf16[512,512]{1,0:T(8,128)(2,1)S(1)}, bf16[512,512]{1,0:T(8,128)(2,1)S(1)}, u32[]{:S(2)}, u32[]{:S(2)}) %collective-permute-start.16) | collective-permute-done | bytes 524320 | tf_op jit(solution)/shard_map/ppermute | solution.py:236
  87.9 3.2 %collective-permute-start.21 = (bf16[512,512]{1,0:T(8,128)(2,1)S(1)}, bf16[512,512]{1,0:T(8,128)(2,1)S(1)}, u32[]{:S(2)}, u32[]{:S(2)}) collective-permute-start(bf16[512,512]{1,0:T(8,128)(2,1)S(1)} %get-tuple-element.77), channel_id=1, source_target_pairs={{0,14},{2,0},{4,2},{6,4},{8,6},{10,8},{12,10},{14,12},{1,15},{3,1}... | collective-permute-start | bytes 1572872 | tf_op jit(solution)/shard_map/ppermute | solution.py:236
  92.0 2.3 %collective-permute-start.25 = (bf16[4,256,128]{2,1,0:T(8,128)(2,1)S(1)}, bf16[4,256,128]{2,1,0:T(8,128)(2,1)S(1)}, u32[]{:S(2)}, u32[]{:S(2)}) collective-permute-start(bf16[4,256,128]{2,1,0:T(8,128)(2,1)S(1)} %get-tuple-element.81), channel_id=1, source_target_pairs={{0,192},{16,208},{32,224},{48,240},{64,0},{80,16},{96,32},{112,48}... | collective-permute-start | bytes 786440 | tf_op jit(solution)/shard_map/ppermute | solution.py:226
  94.4 6.7 %collective-permute-done.24.rv_ref = bf16[4,256,128]{2,1,0:T(8,128)(2,1)S(1)} collective-permute-done((bf16[4,256,128]{2,1,0:T(8,128)(2,1)S(1)}, bf16[4,256,128]{2,1,0:T(8,128)(2,1)S(1)}, u32[]{:S(2)}, u32[]{:S(2)}) %collective-permute-start.24) | collective-permute-done | bytes 262176 | tf_op jit(solution)/shard_map/ppermute | solution.py:226
  101.1 2.8 %collective-permute-done.22.ru_ref = bf16[4,256,128]{2,1,0:T(8,128)(2,1)S(1)} collective-permute-done((bf16[4,256,128]{2,1,0:T(8,128)(2,1)S(1)}, bf16[4,256,128]{2,1,0:T(8,128)(2,1)S(1)}, u32[]{:S(2)}, u32[]{:S(2)}) %collective-permute-start.22) | collective-permute-done | bytes 262176 | tf_op jit(solution)/shard_map/ppermute | solution.py:226
  104.4 3.2 %collective-permute-start.27 = (bf16[512,512]{1,0:T(8,128)(2,1)S(1)}, bf16[512,512]{1,0:T(8,128)(2,1)S(1)}, u32[]{:S(2)}, u32[]{:S(2)}) collective-permute-start(bf16[512,512]{1,0:T(8,128)(2,1)S(1)} %get-tuple-element.83), channel_id=1, source_target_pairs={{0,14},{2,0},{4,2},{6,4},{8,6},{10,8},{12,10},{14,12},{1,15},{3,1}... | collective-permute-start | bytes 1572872 | tf_op jit(solution)/shard_map/ppermute | solution.py:236
  108.2 2.3 %collective-permute-start.29 = (bf16[512,128]{1,0:T(8,128)(2,1)S(1)}, bf16[512,128]{1,0:T(8,128)(2,1)S(1)}, u32[]{:S(2)}, u32[]{:S(2)}) collective-permute-start(bf16[512,128]{1,0:T(8,128)(2,1)S(1)} %get-tuple-element.86), channel_id=1, source_target_pairs={{0,32},{16,48},{32,0},{48,16},{64,96},{80,112},{96,64},{112,80},{1... | collective-permute-start | bytes 393224 | tf_op jit(solution)/shard_map/ppermute | solution.py:230
  (70 shorter events, 35.6 us)
Async XLA Ops:
  0.6 4.5 %collective-permute-start = (bf16[2048,512]{1,0:T(8,128)(2,1)}, bf16[2048,512]{1,0:T(8,128)(2,1)S(1)}, u32[]{:S(2)}, u32[]{:S(2)}) collective-permute-start(bf16[2048,512]{1,0:T(8,128)(2,1)} %refs_1_.1), channel_id=1, source_target_pairs={{0,1},{1,0},{2,3},{3,2},{4,5},{5,4},{6,7},{7,6},{8,9},{9,8},{10,11... | collective-permute-start | bytes 6291464 | tf_op jit(solution)/shard_map/ppermute | solution.py:240
  12.4 5.6 %collective-permute-start.3 = (bf16[256,128]{1,0:T(8,128)(2,1)S(1)}, bf16[256,128]{1,0:T(8,128)(2,1)S(1)}, u32[]{:S(2)}, u32[]{:S(2)}) collective-permute-start(bf16[256,128]{1,0:T(8,128)(2,1)S(1)} %fold.9.a_ref), channel_id=1, source_target_pairs={{0,48},{16,32},{32,16},{48,0},{64,112},{80,96},{96,80},{112,64},{1... | collective-permute-start | bytes 196616 | tf_op jit(solution)/shard_map/ppermute | solution.py:222
  22.3 5.6 %collective-permute-start.5 = (bf16[256,128]{1,0:T(8,128)(2,1)S(1)}, bf16[256,128]{1,0:T(8,128)(2,1)S(1)}, u32[]{:S(2)}, u32[]{:S(2)}) collective-permute-start(bf16[256,128]{1,0:T(8,128)(2,1)S(1)} %fold.11), channel_id=1, source_target_pairs={{0,192},{16,208},{32,224},{48,240},{64,128},{80,144},{96,160},{112... | collective-permute-start | bytes 196616 | tf_op jit(solution)/shard_map/ppermute | solution.py:222
  31.9 5.0 %collective-permute-start.8 = (bf16[256,128]{1,0:T(8,128)(2,1)S(1)}, bf16[256,128]{1,0:T(8,128)(2,1)S(1)}, u32[]{:S(2)}, u32[]{:S(2)}) collective-permute-start(bf16[256,128]{1,0:T(8,128)(2,1)S(1)} %fold.12.a_ref), channel_id=1, source_target_pairs={{0,16},{16,0},{32,48},{48,32},{64,80},{80,64},{96,112},{112,96},{1... | collective-permute-start | bytes 196616 | tf_op jit(solution)/shard_map/ppermute | solution.py:222
  36.9 5.6 %collective-permute-start.9 = (bf16[256,128]{1,0:T(8,128)(2,1)S(1)}, bf16[256,128]{1,0:T(8,128)(2,1)S(1)}, u32[]{:S(2)}, u32[]{:S(2)}) collective-permute-start(bf16[256,128]{1,0:T(8,128)(2,1)S(1)} %fold.13.a_ref), channel_id=1, source_target_pairs={{0,48},{16,32},{32,16},{48,0},{64,112},{80,96},{96,80},{112,64},{1... | collective-permute-start | bytes 196616 | tf_op jit(solution)/shard_map/ppermute | solution.py:222
  46.8 5.6 %collective-permute-start.11 = (bf16[256,128]{1,0:T(8,128)(2,1)S(1)}, bf16[256,128]{1,0:T(8,128)(2,1)S(1)}, u32[]{:S(2)}, u32[]{:S(2)}) collective-permute-start(bf16[256,128]{1,0:T(8,128)(2,1)S(1)} %fold.15), channel_id=1, source_target_pairs={{0,192},{16,208},{32,224},{48,240},{64,128},{80,144},{96,160},{112... | collective-permute-start | bytes 196616 | tf_op jit(solution)/shard_map/ppermute | solution.py:222
  57.0 16.1 %collective-permute-start.13 = (bf16[16,512,128]{2,1,0:T(8,128)(2,1)S(1)}, bf16[16,512,128]{2,1,0:T(8,128)(2,1)S(1)}, u32[]{:S(2)}, u32[]{:S(2)}) collective-permute-start(bf16[16,512,128]{2,1,0:T(8,128)(2,1)S(1)} %get-tuple-element.65), channel_id=1, source_target_pairs={{0,1},{1,0},{2,3},{3,2},{4,5},{5,4},{6,7},{7,6},{8,9},{9,8},{10,11... | collective-permute-start | bytes 6291464 | tf_op jit(solution)/shard_map/ppermute | solution.py:240
  57.3 12.7 %collective-permute-start.14 = (bf16[256,512]{1,0:T(8,128)(2,1)S(1)}, bf16[256,512]{1,0:T(8,128)(2,1)S(1)}, u32[]{:S(2)}, u32[]{:S(2)}) collective-permute-start(bf16[256,512]{1,0:T(8,128)(2,1)S(1)} %get-tuple-element.66), channel_id=1, source_target_pairs={{0,2},{2,4},{4,6},{6,8},{8,10},{10,12},{12,14},{14,0},{1,3},{3,5},... | collective-permute-start | bytes 786440 | tf_op jit(solution)/shard_map/ppermute | solution.py:236
  59.2 10.8 %collective-permute-start.15 = (bf16[256,512]{1,0:T(8,128)(2,1)S(1)}, bf16[256,512]{1,0:T(8,128)(2,1)S(1)}, u32[]{:S(2)}, u32[]{:S(2)}) collective-permute-start(bf16[256,512]{1,0:T(8,128)(2,1)S(1)} %get-tuple-element.67), channel_id=1, source_target_pairs={{0,14},{2,0},{4,2},{6,4},{8,6},{10,8},{12,10},{14,12},{1,15},{3,1}... | collective-permute-start | bytes 786440 | tf_op jit(solution)/shard_map/ppermute | solution.py:236
  70.1 13.9 %collective-permute-start.17 = (bf16[512,512]{1,0:T(8,128)(2,1)S(1)}, bf16[512,512]{1,0:T(8,128)(2,1)S(1)}, u32[]{:S(2)}, u32[]{:S(2)}) collective-permute-start(bf16[512,512]{1,0:T(8,128)(2,1)S(1)} %get-tuple-element.71), channel_id=1, source_target_pairs={{0,14},{2,0},{4,2},{6,4},{8,6},{10,8},{12,10},{14,12},{1,15},{3,1}... | collective-permute-start | bytes 1572872 | tf_op jit(solution)/shard_map/ppermute | solution.py:236
  73.1 14.3 %collective-permute-start.16 = (bf16[512,512]{1,0:T(8,128)(2,1)S(1)}, bf16[512,512]{1,0:T(8,128)(2,1)S(1)}, u32[]{:S(2)}, u32[]{:S(2)}) collective-permute-start(bf16[512,512]{1,0:T(8,128)(2,1)S(1)} %get-tuple-element.69._), channel_id=1, source_target_pairs={{0,2},{2,4},{4,6},{6,8},{8,10},{10,12},{12,14},{14,0},{1,3},{3,5},... | collective-permute-start | bytes 1572872 | tf_op jit(solution)/shard_map/ppermute | solution.py:236
  73.6 13.8 %collective-permute-start.18 = (bf16[4,256,128]{2,1,0:T(8,128)(2,1)S(1)}, bf16[4,256,128]{2,1,0:T(8,128)(2,1)S(1)}, u32[]{:S(2)}, u32[]{:S(2)}) collective-permute-start(bf16[4,256,128]{2,1,0:T(8,128)(2,1)S(1)} %get-tuple-element.73), channel_id=1, source_target_pairs={{0,64},{16,80},{32,96},{48,112},{64,128},{80,144},{96,160},{112,17... | collective-permute-start | bytes 786440 | tf_op jit(solution)/shard_map/ppermute | solution.py:226
  73.7 13.7 %collective-permute-start.19 = (bf16[4,256,128]{2,1,0:T(8,128)(2,1)S(1)}, bf16[4,256,128]{2,1,0:T(8,128)(2,1)S(1)}, u32[]{:S(2)}, u32[]{:S(2)}) collective-permute-start(bf16[4,256,128]{2,1,0:T(8,128)(2,1)S(1)} %get-tuple-element.75), channel_id=1, source_target_pairs={{0,192},{16,208},{32,224},{48,240},{64,0},{80,16},{96,32},{112,48}... | collective-permute-start | bytes 786440 | tf_op jit(solution)/shard_map/ppermute | solution.py:226
  76.9 15.1 %collective-permute-start.23 = (bf16[4,256,128]{2,1,0:T(8,128)(2,1)S(1)}, bf16[4,256,128]{2,1,0:T(8,128)(2,1)S(1)}, u32[]{:S(2)}, u32[]{:S(2)}) collective-permute-start(bf16[4,256,128]{2,1,0:T(8,128)(2,1)S(1)} %get-tuple-element.79), channel_id=1, source_target_pairs={{0,192},{16,208},{32,224},{48,240},{64,0},{80,16},{96,32},{112,48}... | collective-permute-start | bytes 786440 | tf_op jit(solution)/shard_map/ppermute | solution.py:226
  87.8 16.1 %collective-permute-start.20 = (bf16[512,512]{1,0:T(8,128)(2,1)S(1)}, bf16[512,512]{1,0:T(8,128)(2,1)S(1)}, u32[]{:S(2)}, u32[]{:S(2)}) collective-permute-start(bf16[512,512]{1,0:T(8,128)(2,1)S(1)} %get-tuple-element.76), channel_id=1, source_target_pairs={{0,2},{2,4},{4,6},{6,8},{8,10},{10,12},{12,14},{14,0},{1,3},{3,5},... | collective-permute-start | bytes 1572872 | tf_op jit(solution)/shard_map/ppermute | solution.py:236
  87.9 16.0 %collective-permute-start.21 = (bf16[512,512]{1,0:T(8,128)(2,1)S(1)}, bf16[512,512]{1,0:T(8,128)(2,1)S(1)}, u32[]{:S(2)}, u32[]{:S(2)}) collective-permute-start(bf16[512,512]{1,0:T(8,128)(2,1)S(1)} %get-tuple-element.77), channel_id=1, source_target_pairs={{0,14},{2,0},{4,2},{6,4},{8,6},{10,8},{12,10},{14,12},{1,15},{3,1}... | collective-permute-start | bytes 1572872 | tf_op jit(solution)/shard_map/ppermute | solution.py:236
  91.1 10.0 %collective-permute-start.24 = (bf16[4,256,128]{2,1,0:T(8,128)(2,1)S(1)}, bf16[4,256,128]{2,1,0:T(8,128)(2,1)S(1)}, u32[]{:S(2)}, u32[]{:S(2)}) collective-permute-start(bf16[4,256,128]{2,1,0:T(8,128)(2,1)S(1)} %get-tuple-element.80), channel_id=1, source_target_pairs={{0,64},{16,80},{32,96},{48,112},{64,128},{80,144},{96,160},{112,17... | collective-permute-start | bytes 786440 | tf_op jit(solution)/shard_map/ppermute | solution.py:226
  91.1 12.8 %collective-permute-start.22 = (bf16[4,256,128]{2,1,0:T(8,128)(2,1)S(1)}, bf16[4,256,128]{2,1,0:T(8,128)(2,1)S(1)}, u32[]{:S(2)}, u32[]{:S(2)}) collective-permute-start(bf16[4,256,128]{2,1,0:T(8,128)(2,1)S(1)} %get-tuple-element.78), channel_id=1, source_target_pairs={{0,64},{16,80},{32,96},{48,112},{64,128},{80,144},{96,160},{112,17... | collective-permute-start | bytes 786440 | tf_op jit(solution)/shard_map/ppermute | solution.py:226
  92.0 11.9 %collective-permute-start.25 = (bf16[4,256,128]{2,1,0:T(8,128)(2,1)S(1)}, bf16[4,256,128]{2,1,0:T(8,128)(2,1)S(1)}, u32[]{:S(2)}, u32[]{:S(2)}) collective-permute-start(bf16[4,256,128]{2,1,0:T(8,128)(2,1)S(1)} %get-tuple-element.81), channel_id=1, source_target_pairs={{0,192},{16,208},{32,224},{48,240},{64,0},{80,16},{96,32},{112,48}... | collective-permute-start | bytes 786440 | tf_op jit(solution)/shard_map/ppermute | solution.py:226
  104.3 13.2 %collective-permute-start.26 = (bf16[512,512]{1,0:T(8,128)(2,1)S(1)}, bf16[512,512]{1,0:T(8,128)(2,1)S(1)}, u32[]{:S(2)}, u32[]{:S(2)}) collective-permute-start(bf16[512,512]{1,0:T(8,128)(2,1)S(1)} %get-tuple-element.82), channel_id=1, source_target_pairs={{0,2},{2,4},{4,6},{6,8},{8,10},{10,12},{12,14},{14,0},{1,3},{3,5},... | collective-permute-start | bytes 1572872 | tf_op jit(solution)/shard_map/ppermute | solution.py:236
  104.4 13.1 %collective-permute-start.27 = (bf16[512,512]{1,0:T(8,128)(2,1)S(1)}, bf16[512,512]{1,0:T(8,128)(2,1)S(1)}, u32[]{:S(2)}, u32[]{:S(2)}) collective-permute-start(bf16[512,512]{1,0:T(8,128)(2,1)S(1)} %get-tuple-element.83), channel_id=1, source_target_pairs={{0,14},{2,0},{4,2},{6,4},{8,6},{10,8},{12,10},{14,12},{1,15},{3,1}... | collective-permute-start | bytes 1572872 | tf_op jit(solution)/shard_map/ppermute | solution.py:236
  107.6 5.0 %collective-permute-start.28 = (bf16[512,128]{1,0:T(8,128)(2,1)S(1)}, bf16[512,128]{1,0:T(8,128)(2,1)S(1)}, u32[]{:S(2)}, u32[]{:S(2)}) collective-permute-start(bf16[512,128]{1,0:T(8,128)(2,1)S(1)} %get-tuple-element.85), channel_id=1, source_target_pairs={{0,16},{16,32},{32,48},{48,0},{64,80},{80,96},{96,112},{112,64},{1... | collective-permute-start | bytes 393224 | tf_op jit(solution)/shard_map/ppermute | solution.py:230
  108.2 6.5 %collective-permute-start.29 = (bf16[512,128]{1,0:T(8,128)(2,1)S(1)}, bf16[512,128]{1,0:T(8,128)(2,1)S(1)}, u32[]{:S(2)}, u32[]{:S(2)}) collective-permute-start(bf16[512,128]{1,0:T(8,128)(2,1)S(1)} %get-tuple-element.86), channel_id=1, source_target_pairs={{0,32},{16,48},{32,0},{48,16},{64,96},{80,112},{96,64},{112,80},{1... | collective-permute-start | bytes 393224 | tf_op jit(solution)/shard_map/ppermute | solution.py:230
  110.5 6.2 %collective-permute-start.30 = (bf16[512,128]{1,0:T(8,128)(2,1)S(1)}, bf16[512,128]{1,0:T(8,128)(2,1)S(1)}, u32[]{:S(2)}, u32[]{:S(2)}) collective-permute-start(bf16[512,128]{1,0:T(8,128)(2,1)S(1)} %get-tuple-element.87), channel_id=1, source_target_pairs={{0,48},{16,0},{32,16},{48,32},{64,112},{80,64},{96,80},{112,96},{1... | collective-permute-start | bytes 393224 | tf_op jit(solution)/shard_map/ppermute | solution.py:230
  (11 other events, 62.0 us)
where the time goes:
time: 119 us
  waiting for transfers between devices  50.8 us (43%)
  starting transfers between devices  40.1 us (34%)
  Pallas kernels  26.8 us (23%)
    pallas_call x24, Pallas kernels, call(): pl.pallas_call(body, out_shape=tuple(outs), in_specs=specs, out_specs=tup...  26.8 us
    ppermute x8, waiting for transfers between devices, along(): return lax.ppermute(a, 'ctx', [(i, other(i)) for i in range(SIDE * SIDE)])  20.6 us
    ppermute x8, starting transfers between devices, along_z(): return lax.ppermute(a, 'head', [(i, (i + k) % RING) for i in range(RING)])  15.5 us
    ppermute x8, starting transfers between devices, along(): return lax.ppermute(a, 'ctx', [(i, other(i)) for i in range(SIDE * SIDE)])  12.7 us
    ppermute x6, waiting for transfers between devices, along_x_ring(): return lax.ppermute(a, 'ctx', [(i, (i + SIDE * k) % 16) for i in range(16)])  9.55 us
    ppermute x8, waiting for transfers between devices, along_z(): return lax.ppermute(a, 'head', [(i, (i + k) % RING) for i in range(RING)])  8.54 us
    ppermute x6, starting transfers between devices, along_x_ring(): return lax.ppermute(a, 'ctx', [(i, (i + SIDE * k) % 16) for i in range(16)])  8.13 us
    ppermute x3, waiting for transfers between devices, along_y_ring(): lax.ppermute(a, 'ctx', [(i, i // SIDE * SIDE + (i + k) % SIDE) for i in r...  6.17 us
  transfers between devices with their start and end apart: 31, of which 20 were waited for; matrix products, arithmetic and copies ran while one was open for 0% of the time, Pallas kernels for 16%

commit v1 on v0

--- a/solution.py
+++ b/solution.py
@@ -110,17 +110,14 @@
         xs[j].start()
     for j in range(half, n):
         xs[j].start()
-    part_ref[...] = jnp.zeros_like(part_ref)
-
-    @pl.loop(0, half)
-    def _(j):
-        rows = pl.ds(pl.multiple_of(j * step, step), step)
-        pltpu.make_async_copy(w_hbm.at[rows, :], w_ref.at[rows, :], sems.at[n + j]).wait()
-        pltpu.make_async_copy(
-            x_hbm.at[:, x_cols(j)], x_ref.at[:, x_cols(j)], sems.at[j]
-        ).wait()
-        part_ref[...] += dot(x_ref[:, x_cols(j)], w_ref[rows, :])
-
+    for j in range(half):
+        ws[j].wait()
+        xs[j].wait()
+        prod = dot(x_ref[:, x_cols(j)], w_ref[j * step : (j + 1) * step, :])
+        if j == 0:
+            part_ref[...] = prod
+        else:
+            part_ref[...] += prod
     for j in range(half, n):
         xs[j].wait()
 
@@ -177,13 +174,19 @@
     split(local, keep_ref, give_ref)
 
 
-def cross_kernel(q_ref, k_ref, v_ref, low_ref, state_ref, vp_ref, kp_ref, qg_ref):
+def masked_kernel(q_ref, k_ref, low_ref, vp_ref):
     def head(c):
-        q, k, low = q_ref[:, c], k_ref[:, c], low_ref[:, c]
+        vp_ref[:, c] = dot(tril(dot(q_ref[:, c], k_ref[:, c], NT)), low_ref[:, c], TN)
+
+    each_head(q_ref, head)
+
+
+def cross_kernel(q_ref, k_ref, v_ref, low_ref, state_ref, qg_ref, kp_ref):
+    def head(c):
+        low = low_ref[:, c]
         cross = tril(dot(low, v_ref[:, c], NT))
-        qg_ref[:, c] = (dot(cross, k) + dot(low, state_ref[c, :], NT)).astype(BF16)
-        kp_ref[:, c] = dot(cross, q, TN)
-        vp_ref[:, c] = dot(tril(dot(q, k, NT)), low, TN)
+        qg_ref[:, c] = (dot(cross, k_ref[:, c]) + dot(low, state_ref[c, :], NT)).astype(BF16)
+        kp_ref[:, c] = dot(cross, q_ref[:, c], TN)
 
     each_head(q_ref, head)
 
@@ -240,7 +243,7 @@
     return lax.ppermute(a, "fsdp", [(0, 1), (1, 0)])
 
 
-def exclusive(keep, give, sign, work):
+def exclusive(keep, give, sign, first, second=lambda: ()):
     shape = sds(keep.shape)
 
     def fold(kernel, *arrays):
@@ -250,10 +253,11 @@
     got = swap(give)
     t = fold(chip_sum_kernel, keep, got, keep)
     y1 = along(t, "y", True)
-    done = work()
+    done = list(first())
     t = fold(pair_sum_kernel, t, y1, done[0])
     y2 = along(t, "y", False)
-    t = fold(pair_sum_kernel, t, y2, done[0])
+    done += list(second())
+    t = fold(pair_sum_kernel, t, y2, done[-1])
     x1 = along(t, "x", True)
     t = fold(pair_sum_kernel, t, x1, done[0])
     x2 = along(t, "x", False)
@@ -331,10 +335,7 @@
 def weight_pieces(scale, side, vg_ref, x_ref, o_ref):
     turned = vg_ref[...].T
     shift = side * 128
-
-    @pl.loop(0, o_ref.shape[0] // 4)
-    def _(group):
-        first = group * 4
+    for first in range(0, o_ref.shape[0], 4):
         x = jnp.concatenate(
             [
                 x_ref[:, pl.ds(pl.multiple_of((first + p) * 256 + shift, 128), 128)]
@@ -434,15 +435,18 @@
         [square, states, halves, halves],
         "norm_grad",
     )
-    near, far, (value_part, key_part, query_grad) = exclusive(
+    near, far, (value_part, query_grad, key_part) = exclusive(
         keep,
         give,
         -1,
         lambda: call(
+            masked_kernel, [VMEM] * 3, [query_act, key_act, low], [square_f32], "masked"
+        ),
+        lambda: call(
             cross_kernel,
             [VMEM] * 5,
             [query_act, key_act, value, low, state],
-            [square_f32, square_f32, square],
+            [square, square_f32],
             "cross",
         ),
     )

time: 119 us -> 117 us (0.983)
    ppermute x8, waiting for transfers between devices: 20.6 us -> 18.8 us  [along(): return lax.ppermute(a, 'ctx', [(i, other(i)) for i in range(SIDE * SIDE)])]
    pallas_call x24 -> x25, Pallas kernels: 26.8 us -> 26.3 us  [call(): pl.pallas_call(body, out_shape=tuple(outs), in_specs=specs, out_specs=tup...]
  transfers between devices with their start and end apart: 31 -> 31, of which waited for: 20 -> 20; matrix products, arithmetic and copies ran while one was open for 0% -> 0% of each run, Pallas kernels for 16% -> 17%
where the time goes in v1:
time: 117 us
  waiting for transfers between devices  50.6 us (43%)
  starting transfers between devices  39.4 us (34%)
  Pallas kernels  26.3 us (22%)
    pallas_call x25, Pallas kernels, call(): pl.pallas_call(body, out_shape=tuple(outs), in_specs=specs, out_specs=tup...  26.3 us
    ppermute x8, waiting for transfers between devices, along(): return lax.ppermute(a, 'ctx', [(i, other(i)) for i in range(SIDE * SIDE)])  18.8 us
    ppermute x8, starting transfers between devices, along_z(): return lax.ppermute(a, 'head', [(i, (i + k) % RING) for i in range(RING)])  15.5 us
    ppermute x8, starting transfers between devices, along(): return lax.ppermute(a, 'ctx', [(i, other(i)) for i in range(SIDE * SIDE)])  12.7 us
    ppermute x6, waiting for transfers between devices, along_x_ring(): return lax.ppermute(a, 'ctx', [(i, (i + SIDE * k) % 16) for i in range(16)])  9.55 us
    ppermute x8, waiting for transfers between devices, along_z(): return lax.ppermute(a, 'head', [(i, (i + k) % RING) for i in range(RING)])  9.24 us
    ppermute x6, starting transfers between devices, along_x_ring(): return lax.ppermute(a, 'ctx', [(i, (i + SIDE * k) % 16) for i in range(16)])  8.12 us
    ppermute x3, waiting for transfers between devices, along_y_ring(): lax.ppermute(a, 'ctx', [(i, i // SIDE * SIDE + (i + k) % SIDE) for i in r...  6.94 us
  transfers between devices with their start and end apart: 31, of which 20 were waited for; matrix products, arithmetic and copies ran while one was open for 0% of the time, Pallas kernels for 17%

profile of v1, /device:TPU:24, one launch (start us, length us, event | category | flops | bytes accessed | tf_op | source)
XLA Modules:
  0.0 117.2 jit_solution(5922658594704580132)
XLA Ops:
  0.7 2.9 %value_own.1 = (bf16[512,4096]{1,0:T(8,128)(2,1)S(1)}, f32[512,512]{1,0:T(8,128)S(1)}) custom-call(bf16[512,4096]{1,0:T(8,128)(2,1)} %x_hbm.1, bf16[2048,512]{1,0:T(8,128)(2,1)} %refs_1_.1), custom_call_target="tpu_custom_call" | custom-call | flops 1000 | bytes 11534336 | tf_op jit(solution)/shard_map/value_own/pallas_call | solution.py:52
  14.4 3.5 %collective-permute-done.3.b_ref.refs_3_ = bf16[256,128]{1,0:T(8,128)(2,1)S(1)} collective-permute-done((bf16[256,128]{1,0:T(8,128)(2,1)S(1)}, bf16[256,128]{1,0:T(8,128)(2,1)S(1)}, u32[]{:S(2)}, u32[]{:S(2)}) %collective-permute-start.3) | collective-permute-done | bytes 65568 | tf_op jit(solution)/shard_map/ppermute | solution.py:225
  19.5 2.8 %collective-permute-done.4.b_ref.refs_4_ = bf16[256,128]{1,0:T(8,128)(2,1)S(1)} collective-permute-done((bf16[256,128]{1,0:T(8,128)(2,1)S(1)}, bf16[256,128]{1,0:T(8,128)(2,1)S(1)}, u32[]{:S(2)}, u32[]{:S(2)}) %collective-permute-start.4) | collective-permute-done | bytes 65568 | tf_op jit(solution)/shard_map/ppermute | solution.py:225
  22.3 2.8 %collective-permute-start.5 = (bf16[256,128]{1,0:T(8,128)(2,1)S(1)}, bf16[256,128]{1,0:T(8,128)(2,1)S(1)}, u32[]{:S(2)}, u32[]{:S(2)}) collective-permute-start(bf16[256,128]{1,0:T(8,128)(2,1)S(1)} %fold.11), channel_id=1, source_target_pairs={{0,192},{16,208},{32,224},{48,240},{64,128},{80,144},{96,160},{112... | collective-permute-start | bytes 196616 | tf_op jit(solution)/shard_map/ppermute | solution.py:225
  25.2 2.7 %collective-permute-done.5.refs_5_ = bf16[256,128]{1,0:T(8,128)(2,1)S(1)} collective-permute-done((bf16[256,128]{1,0:T(8,128)(2,1)S(1)}, bf16[256,128]{1,0:T(8,128)(2,1)S(1)}, u32[]{:S(2)}, u32[]{:S(2)}) %collective-permute-start.5) | collective-permute-done | bytes 65568 | tf_op jit(solution)/shard_map/ppermute | solution.py:225
  32.0 2.6 %masked.1._.refs_1_ = f32[512,512]{1,0:T(8,128)S(1)} custom-call(bf16[512,512]{1,0:T(8,128)(2,1)S(1)} %copy-done.2, bf16[512,512]{1,0:T(8,128)(2,1)S(1)} %copy-done.1, bf16[512,512]{1,0:T(8,128)(2,1)S(1)} %get-tuple-element.52.low_ref), custom_call_target="tpu_custom_call" | custom-call | flops 1000 | bytes 2621440 | tf_op jit(solution)/shard_map/masked/pallas_call | solution.py:52
  38.3 3.5 %cross.1 = (bf16[512,512]{1,0:T(8,128)(2,1)}, f32[512,512]{1,0:T(8,128)S(1)}) custom-call(bf16[512,512]{1,0:T(8,128)(2,1)S(1)} %copy-done.2, bf16[512,512]{1,0:T(8,128)(2,1)S(1)} %copy-done.1, bf16[512,512]{1,0:T(8,128)(2,1)S(1)} %get-tuple-element.47.v_ref, bf16[512,512]{1,0:T(8,128)(2,1)S(1)} %get-tuple-element.52.low_ref, ...), custom_call_target="tpu_custom_call" | custom-call | flops 1000 | bytes 3801088 | tf_op jit(solution)/shard_map/cross/pallas_call | solution.py:52
  42.2 4.0 %collective-permute-done.10.b_ref.refs_4_ = bf16[256,128]{1,0:T(8,128)(2,1)S(1)} collective-permute-done((bf16[256,128]{1,0:T(8,128)(2,1)S(1)}, bf16[256,128]{1,0:T(8,128)(2,1)S(1)}, u32[]{:S(2)}, u32[]{:S(2)}) %collective-permute-start.10) | collective-permute-done | bytes 65568 | tf_op jit(solution)/shard_map/ppermute | solution.py:225
  46.2 2.8 %collective-permute-start.11 = (bf16[256,128]{1,0:T(8,128)(2,1)S(1)}, bf16[256,128]{1,0:T(8,128)(2,1)S(1)}, u32[]{:S(2)}, u32[]{:S(2)}) collective-permute-start(bf16[256,128]{1,0:T(8,128)(2,1)S(1)} %fold.15), channel_id=1, source_target_pairs={{0,192},{16,208},{32,224},{48,240},{64,128},{80,144},{96,160},{112... | collective-permute-start | bytes 196616 | tf_op jit(solution)/shard_map/ppermute | solution.py:225
  49.1 2.7 %collective-permute-done.11.refs_5_ = bf16[256,128]{1,0:T(8,128)(2,1)S(1)} collective-permute-done((bf16[256,128]{1,0:T(8,128)(2,1)S(1)}, bf16[256,128]{1,0:T(8,128)(2,1)S(1)}, u32[]{:S(2)}, u32[]{:S(2)}) %collective-permute-start.11) | collective-permute-done | bytes 65568 | tf_op jit(solution)/shard_map/ppermute | solution.py:225
  53.2 2.4 %value_grad.1 = (bf16[512,512]{1,0:T(8,128)(2,1)S(1)}, bf16[512,128]{1,0:T(8,128)(2,1)S(1)}, bf16[256,512]{1,0:T(8,128)(2,1)S(1)}, bf16[256,512]{1,0:T(8,128)(2,1)S(1)}, bf16[16,512,128]{2,1,0:T(8,128)(2,1)S(1)}) custom-call(bf16[512,512]{1,0:T(8,128)(2,1)S(1)} %copy-done.1, f32[512,512]{1,0:T(8,128)S(1)} %masked.1._.refs_1_, ...), custom_call_target="tpu_custom_call" | custom-call | flops 1000 | bytes 13434880 | tf_op jit(solution)/shard_map/value_grad/pallas_call | solution.py:52
  57.8 3.9 %collective-permute-start.15 = (bf16[256,512]{1,0:T(8,128)(2,1)S(1)}, bf16[256,512]{1,0:T(8,128)(2,1)S(1)}, u32[]{:S(2)}, u32[]{:S(2)}) collective-permute-start(bf16[256,512]{1,0:T(8,128)(2,1)S(1)} %get-tuple-element.65), channel_id=1, source_target_pairs={{0,14},{2,0},{4,2},{6,4},{8,6},{10,8},{12,10},{14,12},{1,15},{3,1}... | collective-permute-start | bytes 786440 | tf_op jit(solution)/shard_map/ppermute | solution.py:239
  61.8 4.9 %work.1 = (bf16[7,512,512]{2,1,0:T(8,128)(2,1)S(1)}, bf16[16,512,128]{2,1,0:T(8,128)(2,1)S(1)}) custom-call(bf16[512,512]{1,0:T(8,128)(2,1)S(1)} %get-tuple-element.61.refs_0_, bf16[2048,512]{1,0:T(8,128)(2,1)S(1)} %copy-done, bf16[2048,512]{1,0:T(8,128)(2,1)S(1)} %collective-permute-done.w_ref.refs_5_.refs_2_, ...), custom_call_target="tpu_custom_call" | custom-call | flops 1000 | bytes 14680064 | tf_op jit(solution)/shard_map/work/pallas_call | solution.py:52
  68.7 3.0 %collective-permute-start.17 = (bf16[512,512]{1,0:T(8,128)(2,1)S(1)}, bf16[512,512]{1,0:T(8,128)(2,1)S(1)}, u32[]{:S(2)}, u32[]{:S(2)}) collective-permute-start(bf16[512,512]{1,0:T(8,128)(2,1)S(1)} %get-tuple-element.69), channel_id=1, source_target_pairs={{0,14},{2,0},{4,2},{6,4},{8,6},{10,8},{12,10},{14,12},{1,15},{3,1}... | collective-permute-start | bytes 1572872 | tf_op jit(solution)/shard_map/ppermute | solution.py:239
  72.3 3.2 %collective-permute-start.19 = (bf16[4,256,128]{2,1,0:T(8,128)(2,1)S(1)}, bf16[4,256,128]{2,1,0:T(8,128)(2,1)S(1)}, u32[]{:S(2)}, u32[]{:S(2)}) collective-permute-start(bf16[4,256,128]{2,1,0:T(8,128)(2,1)S(1)} %get-tuple-element.73), channel_id=1, source_target_pairs={{0,192},{16,208},{32,224},{48,240},{64,0},{80,16},{96,32},{112,48}... | collective-permute-start | bytes 786440 | tf_op jit(solution)/shard_map/ppermute | solution.py:229
  78.6 4.0 %collective-permute-done.17.l_ref = bf16[512,512]{1,0:T(8,128)(2,1)S(1)} collective-permute-done((bf16[512,512]{1,0:T(8,128)(2,1)S(1)}, bf16[512,512]{1,0:T(8,128)(2,1)S(1)}, u32[]{:S(2)}, u32[]{:S(2)}) %collective-permute-start.17) | collective-permute-done | bytes 524320 | tf_op jit(solution)/shard_map/ppermute | solution.py:239
  82.6 3.4 %collective-permute-done.16.r_ref = bf16[512,512]{1,0:T(8,128)(2,1)S(1)} collective-permute-done((bf16[512,512]{1,0:T(8,128)(2,1)S(1)}, bf16[512,512]{1,0:T(8,128)(2,1)S(1)}, u32[]{:S(2)}, u32[]{:S(2)}) %collective-permute-start.16) | collective-permute-done | bytes 524320 | tf_op jit(solution)/shard_map/ppermute | solution.py:239
  86.5 3.2 %collective-permute-start.21 = (bf16[512,512]{1,0:T(8,128)(2,1)S(1)}, bf16[512,512]{1,0:T(8,128)(2,1)S(1)}, u32[]{:S(2)}, u32[]{:S(2)}) collective-permute-start(bf16[512,512]{1,0:T(8,128)(2,1)S(1)} %get-tuple-element.75), channel_id=1, source_target_pairs={{0,14},{2,0},{4,2},{6,4},{8,6},{10,8},{12,10},{14,12},{1,15},{3,1}... | collective-permute-start | bytes 1572872 | tf_op jit(solution)/shard_map/ppermute | solution.py:239
  90.7 2.3 %collective-permute-start.25 = (bf16[4,256,128]{2,1,0:T(8,128)(2,1)S(1)}, bf16[4,256,128]{2,1,0:T(8,128)(2,1)S(1)}, u32[]{:S(2)}, u32[]{:S(2)}) collective-permute-start(bf16[4,256,128]{2,1,0:T(8,128)(2,1)S(1)} %get-tuple-element.79), channel_id=1, source_target_pairs={{0,192},{16,208},{32,224},{48,240},{64,0},{80,16},{96,32},{112,48}... | collective-permute-start | bytes 786440 | tf_op jit(solution)/shard_map/ppermute | solution.py:229
  93.0 6.7 %collective-permute-done.24.rv_ref = bf16[4,256,128]{2,1,0:T(8,128)(2,1)S(1)} collective-permute-done((bf16[4,256,128]{2,1,0:T(8,128)(2,1)S(1)}, bf16[4,256,128]{2,1,0:T(8,128)(2,1)S(1)}, u32[]{:S(2)}, u32[]{:S(2)}) %collective-permute-start.24) | collective-permute-done | bytes 262176 | tf_op jit(solution)/shard_map/ppermute | solution.py:229
  99.7 2.8 %collective-permute-done.22.ru_ref = bf16[4,256,128]{2,1,0:T(8,128)(2,1)S(1)} collective-permute-done((bf16[4,256,128]{2,1,0:T(8,128)(2,1)S(1)}, bf16[4,256,128]{2,1,0:T(8,128)(2,1)S(1)}, u32[]{:S(2)}, u32[]{:S(2)}) %collective-permute-start.22) | collective-permute-done | bytes 262176 | tf_op jit(solution)/shard_map/ppermute | solution.py:229
  103.1 3.2 %collective-permute-start.27 = (bf16[512,512]{1,0:T(8,128)(2,1)S(1)}, bf16[512,512]{1,0:T(8,128)(2,1)S(1)}, u32[]{:S(2)}, u32[]{:S(2)}) collective-permute-start(bf16[512,512]{1,0:T(8,128)(2,1)S(1)} %get-tuple-element.81), channel_id=1, source_target_pairs={{0,14},{2,0},{4,2},{6,4},{8,6},{10,8},{12,10},{14,12},{1,15},{3,1}... | collective-permute-start | bytes 1572872 | tf_op jit(solution)/shard_map/ppermute | solution.py:239
  108.4 2.9 %collective-permute-done.28.a_ref = bf16[512,128]{1,0:T(8,128)(2,1)S(1)} collective-permute-done((bf16[512,128]{1,0:T(8,128)(2,1)S(1)}, bf16[512,128]{1,0:T(8,128)(2,1)S(1)}, u32[]{:S(2)}, u32[]{:S(2)}) %collective-permute-start.28) | collective-permute-done | bytes 131104 | tf_op jit(solution)/shard_map/ppermute | solution.py:233
  111.2 2.9 %collective-permute-done.29.b_ref = bf16[512,128]{1,0:T(8,128)(2,1)S(1)} collective-permute-done((bf16[512,128]{1,0:T(8,128)(2,1)S(1)}, bf16[512,128]{1,0:T(8,128)(2,1)S(1)}, u32[]{:S(2)}, u32[]{:S(2)}) %collective-permute-start.29) | collective-permute-done | bytes 131104 | tf_op jit(solution)/shard_map/ppermute | solution.py:233
  (71 shorter events, 36.9 us)
Async XLA Ops:
  0.6 4.5 %collective-permute-start = (bf16[2048,512]{1,0:T(8,128)(2,1)}, bf16[2048,512]{1,0:T(8,128)(2,1)S(1)}, u32[]{:S(2)}, u32[]{:S(2)}) collective-permute-start(bf16[2048,512]{1,0:T(8,128)(2,1)} %refs_1_.1), channel_id=1, source_target_pairs={{0,1},{1,0},{2,3},{3,2},{4,5},{5,4},{6,7},{7,6},{8,9},{9,8},{10,11... | collective-permute-start | bytes 6291464 | tf_op jit(solution)/shard_map/ppermute | solution.py:243
  8.0 4.4 %collective-permute-start.2 = (bf16[256,128]{1,0:T(8,128)(2,1)S(1)}, bf16[256,128]{1,0:T(8,128)(2,1)S(1)}, u32[]{:S(2)}, u32[]{:S(2)}) collective-permute-start(bf16[256,128]{1,0:T(8,128)(2,1)S(1)} %fold.8.a_ref), channel_id=1, source_target_pairs={{0,16},{16,0},{32,48},{48,32},{64,80},{80,64},{96,112},{112,96},{1... | collective-permute-start | bytes 196616 | tf_op jit(solution)/shard_map/ppermute | solution.py:225
  12.4 5.6 %collective-permute-start.3 = (bf16[256,128]{1,0:T(8,128)(2,1)S(1)}, bf16[256,128]{1,0:T(8,128)(2,1)S(1)}, u32[]{:S(2)}, u32[]{:S(2)}) collective-permute-start(bf16[256,128]{1,0:T(8,128)(2,1)S(1)} %fold.9.a_ref), channel_id=1, source_target_pairs={{0,48},{16,32},{32,16},{48,0},{64,112},{80,96},{96,80},{112,64},{1... | collective-permute-start | bytes 196616 | tf_op jit(solution)/shard_map/ppermute | solution.py:225
  22.3 5.6 %collective-permute-start.5 = (bf16[256,128]{1,0:T(8,128)(2,1)S(1)}, bf16[256,128]{1,0:T(8,128)(2,1)S(1)}, u32[]{:S(2)}, u32[]{:S(2)}) collective-permute-start(bf16[256,128]{1,0:T(8,128)(2,1)S(1)} %fold.11), channel_id=1, source_target_pairs={{0,192},{16,208},{32,224},{48,240},{64,128},{80,144},{96,160},{112... | collective-permute-start | bytes 196616 | tf_op jit(solution)/shard_map/ppermute | solution.py:225
  36.2 5.6 %collective-permute-start.9 = (bf16[256,128]{1,0:T(8,128)(2,1)S(1)}, bf16[256,128]{1,0:T(8,128)(2,1)S(1)}, u32[]{:S(2)}, u32[]{:S(2)}) collective-permute-start(bf16[256,128]{1,0:T(8,128)(2,1)S(1)} %fold.13.a_ref), channel_id=1, source_target_pairs={{0,48},{16,32},{32,16},{48,0},{64,112},{80,96},{96,80},{112,64},{1... | collective-permute-start | bytes 196616 | tf_op jit(solution)/shard_map/ppermute | solution.py:225
  46.2 5.6 %collective-permute-start.11 = (bf16[256,128]{1,0:T(8,128)(2,1)S(1)}, bf16[256,128]{1,0:T(8,128)(2,1)S(1)}, u32[]{:S(2)}, u32[]{:S(2)}) collective-permute-start(bf16[256,128]{1,0:T(8,128)(2,1)S(1)} %fold.15), channel_id=1, source_target_pairs={{0,192},{16,208},{32,224},{48,240},{64,128},{80,144},{96,160},{112... | collective-permute-start | bytes 196616 | tf_op jit(solution)/shard_map/ppermute | solution.py:225
  55.7 16.1 %collective-permute-start.13 = (bf16[16,512,128]{2,1,0:T(8,128)(2,1)S(1)}, bf16[16,512,128]{2,1,0:T(8,128)(2,1)S(1)}, u32[]{:S(2)}, u32[]{:S(2)}) collective-permute-start(bf16[16,512,128]{2,1,0:T(8,128)(2,1)S(1)} %get-tuple-element.63), channel_id=1, source_target_pairs={{0,1},{1,0},{2,3},{3,2},{4,5},{5,4},{6,7},{7,6},{8,9},{9,8},{10,11... | collective-permute-start | bytes 6291464 | tf_op jit(solution)/shard_map/ppermute | solution.py:243
  55.9 12.7 %collective-permute-start.14 = (bf16[256,512]{1,0:T(8,128)(2,1)S(1)}, bf16[256,512]{1,0:T(8,128)(2,1)S(1)}, u32[]{:S(2)}, u32[]{:S(2)}) collective-permute-start(bf16[256,512]{1,0:T(8,128)(2,1)S(1)} %get-tuple-element.64), channel_id=1, source_target_pairs={{0,2},{2,4},{4,6},{6,8},{8,10},{10,12},{12,14},{14,0},{1,3},{3,5},... | collective-permute-start | bytes 786440 | tf_op jit(solution)/shard_map/ppermute | solution.py:239
  57.8 10.7 %collective-permute-start.15 = (bf16[256,512]{1,0:T(8,128)(2,1)S(1)}, bf16[256,512]{1,0:T(8,128)(2,1)S(1)}, u32[]{:S(2)}, u32[]{:S(2)}) collective-permute-start(bf16[256,512]{1,0:T(8,128)(2,1)S(1)} %get-tuple-element.65), channel_id=1, source_target_pairs={{0,14},{2,0},{4,2},{6,4},{8,6},{10,8},{12,10},{14,12},{1,15},{3,1}... | collective-permute-start | bytes 786440 | tf_op jit(solution)/shard_map/ppermute | solution.py:239
  68.7 13.9 %collective-permute-start.17 = (bf16[512,512]{1,0:T(8,128)(2,1)S(1)}, bf16[512,512]{1,0:T(8,128)(2,1)S(1)}, u32[]{:S(2)}, u32[]{:S(2)}) collective-permute-start(bf16[512,512]{1,0:T(8,128)(2,1)S(1)} %get-tuple-element.69), channel_id=1, source_target_pairs={{0,14},{2,0},{4,2},{6,4},{8,6},{10,8},{12,10},{14,12},{1,15},{3,1}... | collective-permute-start | bytes 1572872 | tf_op jit(solution)/shard_map/ppermute | solution.py:239
  71.7 14.3 %collective-permute-start.16 = (bf16[512,512]{1,0:T(8,128)(2,1)S(1)}, bf16[512,512]{1,0:T(8,128)(2,1)S(1)}, u32[]{:S(2)}, u32[]{:S(2)}) collective-permute-start(bf16[512,512]{1,0:T(8,128)(2,1)S(1)} %get-tuple-element.67._), channel_id=1, source_target_pairs={{0,2},{2,4},{4,6},{6,8},{8,10},{10,12},{12,14},{14,0},{1,3},{3,5},... | collective-permute-start | bytes 1572872 | tf_op jit(solution)/shard_map/ppermute | solution.py:239
  72.2 13.8 %collective-permute-start.18 = (bf16[4,256,128]{2,1,0:T(8,128)(2,1)S(1)}, bf16[4,256,128]{2,1,0:T(8,128)(2,1)S(1)}, u32[]{:S(2)}, u32[]{:S(2)}) collective-permute-start(bf16[4,256,128]{2,1,0:T(8,128)(2,1)S(1)} %get-tuple-element.71), channel_id=1, source_target_pairs={{0,64},{16,80},{32,96},{48,112},{64,128},{80,144},{96,160},{112,17... | collective-permute-start | bytes 786440 | tf_op jit(solution)/shard_map/ppermute | solution.py:229
  72.3 13.7 %collective-permute-start.19 = (bf16[4,256,128]{2,1,0:T(8,128)(2,1)S(1)}, bf16[4,256,128]{2,1,0:T(8,128)(2,1)S(1)}, u32[]{:S(2)}, u32[]{:S(2)}) collective-permute-start(bf16[4,256,128]{2,1,0:T(8,128)(2,1)S(1)} %get-tuple-element.73), channel_id=1, source_target_pairs={{0,192},{16,208},{32,224},{48,240},{64,0},{80,16},{96,32},{112,48}... | collective-permute-start | bytes 786440 | tf_op jit(solution)/shard_map/ppermute | solution.py:229
  75.5 15.1 %collective-permute-start.23 = (bf16[4,256,128]{2,1,0:T(8,128)(2,1)S(1)}, bf16[4,256,128]{2,1,0:T(8,128)(2,1)S(1)}, u32[]{:S(2)}, u32[]{:S(2)}) collective-permute-start(bf16[4,256,128]{2,1,0:T(8,128)(2,1)S(1)} %get-tuple-element.77), channel_id=1, source_target_pairs={{0,192},{16,208},{32,224},{48,240},{64,0},{80,16},{96,32},{112,48}... | collective-permute-start | bytes 786440 | tf_op jit(solution)/shard_map/ppermute | solution.py:229
  86.4 16.1 %collective-permute-start.20 = (bf16[512,512]{1,0:T(8,128)(2,1)S(1)}, bf16[512,512]{1,0:T(8,128)(2,1)S(1)}, u32[]{:S(2)}, u32[]{:S(2)}) collective-permute-start(bf16[512,512]{1,0:T(8,128)(2,1)S(1)} %get-tuple-element.74), channel_id=1, source_target_pairs={{0,2},{2,4},{4,6},{6,8},{8,10},{10,12},{12,14},{14,0},{1,3},{3,5},... | collective-permute-start | bytes 1572872 | tf_op jit(solution)/shard_map/ppermute | solution.py:239
  86.5 16.0 %collective-permute-start.21 = (bf16[512,512]{1,0:T(8,128)(2,1)S(1)}, bf16[512,512]{1,0:T(8,128)(2,1)S(1)}, u32[]{:S(2)}, u32[]{:S(2)}) collective-permute-start(bf16[512,512]{1,0:T(8,128)(2,1)S(1)} %get-tuple-element.75), channel_id=1, source_target_pairs={{0,14},{2,0},{4,2},{6,4},{8,6},{10,8},{12,10},{14,12},{1,15},{3,1}... | collective-permute-start | bytes 1572872 | tf_op jit(solution)/shard_map/ppermute | solution.py:239
  89.7 10.0 %collective-permute-start.24 = (bf16[4,256,128]{2,1,0:T(8,128)(2,1)S(1)}, bf16[4,256,128]{2,1,0:T(8,128)(2,1)S(1)}, u32[]{:S(2)}, u32[]{:S(2)}) collective-permute-start(bf16[4,256,128]{2,1,0:T(8,128)(2,1)S(1)} %get-tuple-element.78), channel_id=1, source_target_pairs={{0,64},{16,80},{32,96},{48,112},{64,128},{80,144},{96,160},{112,17... | collective-permute-start | bytes 786440 | tf_op jit(solution)/shard_map/ppermute | solution.py:229
  89.7 12.8 %collective-permute-start.22 = (bf16[4,256,128]{2,1,0:T(8,128)(2,1)S(1)}, bf16[4,256,128]{2,1,0:T(8,128)(2,1)S(1)}, u32[]{:S(2)}, u32[]{:S(2)}) collective-permute-start(bf16[4,256,128]{2,1,0:T(8,128)(2,1)S(1)} %get-tuple-element.76), channel_id=1, source_target_pairs={{0,64},{16,80},{32,96},{48,112},{64,128},{80,144},{96,160},{112,17... | collective-permute-start | bytes 786440 | tf_op jit(solution)/shard_map/ppermute | solution.py:229
  90.7 11.9 %collective-permute-start.25 = (bf16[4,256,128]{2,1,0:T(8,128)(2,1)S(1)}, bf16[4,256,128]{2,1,0:T(8,128)(2,1)S(1)}, u32[]{:S(2)}, u32[]{:S(2)}) collective-permute-start(bf16[4,256,128]{2,1,0:T(8,128)(2,1)S(1)} %get-tuple-element.79), channel_id=1, source_target_pairs={{0,192},{16,208},{32,224},{48,240},{64,0},{80,16},{96,32},{112,48}... | collective-permute-start | bytes 786440 | tf_op jit(solution)/shard_map/ppermute | solution.py:229
  103.0 13.2 %collective-permute-start.26 = (bf16[512,512]{1,0:T(8,128)(2,1)S(1)}, bf16[512,512]{1,0:T(8,128)(2,1)S(1)}, u32[]{:S(2)}, u32[]{:S(2)}) collective-permute-start(bf16[512,512]{1,0:T(8,128)(2,1)S(1)} %get-tuple-element.80), channel_id=1, source_target_pairs={{0,2},{2,4},{4,6},{6,8},{8,10},{10,12},{12,14},{14,0},{1,3},{3,5},... | collective-permute-start | bytes 1572872 | tf_op jit(solution)/shard_map/ppermute | solution.py:239
  103.1 13.1 %collective-permute-start.27 = (bf16[512,512]{1,0:T(8,128)(2,1)S(1)}, bf16[512,512]{1,0:T(8,128)(2,1)S(1)}, u32[]{:S(2)}, u32[]{:S(2)}) collective-permute-start(bf16[512,512]{1,0:T(8,128)(2,1)S(1)} %get-tuple-element.81), channel_id=1, source_target_pairs={{0,14},{2,0},{4,2},{6,4},{8,6},{10,8},{12,10},{14,12},{1,15},{3,1}... | collective-permute-start | bytes 1572872 | tf_op jit(solution)/shard_map/ppermute | solution.py:239
  106.3 5.0 %collective-permute-start.28 = (bf16[512,128]{1,0:T(8,128)(2,1)S(1)}, bf16[512,128]{1,0:T(8,128)(2,1)S(1)}, u32[]{:S(2)}, u32[]{:S(2)}) collective-permute-start(bf16[512,128]{1,0:T(8,128)(2,1)S(1)} %get-tuple-element.83), channel_id=1, source_target_pairs={{0,16},{16,32},{32,48},{48,0},{64,80},{80,96},{96,112},{112,64},{1... | collective-permute-start | bytes 393224 | tf_op jit(solution)/shard_map/ppermute | solution.py:233
  107.5 6.6 %collective-permute-start.29 = (bf16[512,128]{1,0:T(8,128)(2,1)S(1)}, bf16[512,128]{1,0:T(8,128)(2,1)S(1)}, u32[]{:S(2)}, u32[]{:S(2)}) collective-permute-start(bf16[512,128]{1,0:T(8,128)(2,1)S(1)} %get-tuple-element.84), channel_id=1, source_target_pairs={{0,32},{16,48},{32,0},{48,16},{64,96},{80,112},{96,64},{112,80},{1... | collective-permute-start | bytes 393224 | tf_op jit(solution)/shard_map/ppermute | solution.py:233
  107.5 7.8 %collective-permute-start.30 = (bf16[512,128]{1,0:T(8,128)(2,1)S(1)}, bf16[512,128]{1,0:T(8,128)(2,1)S(1)}, u32[]{:S(2)}, u32[]{:S(2)}) collective-permute-start(bf16[512,128]{1,0:T(8,128)(2,1)S(1)} %get-tuple-element.85), channel_id=1, source_target_pairs={{0,48},{16,0},{32,16},{48,32},{64,112},{80,64},{96,80},{112,96},{1... | collective-permute-start | bytes 393224 | tf_op jit(solution)/shard_map/ppermute | solution.py:233
  (11 other events, 59.9 us)

commit v2 on v1

--- a/solution.py
+++ b/solution.py
@@ -75,10 +75,10 @@
 
 
 def each_head(ref, body):
-    @pl.loop(0, ref.shape[1] // HDIM)
-    def _(h):
-        at = pl.multiple_of(h * HDIM, HDIM)
-        body(pl.ds(at, HDIM))
+    @pl.loop(0, ref.shape[1] // (2 * HDIM))
+    def _(pair):
+        for h in range(2):
+            body(pl.ds(pl.multiple_of((2 * pair + h) * HDIM, HDIM), HDIM))
 
 
 def tril(scores):
@@ -298,13 +298,17 @@
     weight_pieces(scale, 1 - core(), vg_ref, x_ref, piece_ref)
 
 
-def work_kernel(scale, vg_ref, own_ref, other_ref, x_ref, p_ref, piece_ref):
+def chunks(first, vg_ref, own_ref, other_ref, p_ref):
     @pl.loop(0, p_ref.shape[0])
     def _(i):
         def use(p):
             p_ref[i] = p
 
-        chunk_product(1 + i, vg_ref[...], own_ref, other_ref, use)
+        chunk_product(first + i, vg_ref[...], own_ref, other_ref, use)
+
+
+def work_kernel(scale, vg_ref, own_ref, other_ref, x_ref, p_ref, piece_ref):
+    chunks(1, vg_ref, own_ref, other_ref, p_ref)
     weight_pieces(scale, core(), vg_ref, x_ref, piece_ref)
 
 
@@ -321,15 +325,12 @@
     lo_ref[...] = (wide(l_ref) + p_ref[first + 1].astype(F32)).astype(BF16)
 
 
-def last_turn_kernel(r_ref, l_ref, p_ref, o_ref):
-    o_ref[...] = (p_ref[p_ref.shape[0] - 1].astype(F32) + wide(r_ref) + wide(l_ref)).astype(BF16)
-
-
-def key_grad_kernel(v_ref, kp_ref, state_ref, _, kg_ref):
+def key_grad_kernel(v_ref, kp_ref, state_ref, vg_ref, own_ref, other_ref, _, kg_ref, p_ref):
     def head(c):
         kg_ref[:, c] = (kp_ref[:, c] + dot(v_ref[:, c], state_ref[c, :], NT)).astype(BF16)
 
     each_head(v_ref, head)
+    chunks(3, vg_ref, own_ref, other_ref, p_ref)
 
 
 def weight_pieces(scale, side, vg_ref, x_ref, o_ref):
@@ -369,14 +370,14 @@
     own[...] = s(0)
 
 
-def pair_kernel(r_ref, l_ref, p_ref, a_ref, b_ref, c_ref, d_ref, _, ro_ref, lo_ref, o_ref, q_ref):
-    turn(2, r_ref, l_ref, p_ref, ro_ref, lo_ref)
+def pair_kernel(r_ref, l_ref, p_ref, a_ref, b_ref, c_ref, d_ref, ro_ref, lo_ref, o_ref, q_ref):
+    turn(0, r_ref, l_ref, p_ref, ro_ref, lo_ref)
     o_ref[...] = (wide(a_ref) + wide(b_ref)).astype(BF16)
     q_ref[...] = (wide(c_ref) + wide(d_ref)).astype(BF16)
 
 
 def line_kernel(r_ref, l_ref, p_ref, own_ref, ru_ref, lu_ref, rv_ref, lv_ref, ro_ref, lo_ref, m1, m2, m3, keep):
-    turn(4, r_ref, l_ref, p_ref, ro_ref, lo_ref)
+    turn(2, r_ref, l_ref, p_ref, ro_ref, lo_ref)
     half = ru_ref.shape[1]
     _, y = place()
     for hop, ref in ((1, m1), (2, m2), (3, m3), (0, keep)):
@@ -388,7 +389,8 @@
         ref[half:] = v.astype(ref.dtype)
 
 
-def owner_kernel(keep_ref, a_ref, b_ref, c_ref, o_ref):
+def last_kernel(keep_ref, a_ref, b_ref, c_ref, r_ref, l_ref, p_ref, o_ref, i_ref):
+    i_ref[...] = (p_ref[p_ref.shape[0] - 1].astype(F32) + wide(r_ref) + wide(l_ref)).astype(BF16)
     o_ref[...] = (keep_ref[...] + wide(a_ref) + wide(b_ref) + wide(c_ref)).T
 
 
@@ -464,14 +466,14 @@
     )
     r, l = along_z(r, 1), along_z(l, -1)
     got = swap(other)
-    parts, mine = call(
+    threes, mine = call(
         lambda *refs: work_kernel(scale, *refs),
         [VMEM] * 4,
         [value_grad, value_weight, w_other, x_near],
-        [sds((RING - 1, tok, 512)), pieces],
+        [sds((2, tok, 512)), pieces],
         "work",
     )
-    r, l = call(open_turn_kernel, [VMEM] * 3, [r, l, parts], [full] * 2, "turn")
+    r, l = call(open_turn_kernel, [VMEM] * 3, [r, l, threes], [full] * 2, "turn")
     after = r
     r, l = along_z(r, 1), along_z(l, -1)
 
@@ -486,17 +488,17 @@
     )
     ru2, lv2 = along_x_ring(ru2, 1), along_x_ring(lv2, -1)
     rv1, lu1 = along_x_ring(rv1, 1), along_x_ring(lu1, -1)
-    (key_grad,) = call(
+    key_grad, parts = call(
         key_grad_kernel,
-        [VMEM] * 3 + [ANY],
-        [value, key_part, state_grad, own],
-        [square],
+        [VMEM] * 6 + [ANY],
+        [value, key_part, state_grad, value_grad, value_weight, w_other, own],
+        [square, sds((5, tok, 512))],
         "key_grad",
     )
     r, l, ru1, lv1 = call(
         pair_kernel,
-        [VMEM] * 7 + [HBM],
-        [r, l, parts, cu1, ru2, cv1, lv2, in_hbm(key_grad)],
+        [VMEM] * 7,
+        [r, l, parts, cu1, ru2, cv1, lv2],
         [full] * 2 + [piece] * 2,
         "pair",
     )
@@ -511,10 +513,13 @@
     )
     r, l = along_z(r, 1), along_z(l, -1)
     got = [along_y_ring(m, k) for m, k in zip((m1, m2, m3), (1, 2, 3))]
-    (weight_grad,) = call(
-        owner_kernel, [VMEM] * 4, [keep, *got], [sds((128, cols), F32)], "owner"
-    )
-    (input_grad,) = call(last_turn_kernel, [VMEM] * 3, [r, l, parts], [full], "last_turn")
+    weight_grad, input_grad = call(
+        last_kernel,
+        [VMEM] * 7,
+        [keep, *got, r, l, parts],
+        [sds((128, cols), F32), full],
+        "last",
+    )
     return (query_grad, key_grad, input_grad, weight_grad)
 
 

time: 117 us -> 117 us (level)
  Pallas kernels: 26.3 us -> 23.6 us
  waiting for transfers between devices: 50.6 us -> 52.3 us
    pallas_call x25 -> x24, Pallas kernels: 26.3 us -> 23.6 us  [call(): pl.pallas_call(body, out_shape=tuple(outs), in_specs=specs, out_specs=tup...]
    ppermute x8, waiting for transfers between devices: 18.8 us -> 20.5 us  [along(): return lax.ppermute(a, 'ctx', [(i, other(i)) for i in range(SIDE * SIDE)])]
  transfers between devices with their start and end apart: 31 -> 31, of which waited for: 20 -> 21; matrix products, arithmetic and copies ran while one was open for 0% -> 0% of each run, Pallas kernels for 17% -> 14%
where the time goes in v2:
time: 117 us; the launch traced here: 116 us
  waiting for transfers between devices  52.3 us (45%)
  starting transfers between devices  39.7 us (34%)
  Pallas kernels  23.6 us (20%)
    pallas_call x24, Pallas kernels, call(): pl.pallas_call(body, out_shape=tuple(outs), in_specs=specs, out_specs=tup...  23.6 us
    ppermute x8, waiting for transfers between devices, along(): return lax.ppermute(a, 'ctx', [(i, other(i)) for i in range(SIDE * SIDE)])  20.5 us
    ppermute x8, starting transfers between devices, along_z(): return lax.ppermute(a, 'head', [(i, (i + k) % RING) for i in range(RING)])  15.7 us
    ppermute x8, starting transfers between devices, along(): return lax.ppermute(a, 'ctx', [(i, other(i)) for i in range(SIDE * SIDE)])  12.8 us
    ppermute x6, waiting for transfers between devices, along_x_ring(): return lax.ppermute(a, 'ctx', [(i, (i + SIDE * k) % 16) for i in range(16)])  9.55 us
    ppermute x8, waiting for transfers between devices, along_z(): return lax.ppermute(a, 'head', [(i, (i + k) % RING) for i in range(RING)])  9.5 us
    ppermute x6, starting transfers between devices, along_x_ring(): return lax.ppermute(a, 'ctx', [(i, (i + SIDE * k) % 16) for i in range(16)])  8.12 us
    ppermute x3, waiting for transfers between devices, along_y_ring(): lax.ppermute(a, 'ctx', [(i, i // SIDE * SIDE + (i + k) % SIDE) for i in r...  6.68 us
  transfers between devices with their start and end apart: 31, of which 21 were waited for; matrix products, arithmetic and copies ran while one was open for 0% of the time, Pallas kernels for 14%

profile of v2, /device:TPU:24, one launch (start us, length us, event | category | flops | bytes accessed | tf_op | source)
XLA Modules:
  0.0 116.5 jit_solution(18148410749840799747)
XLA Ops:
  0.7 2.9 %value_own.1 = (bf16[512,4096]{1,0:T(8,128)(2,1)S(1)}, f32[512,512]{1,0:T(8,128)S(1)}) custom-call(bf16[512,4096]{1,0:T(8,128)(2,1)} %x_hbm.1, bf16[2048,512]{1,0:T(8,128)(2,1)} %own_ref.1), custom_call_target="tpu_custom_call" | custom-call | flops 1000 | bytes 11534336 | tf_op jit(solution)/shard_map/value_own/pallas_call | solution.py:52
  14.4 3.5 %collective-permute-done.3.b_ref.refs_3_ = bf16[256,128]{1,0:T(8,128)(2,1)S(1)} collective-permute-done((bf16[256,128]{1,0:T(8,128)(2,1)S(1)}, bf16[256,128]{1,0:T(8,128)(2,1)S(1)}, u32[]{:S(2)}, u32[]{:S(2)}) %collective-permute-start.3) | collective-permute-done | bytes 65568 | tf_op jit(solution)/shard_map/ppermute | solution.py:225
  19.5 2.8 %collective-permute-done.4.b_ref.refs_4_ = bf16[256,128]{1,0:T(8,128)(2,1)S(1)} collective-permute-done((bf16[256,128]{1,0:T(8,128)(2,1)S(1)}, bf16[256,128]{1,0:T(8,128)(2,1)S(1)}, u32[]{:S(2)}, u32[]{:S(2)}) %collective-permute-start.4) | collective-permute-done | bytes 65568 | tf_op jit(solution)/shard_map/ppermute | solution.py:225
  22.3 2.8 %collective-permute-start.5 = (bf16[256,128]{1,0:T(8,128)(2,1)S(1)}, bf16[256,128]{1,0:T(8,128)(2,1)S(1)}, u32[]{:S(2)}, u32[]{:S(2)}) collective-permute-start(bf16[256,128]{1,0:T(8,128)(2,1)S(1)} %fold.11), channel_id=1, source_target_pairs={{0,192},{16,208},{32,224},{48,240},{64,128},{80,144},{96,160},{112... | collective-permute-start | bytes 196616 | tf_op jit(solution)/shard_map/ppermute | solution.py:225
  25.2 2.7 %collective-permute-done.5.refs_5_ = bf16[256,128]{1,0:T(8,128)(2,1)S(1)} collective-permute-done((bf16[256,128]{1,0:T(8,128)(2,1)S(1)}, bf16[256,128]{1,0:T(8,128)(2,1)S(1)}, u32[]{:S(2)}, u32[]{:S(2)}) %collective-permute-start.5) | collective-permute-done | bytes 65568 | tf_op jit(solution)/shard_map/ppermute | solution.py:225
  33.8 2.4 %collective-permute-done.8.b_ref.refs_2_ = bf16[256,128]{1,0:T(8,128)(2,1)S(1)} collective-permute-done((bf16[256,128]{1,0:T(8,128)(2,1)S(1)}, bf16[256,128]{1,0:T(8,128)(2,1)S(1)}, u32[]{:S(2)}, u32[]{:S(2)}) %collective-permute-start.8) | collective-permute-done | bytes 65568 | tf_op jit(solution)/shard_map/ppermute | solution.py:225
  38.3 3.1 %cross.1 = (bf16[512,512]{1,0:T(8,128)(2,1)}, f32[512,512]{1,0:T(8,128)S(1)}) custom-call(bf16[512,512]{1,0:T(8,128)(2,1)S(1)} %copy-done.2, bf16[512,512]{1,0:T(8,128)(2,1)S(1)} %copy-done.1, bf16[512,512]{1,0:T(8,128)(2,1)S(1)} %get-tuple-element.51.v_ref, bf16[512,512]{1,0:T(8,128)(2,1)S(1)} %get-tuple-element.56.low_ref, ...), custom_call_target="tpu_custom_call" | custom-call | flops 1000 | bytes 3801088 | tf_op jit(solution)/shard_map/cross/pallas_call | solution.py:52
  42.2 4.0 %collective-permute-done.10.b_ref.refs_4_ = bf16[256,128]{1,0:T(8,128)(2,1)S(1)} collective-permute-done((bf16[256,128]{1,0:T(8,128)(2,1)S(1)}, bf16[256,128]{1,0:T(8,128)(2,1)S(1)}, u32[]{:S(2)}, u32[]{:S(2)}) %collective-permute-start.10) | collective-permute-done | bytes 65568 | tf_op jit(solution)/shard_map/ppermute | solution.py:225
  46.2 3.0 %collective-permute-start.11 = (bf16[256,128]{1,0:T(8,128)(2,1)S(1)}, bf16[256,128]{1,0:T(8,128)(2,1)S(1)}, u32[]{:S(2)}, u32[]{:S(2)}) collective-permute-start(bf16[256,128]{1,0:T(8,128)(2,1)S(1)} %fold.15), channel_id=1, source_target_pairs={{0,192},{16,208},{32,224},{48,240},{64,128},{80,144},{96,160},{112... | collective-permute-start | bytes 196616 | tf_op jit(solution)/shard_map/ppermute | solution.py:225
  49.2 2.7 %collective-permute-done.11.refs_5_ = bf16[256,128]{1,0:T(8,128)(2,1)S(1)} collective-permute-done((bf16[256,128]{1,0:T(8,128)(2,1)S(1)}, bf16[256,128]{1,0:T(8,128)(2,1)S(1)}, u32[]{:S(2)}, u32[]{:S(2)}) %collective-permute-start.11) | collective-permute-done | bytes 65568 | tf_op jit(solution)/shard_map/ppermute | solution.py:225
  57.8 3.9 %collective-permute-start.15 = (bf16[256,512]{1,0:T(8,128)(2,1)S(1)}, bf16[256,512]{1,0:T(8,128)(2,1)S(1)}, u32[]{:S(2)}, u32[]{:S(2)}) collective-permute-start(bf16[256,512]{1,0:T(8,128)(2,1)S(1)} %get-tuple-element.69), channel_id=1, source_target_pairs={{0,14},{2,0},{4,2},{6,4},{8,6},{10,8},{12,10},{14,12},{1,15},{3,1}... | collective-permute-start | bytes 786440 | tf_op jit(solution)/shard_map/ppermute | solution.py:239
  61.8 2.4 %work.1 = (bf16[2,512,512]{2,1,0:T(8,128)(2,1)S(1)}, bf16[16,512,128]{2,1,0:T(8,128)(2,1)S(1)}) custom-call(bf16[512,512]{1,0:T(8,128)(2,1)S(1)} %get-tuple-element.65.refs_0_.vg_ref, bf16[2048,512]{1,0:T(8,128)(2,1)S(1)} %copy-done, bf16[2048,512]{1,0:T(8,128)(2,1)S(1)} %collective-permute-done.w_ref.refs_5_.refs_2_.other_ref, ...), custom_call_target="tpu_custom_call" | custom-call | flops 1000 | bytes 12058624 | tf_op jit(solution)/shard_map/work/pallas_call | solution.py:52
  64.2 4.4 %collective-permute-done.14.r_ref = bf16[256,512]{1,0:T(8,128)(2,1)S(1)} collective-permute-done((bf16[256,512]{1,0:T(8,128)(2,1)S(1)}, bf16[256,512]{1,0:T(8,128)(2,1)S(1)}, u32[]{:S(2)}, u32[]{:S(2)}) %collective-permute-start.14) | collective-permute-done | bytes 262176 | tf_op jit(solution)/shard_map/ppermute | solution.py:239
  68.7 3.0 %collective-permute-start.17 = (bf16[512,512]{1,0:T(8,128)(2,1)S(1)}, bf16[512,512]{1,0:T(8,128)(2,1)S(1)}, u32[]{:S(2)}, u32[]{:S(2)}) collective-permute-start(bf16[512,512]{1,0:T(8,128)(2,1)S(1)} %get-tuple-element.74), channel_id=1, source_target_pairs={{0,14},{2,0},{4,2},{6,4},{8,6},{10,8},{12,10},{14,12},{1,15},{3,1}... | collective-permute-start | bytes 1572872 | tf_op jit(solution)/shard_map/ppermute | solution.py:239
  72.3 3.2 %collective-permute-start.19 = (bf16[4,256,128]{2,1,0:T(8,128)(2,1)S(1)}, bf16[4,256,128]{2,1,0:T(8,128)(2,1)S(1)}, u32[]{:S(2)}, u32[]{:S(2)}) collective-permute-start(bf16[4,256,128]{2,1,0:T(8,128)(2,1)S(1)} %get-tuple-element.79), channel_id=1, source_target_pairs={{0,192},{16,208},{32,224},{48,240},{64,0},{80,16},{96,32},{112,48}... | collective-permute-start | bytes 786440 | tf_op jit(solution)/shard_map/ppermute | solution.py:229
  77.1 3.8 %key_grad.1 = (bf16[512,512]{1,0:T(8,128)(2,1)}, bf16[5,512,512]{2,1,0:T(8,128)(2,1)S(1)}) custom-call(bf16[512,512]{1,0:T(8,128)(2,1)S(1)} %get-tuple-element.51.v_ref, f32[512,512]{1,0:T(8,128)S(1)} %get-tuple-element.59._.kp_ref, bf16[512,128]{1,0:T(8,128)(2,1)S(1)} %get-tuple-element.64.state_ref, bf16[512,512]{1,0:T(8,128)(2,1)S(1)} %get-tuple-element.65.refs_0_.vg_ref, ...), custom_call_target="tpu_custom_call" | custom-call | flops 1000 | bytes 10092544 | tf_op jit(solution)/shard_map/key_grad/pallas_call | solution.py:52
  82.6 3.4 %collective-permute-done.16.r_ref = bf16[512,512]{1,0:T(8,128)(2,1)S(1)} collective-permute-done((bf16[512,512]{1,0:T(8,128)(2,1)S(1)}, bf16[512,512]{1,0:T(8,128)(2,1)S(1)}, u32[]{:S(2)}, u32[]{:S(2)}) %collective-permute-start.16) | collective-permute-done | bytes 524320 | tf_op jit(solution)/shard_map/ppermute | solution.py:239
  86.7 3.2 %collective-permute-start.21 = (bf16[512,512]{1,0:T(8,128)(2,1)S(1)}, bf16[512,512]{1,0:T(8,128)(2,1)S(1)}, u32[]{:S(2)}, u32[]{:S(2)}) collective-permute-start(bf16[512,512]{1,0:T(8,128)(2,1)S(1)} %get-tuple-element.81), channel_id=1, source_target_pairs={{0,14},{2,0},{4,2},{6,4},{8,6},{10,8},{12,10},{14,12},{1,15},{3,1}... | collective-permute-start | bytes 1572872 | tf_op jit(solution)/shard_map/ppermute | solution.py:239
  90.9 2.3 %collective-permute-start.25 = (bf16[4,256,128]{2,1,0:T(8,128)(2,1)S(1)}, bf16[4,256,128]{2,1,0:T(8,128)(2,1)S(1)}, u32[]{:S(2)}, u32[]{:S(2)}) collective-permute-start(bf16[4,256,128]{2,1,0:T(8,128)(2,1)S(1)} %get-tuple-element.85), channel_id=1, source_target_pairs={{0,192},{16,208},{32,224},{48,240},{64,0},{80,16},{96,32},{112,48}... | collective-permute-start | bytes 786440 | tf_op jit(solution)/shard_map/ppermute | solution.py:229
  93.2 6.7 %collective-permute-done.24.rv_ref = bf16[4,256,128]{2,1,0:T(8,128)(2,1)S(1)} collective-permute-done((bf16[4,256,128]{2,1,0:T(8,128)(2,1)S(1)}, bf16[4,256,128]{2,1,0:T(8,128)(2,1)S(1)}, u32[]{:S(2)}, u32[]{:S(2)}) %collective-permute-start.24) | collective-permute-done | bytes 262176 | tf_op jit(solution)/shard_map/ppermute | solution.py:229
  99.9 2.8 %collective-permute-done.22.ru_ref = bf16[4,256,128]{2,1,0:T(8,128)(2,1)S(1)} collective-permute-done((bf16[4,256,128]{2,1,0:T(8,128)(2,1)S(1)}, bf16[4,256,128]{2,1,0:T(8,128)(2,1)S(1)}, u32[]{:S(2)}, u32[]{:S(2)}) %collective-permute-start.22) | collective-permute-done | bytes 262176 | tf_op jit(solution)/shard_map/ppermute | solution.py:229
  103.3 3.2 %collective-permute-start.30 = (bf16[512,512]{1,0:T(8,128)(2,1)S(1)}, bf16[512,512]{1,0:T(8,128)(2,1)S(1)}, u32[]{:S(2)}, u32[]{:S(2)}) collective-permute-start(bf16[512,512]{1,0:T(8,128)(2,1)S(1)} %get-tuple-element.91), channel_id=1, source_target_pairs={{0,14},{2,0},{4,2},{6,4},{8,6},{10,8},{12,10},{14,12},{1,15},{3,1}... | collective-permute-start | bytes 1572872 | tf_op jit(solution)/shard_map/ppermute | solution.py:239
  108.5 2.9 %collective-permute-done.26.a_ref = bf16[512,128]{1,0:T(8,128)(2,1)S(1)} collective-permute-done((bf16[512,128]{1,0:T(8,128)(2,1)S(1)}, bf16[512,128]{1,0:T(8,128)(2,1)S(1)}, u32[]{:S(2)}, u32[]{:S(2)}) %collective-permute-start.26) | collective-permute-done | bytes 131104 | tf_op jit(solution)/shard_map/ppermute | solution.py:233
  111.5 2.4 %collective-permute-done.27.b_ref = bf16[512,128]{1,0:T(8,128)(2,1)S(1)} collective-permute-done((bf16[512,128]{1,0:T(8,128)(2,1)S(1)}, bf16[512,128]{1,0:T(8,128)(2,1)S(1)}, u32[]{:S(2)}, u32[]{:S(2)}) %collective-permute-start.27) | collective-permute-done | bytes 131104 | tf_op jit(solution)/shard_map/ppermute | solution.py:233
  (70 shorter events, 37.7 us)
Async XLA Ops:
  0.6 4.5 %collective-permute-start = (bf16[2048,512]{1,0:T(8,128)(2,1)}, bf16[2048,512]{1,0:T(8,128)(2,1)S(1)}, u32[]{:S(2)}, u32[]{:S(2)}) collective-permute-start(bf16[2048,512]{1,0:T(8,128)(2,1)} %own_ref.1), channel_id=1, source_target_pairs={{0,1},{1,0},{2,3},{3,2},{4,5},{5,4},{6,7},{7,6},{8,9},{9,8},{10,11... | collective-permute-start | bytes 6291464 | tf_op jit(solution)/shard_map/ppermute | solution.py:243
  8.0 4.4 %collective-permute-start.2 = (bf16[256,128]{1,0:T(8,128)(2,1)S(1)}, bf16[256,128]{1,0:T(8,128)(2,1)S(1)}, u32[]{:S(2)}, u32[]{:S(2)}) collective-permute-start(bf16[256,128]{1,0:T(8,128)(2,1)S(1)} %fold.8.a_ref), channel_id=1, source_target_pairs={{0,16},{16,0},{32,48},{48,32},{64,80},{80,64},{96,112},{112,96},{1... | collective-permute-start | bytes 196616 | tf_op jit(solution)/shard_map/ppermute | solution.py:225
  12.4 5.6 %collective-permute-start.3 = (bf16[256,128]{1,0:T(8,128)(2,1)S(1)}, bf16[256,128]{1,0:T(8,128)(2,1)S(1)}, u32[]{:S(2)}, u32[]{:S(2)}) collective-permute-start(bf16[256,128]{1,0:T(8,128)(2,1)S(1)} %fold.9.a_ref), channel_id=1, source_target_pairs={{0,48},{16,32},{32,16},{48,0},{64,112},{80,96},{96,80},{112,64},{1... | collective-permute-start | bytes 196616 | tf_op jit(solution)/shard_map/ppermute | solution.py:225
  22.3 5.6 %collective-permute-start.5 = (bf16[256,128]{1,0:T(8,128)(2,1)S(1)}, bf16[256,128]{1,0:T(8,128)(2,1)S(1)}, u32[]{:S(2)}, u32[]{:S(2)}) collective-permute-start(bf16[256,128]{1,0:T(8,128)(2,1)S(1)} %fold.11), channel_id=1, source_target_pairs={{0,192},{16,208},{32,224},{48,240},{64,128},{80,144},{96,160},{112... | collective-permute-start | bytes 196616 | tf_op jit(solution)/shard_map/ppermute | solution.py:225
  36.2 5.6 %collective-permute-start.9 = (bf16[256,128]{1,0:T(8,128)(2,1)S(1)}, bf16[256,128]{1,0:T(8,128)(2,1)S(1)}, u32[]{:S(2)}, u32[]{:S(2)}) collective-permute-start(bf16[256,128]{1,0:T(8,128)(2,1)S(1)} %fold.13.a_ref), channel_id=1, source_target_pairs={{0,48},{16,32},{32,16},{48,0},{64,112},{80,96},{96,80},{112,64},{1... | collective-permute-start | bytes 196616 | tf_op jit(solution)/shard_map/ppermute | solution.py:225
  46.2 5.7 %collective-permute-start.11 = (bf16[256,128]{1,0:T(8,128)(2,1)S(1)}, bf16[256,128]{1,0:T(8,128)(2,1)S(1)}, u32[]{:S(2)}, u32[]{:S(2)}) collective-permute-start(bf16[256,128]{1,0:T(8,128)(2,1)S(1)} %fold.15), channel_id=1, source_target_pairs={{0,192},{16,208},{32,224},{48,240},{64,128},{80,144},{96,160},{112... | collective-permute-start | bytes 196616 | tf_op jit(solution)/shard_map/ppermute | solution.py:225
  55.7 16.1 %collective-permute-start.13 = (bf16[16,512,128]{2,1,0:T(8,128)(2,1)S(1)}, bf16[16,512,128]{2,1,0:T(8,128)(2,1)S(1)}, u32[]{:S(2)}, u32[]{:S(2)}) collective-permute-start(bf16[16,512,128]{2,1,0:T(8,128)(2,1)S(1)} %get-tuple-element.67), channel_id=1, source_target_pairs={{0,1},{1,0},{2,3},{3,2},{4,5},{5,4},{6,7},{7,6},{8,9},{9,8},{10,11... | collective-permute-start | bytes 6291464 | tf_op jit(solution)/shard_map/ppermute | solution.py:243
  55.9 12.7 %collective-permute-start.14 = (bf16[256,512]{1,0:T(8,128)(2,1)S(1)}, bf16[256,512]{1,0:T(8,128)(2,1)S(1)}, u32[]{:S(2)}, u32[]{:S(2)}) collective-permute-start(bf16[256,512]{1,0:T(8,128)(2,1)S(1)} %get-tuple-element.68), channel_id=1, source_target_pairs={{0,2},{2,4},{4,6},{6,8},{8,10},{10,12},{12,14},{14,0},{1,3},{3,5},... | collective-permute-start | bytes 786440 | tf_op jit(solution)/shard_map/ppermute | solution.py:239
  57.8 10.7 %collective-permute-start.15 = (bf16[256,512]{1,0:T(8,128)(2,1)S(1)}, bf16[256,512]{1,0:T(8,128)(2,1)S(1)}, u32[]{:S(2)}, u32[]{:S(2)}) collective-permute-start(bf16[256,512]{1,0:T(8,128)(2,1)S(1)} %get-tuple-element.69), channel_id=1, source_target_pairs={{0,14},{2,0},{4,2},{6,4},{8,6},{10,8},{12,10},{14,12},{1,15},{3,1}... | collective-permute-start | bytes 786440 | tf_op jit(solution)/shard_map/ppermute | solution.py:239
  68.7 13.9 %collective-permute-start.17 = (bf16[512,512]{1,0:T(8,128)(2,1)S(1)}, bf16[512,512]{1,0:T(8,128)(2,1)S(1)}, u32[]{:S(2)}, u32[]{:S(2)}) collective-permute-start(bf16[512,512]{1,0:T(8,128)(2,1)S(1)} %get-tuple-element.74), channel_id=1, source_target_pairs={{0,14},{2,0},{4,2},{6,4},{8,6},{10,8},{12,10},{14,12},{1,15},{3,1}... | collective-permute-start | bytes 1572872 | tf_op jit(solution)/shard_map/ppermute | solution.py:239
  71.7 14.3 %collective-permute-start.16 = (bf16[512,512]{1,0:T(8,128)(2,1)S(1)}, bf16[512,512]{1,0:T(8,128)(2,1)S(1)}, u32[]{:S(2)}, u32[]{:S(2)}) collective-permute-start(bf16[512,512]{1,0:T(8,128)(2,1)S(1)} %get-tuple-element.71._), channel_id=1, source_target_pairs={{0,2},{2,4},{4,6},{6,8},{8,10},{10,12},{12,14},{14,0},{1,3},{3,5},... | collective-permute-start | bytes 1572872 | tf_op jit(solution)/shard_map/ppermute | solution.py:239
  72.2 13.8 %collective-permute-start.18 = (bf16[4,256,128]{2,1,0:T(8,128)(2,1)S(1)}, bf16[4,256,128]{2,1,0:T(8,128)(2,1)S(1)}, u32[]{:S(2)}, u32[]{:S(2)}) collective-permute-start(bf16[4,256,128]{2,1,0:T(8,128)(2,1)S(1)} %get-tuple-element.77), channel_id=1, source_target_pairs={{0,64},{16,80},{32,96},{48,112},{64,128},{80,144},{96,160},{112,17... | collective-permute-start | bytes 786440 | tf_op jit(solution)/shard_map/ppermute | solution.py:229
  72.3 13.7 %collective-permute-start.19 = (bf16[4,256,128]{2,1,0:T(8,128)(2,1)S(1)}, bf16[4,256,128]{2,1,0:T(8,128)(2,1)S(1)}, u32[]{:S(2)}, u32[]{:S(2)}) collective-permute-start(bf16[4,256,128]{2,1,0:T(8,128)(2,1)S(1)} %get-tuple-element.79), channel_id=1, source_target_pairs={{0,192},{16,208},{32,224},{48,240},{64,0},{80,16},{96,32},{112,48}... | collective-permute-start | bytes 786440 | tf_op jit(solution)/shard_map/ppermute | solution.py:229
  75.5 15.4 %collective-permute-start.23 = (bf16[4,256,128]{2,1,0:T(8,128)(2,1)S(1)}, bf16[4,256,128]{2,1,0:T(8,128)(2,1)S(1)}, u32[]{:S(2)}, u32[]{:S(2)}) collective-permute-start(bf16[4,256,128]{2,1,0:T(8,128)(2,1)S(1)} %get-tuple-element.83), channel_id=1, source_target_pairs={{0,192},{16,208},{32,224},{48,240},{64,0},{80,16},{96,32},{112,48}... | collective-permute-start | bytes 786440 | tf_op jit(solution)/shard_map/ppermute | solution.py:229
  86.4 16.4 %collective-permute-start.20 = (bf16[512,512]{1,0:T(8,128)(2,1)S(1)}, bf16[512,512]{1,0:T(8,128)(2,1)S(1)}, u32[]{:S(2)}, u32[]{:S(2)}) collective-permute-start(bf16[512,512]{1,0:T(8,128)(2,1)S(1)} %get-tuple-element.80), channel_id=1, source_target_pairs={{0,2},{2,4},{4,6},{6,8},{8,10},{10,12},{12,14},{14,0},{1,3},{3,5},... | collective-permute-start | bytes 1572872 | tf_op jit(solution)/shard_map/ppermute | solution.py:239
  86.7 16.0 %collective-permute-start.21 = (bf16[512,512]{1,0:T(8,128)(2,1)S(1)}, bf16[512,512]{1,0:T(8,128)(2,1)S(1)}, u32[]{:S(2)}, u32[]{:S(2)}) collective-permute-start(bf16[512,512]{1,0:T(8,128)(2,1)S(1)} %get-tuple-element.81), channel_id=1, source_target_pairs={{0,14},{2,0},{4,2},{6,4},{8,6},{10,8},{12,10},{14,12},{1,15},{3,1}... | collective-permute-start | bytes 1572872 | tf_op jit(solution)/shard_map/ppermute | solution.py:239
  89.9 10.0 %collective-permute-start.24 = (bf16[4,256,128]{2,1,0:T(8,128)(2,1)S(1)}, bf16[4,256,128]{2,1,0:T(8,128)(2,1)S(1)}, u32[]{:S(2)}, u32[]{:S(2)}) collective-permute-start(bf16[4,256,128]{2,1,0:T(8,128)(2,1)S(1)} %get-tuple-element.84), channel_id=1, source_target_pairs={{0,64},{16,80},{32,96},{48,112},{64,128},{80,144},{96,160},{112,17... | collective-permute-start | bytes 786440 | tf_op jit(solution)/shard_map/ppermute | solution.py:229
  89.9 12.8 %collective-permute-start.22 = (bf16[4,256,128]{2,1,0:T(8,128)(2,1)S(1)}, bf16[4,256,128]{2,1,0:T(8,128)(2,1)S(1)}, u32[]{:S(2)}, u32[]{:S(2)}) collective-permute-start(bf16[4,256,128]{2,1,0:T(8,128)(2,1)S(1)} %get-tuple-element.82), channel_id=1, source_target_pairs={{0,64},{16,80},{32,96},{48,112},{64,128},{80,144},{96,160},{112,17... | collective-permute-start | bytes 786440 | tf_op jit(solution)/shard_map/ppermute | solution.py:229
  90.9 11.9 %collective-permute-start.25 = (bf16[4,256,128]{2,1,0:T(8,128)(2,1)S(1)}, bf16[4,256,128]{2,1,0:T(8,128)(2,1)S(1)}, u32[]{:S(2)}, u32[]{:S(2)}) collective-permute-start(bf16[4,256,128]{2,1,0:T(8,128)(2,1)S(1)} %get-tuple-element.85), channel_id=1, source_target_pairs={{0,192},{16,208},{32,224},{48,240},{64,0},{80,16},{96,32},{112,48}... | collective-permute-start | bytes 786440 | tf_op jit(solution)/shard_map/ppermute | solution.py:229
  103.2 12.0 %collective-permute-start.29 = (bf16[512,512]{1,0:T(8,128)(2,1)S(1)}, bf16[512,512]{1,0:T(8,128)(2,1)S(1)}, u32[]{:S(2)}, u32[]{:S(2)}) collective-permute-start(bf16[512,512]{1,0:T(8,128)(2,1)S(1)} %get-tuple-element.90), channel_id=1, source_target_pairs={{0,2},{2,4},{4,6},{6,8},{8,10},{10,12},{12,14},{14,0},{1,3},{3,5},... | collective-permute-start | bytes 1572872 | tf_op jit(solution)/shard_map/ppermute | solution.py:239
  103.3 11.9 %collective-permute-start.30 = (bf16[512,512]{1,0:T(8,128)(2,1)S(1)}, bf16[512,512]{1,0:T(8,128)(2,1)S(1)}, u32[]{:S(2)}, u32[]{:S(2)}) collective-permute-start(bf16[512,512]{1,0:T(8,128)(2,1)S(1)} %get-tuple-element.91), channel_id=1, source_target_pairs={{0,14},{2,0},{4,2},{6,4},{8,6},{10,8},{12,10},{14,12},{1,15},{3,1}... | collective-permute-start | bytes 1572872 | tf_op jit(solution)/shard_map/ppermute | solution.py:239
  106.5 5.0 %collective-permute-start.26 = (bf16[512,128]{1,0:T(8,128)(2,1)S(1)}, bf16[512,128]{1,0:T(8,128)(2,1)S(1)}, u32[]{:S(2)}, u32[]{:S(2)}) collective-permute-start(bf16[512,128]{1,0:T(8,128)(2,1)S(1)} %get-tuple-element.87), channel_id=1, source_target_pairs={{0,16},{16,32},{32,48},{48,0},{64,80},{80,96},{96,112},{112,64},{1... | collective-permute-start | bytes 393224 | tf_op jit(solution)/shard_map/ppermute | solution.py:233
  107.3 6.6 %collective-permute-start.27 = (bf16[512,128]{1,0:T(8,128)(2,1)S(1)}, bf16[512,128]{1,0:T(8,128)(2,1)S(1)}, u32[]{:S(2)}, u32[]{:S(2)}) collective-permute-start(bf16[512,128]{1,0:T(8,128)(2,1)S(1)} %get-tuple-element.88), channel_id=1, source_target_pairs={{0,32},{16,48},{32,0},{48,16},{64,96},{80,112},{96,64},{112,80},{1... | collective-permute-start | bytes 393224 | tf_op jit(solution)/shard_map/ppermute | solution.py:233
  107.5 7.7 %collective-permute-start.28 = (bf16[512,128]{1,0:T(8,128)(2,1)S(1)}, bf16[512,128]{1,0:T(8,128)(2,1)S(1)}, u32[]{:S(2)}, u32[]{:S(2)}) collective-permute-start(bf16[512,128]{1,0:T(8,128)(2,1)S(1)} %get-tuple-element.89), channel_id=1, source_target_pairs={{0,48},{16,0},{32,16},{48,32},{64,112},{80,64},{96,80},{112,96},{1... | collective-permute-start | bytes 393224 | tf_op jit(solution)/shard_map/ppermute | solution.py:233
  (11 other events, 60.6 us)

commit v3 on v2

--- a/solution.py
+++ b/solution.py
@@ -349,7 +349,7 @@
             o_ref[first + p] = res[:, p * 128 : p * 128 + 128]
 
 
-def chip_kernel(a_ref, b_ref, _, ru2, lv2, rv1, lu1, cu1, cv1, own):
+def chip_kernel(a_ref, b_ref, _, right, left, cu1, cv1, own):
     half = own.shape[1] // 2
 
     x, _ = place()
@@ -359,32 +359,32 @@
         return (a_ref[i].astype(F32) + b_ref[i].astype(F32)).astype(BF16)
 
     t = s(2)
-    ru2[...] = t[:, :half]
-    lv2[...] = t[:, half:]
+    right[0] = t[:, :half]
+    left[0] = t[:, half:]
     t = s(1)
     cu1[...] = t[:, :half]
-    rv1[...] = t[:, half:]
+    right[1] = t[:, half:]
     t = s(3)
-    lu1[...] = t[:, :half]
+    left[1] = t[:, :half]
     cv1[...] = t[:, half:]
     own[...] = s(0)
 
 
 def pair_kernel(r_ref, l_ref, p_ref, a_ref, b_ref, c_ref, d_ref, ro_ref, lo_ref, o_ref, q_ref):
     turn(0, r_ref, l_ref, p_ref, ro_ref, lo_ref)
-    o_ref[...] = (wide(a_ref) + wide(b_ref)).astype(BF16)
-    q_ref[...] = (wide(c_ref) + wide(d_ref)).astype(BF16)
-
-
-def line_kernel(r_ref, l_ref, p_ref, own_ref, ru_ref, lu_ref, rv_ref, lv_ref, ro_ref, lo_ref, m1, m2, m3, keep):
+    o_ref[...] = (wide(a_ref) + b_ref[0].astype(F32)).astype(BF16)
+    q_ref[...] = (wide(c_ref) + d_ref[0].astype(F32)).astype(BF16)
+
+
+def line_kernel(r_ref, l_ref, p_ref, own_ref, ru_ref, left_ref, right_ref, lv_ref, ro_ref, lo_ref, m1, m2, m3, keep):
     turn(2, r_ref, l_ref, p_ref, ro_ref, lo_ref)
     half = ru_ref.shape[1]
     _, y = place()
     for hop, ref in ((1, m1), (2, m2), (3, m3), (0, keep)):
         i = lax.rem(y + hop, SIDE)
         own = own_ref[i].astype(F32)
-        u = own[:half] + ru_ref[i].astype(F32) + lu_ref[i].astype(F32)
-        v = own[half:] + rv_ref[i].astype(F32) + lv_ref[i].astype(F32)
+        u = own[:half] + ru_ref[i].astype(F32) + left_ref[1, i].astype(F32)
+        v = own[half:] + right_ref[1, i].astype(F32) + lv_ref[i].astype(F32)
         ref[:half] = u.astype(ref.dtype)
         ref[half:] = v.astype(ref.dtype)
 
@@ -479,15 +479,15 @@
 
     square4 = (SIDE, SIDE) + mine.shape[1:]
     piece = sds((SIDE, cols // 2, 128))
-    ru2, lv2, rv1, lu1, cu1, cv1, own = call(
+    two_pieces = sds((2,) + piece.shape)
+    right, left, cu1, cv1, own = call(
         chip_kernel,
         [VMEM] * 2 + [ANY],
         [mine.reshape(square4), got.reshape(square4), after],
-        [piece] * 6 + [sds((SIDE, cols, 128))],
+        [two_pieces] * 2 + [piece] * 2 + [sds((SIDE, cols, 128))],
         "chip",
     )
-    ru2, lv2 = along_x_ring(ru2, 1), along_x_ring(lv2, -1)
-    rv1, lu1 = along_x_ring(rv1, 1), along_x_ring(lu1, -1)
+    right, left = along_x_ring(right, 1), along_x_ring(left, -1)
     key_grad, parts = call(
         key_grad_kernel,
         [VMEM] * 6 + [ANY],
@@ -498,7 +498,7 @@
     r, l, ru1, lv1 = call(
         pair_kernel,
         [VMEM] * 7,
-        [r, l, parts, cu1, ru2, cv1, lv2],
+        [r, l, parts, cu1, right, cv1, left],
         [full] * 2 + [piece] * 2,
         "pair",
     )
@@ -507,7 +507,7 @@
     r, l, m1, m2, m3, keep = call(
         line_kernel,
         [VMEM] * 8,
-        [r, l, parts, own, ru1, lu1, rv1, lv1],
+        [r, l, parts, own, ru1, left, right, lv1],
         [full] * 2 + [sds((cols, 128))] * 3 + [sds((cols, 128), F32)],
         "line",
     )

time: 117 us -> 115 us (0.983)
  starting transfers between devices: 39.7 us -> 37.9 us
    ppermute x6 -> x4, waiting for transfers between devices: 9.55 us -> 4.91 us  [along_x_ring(): return lax.ppermute(a, 'ctx', [(i, (i + SIDE * k) % 16) for i in range(16)])]
    ppermute x8, waiting for transfers between devices: 9.5 us -> 14.1 us  [along_z(): return lax.ppermute(a, 'head', [(i, (i + k) % RING) for i in range(RING)])]
    ppermute x6 -> x4, starting transfers between devices: 8.12 us -> 6.54 us  [along_x_ring(): return lax.ppermute(a, 'ctx', [(i, (i + SIDE * k) % 16) for i in range(16)])]
  transfers between devices with their start and end apart: 31 -> 29, of which waited for: 21 -> 23; matrix products, arithmetic and copies ran while one was open for 0% -> 0% of each run, Pallas kernels for 14% -> 14%
where the time goes in v3:
time: 115 us
  waiting for transfers between devices  52.2 us (45%)
  starting transfers between devices  37.9 us (33%)
  Pallas kernels  23.6 us (21%)
    pallas_call x24, Pallas kernels, call(): pl.pallas_call(body, out_shape=tuple(outs), in_specs=specs, out_specs=tup...  23.6 us
    ppermute x8, waiting for transfers between devices, along(): return lax.ppermute(a, 'ctx', [(i, other(i)) for i in range(SIDE * SIDE)])  20.5 us
    ppermute x8, starting transfers between devices, along_z(): return lax.ppermute(a, 'head', [(i, (i + k) % RING) for i in range(RING)])  15.6 us
    ppermute x8, waiting for transfers between devices, along_z(): return lax.ppermute(a, 'head', [(i, (i + k) % RING) for i in range(RING)])  14.1 us
    ppermute x8, starting transfers between devices, along(): return lax.ppermute(a, 'ctx', [(i, other(i)) for i in range(SIDE * SIDE)])  12.8 us
    ppermute x3, waiting for transfers between devices, along_y_ring(): lax.ppermute(a, 'ctx', [(i, i // SIDE * SIDE + (i + k) % SIDE) for i in r...  6.68 us
    ppermute x4, starting transfers between devices, along_x_ring(): return lax.ppermute(a, 'ctx', [(i, (i + SIDE * k) % 16) for i in range(16)])  6.54 us
    ppermute x6, waiting for transfers between devices, swap(): return lax.ppermute(a, 'fsdp', [(0, 1), (1, 0)])  6.11 us
  transfers between devices with their start and end apart: 29, of which 23 were waited for; matrix products, arithmetic and copies ran while one was open for 0% of the time, Pallas kernels for 14%

profile of v3, /device:TPU:24, one launch (start us, length us, event | category | flops | bytes accessed | tf_op | source)
XLA Modules:
  0.0 114.6 jit_solution(7326224576774548810)
XLA Ops:
  0.7 2.9 %value_own.1 = (bf16[512,4096]{1,0:T(8,128)(2,1)S(1)}, f32[512,512]{1,0:T(8,128)S(1)}) custom-call(bf16[512,4096]{1,0:T(8,128)(2,1)} %x_hbm.1, bf16[2048,512]{1,0:T(8,128)(2,1)} %own_ref.1), custom_call_target="tpu_custom_call" | custom-call | flops 1000 | bytes 11534336 | tf_op jit(solution)/shard_map/value_own/pallas_call | solution.py:52
  14.4 3.5 %collective-permute-done.3.b_ref.refs_3_ = bf16[256,128]{1,0:T(8,128)(2,1)S(1)} collective-permute-done((bf16[256,128]{1,0:T(8,128)(2,1)S(1)}, bf16[256,128]{1,0:T(8,128)(2,1)S(1)}, u32[]{:S(2)}, u32[]{:S(2)}) %collective-permute-start.3) | collective-permute-done | bytes 65568 | tf_op jit(solution)/shard_map/ppermute | solution.py:225
  19.5 2.8 %collective-permute-done.4.b_ref.refs_4_ = bf16[256,128]{1,0:T(8,128)(2,1)S(1)} collective-permute-done((bf16[256,128]{1,0:T(8,128)(2,1)S(1)}, bf16[256,128]{1,0:T(8,128)(2,1)S(1)}, u32[]{:S(2)}, u32[]{:S(2)}) %collective-permute-start.4) | collective-permute-done | bytes 65568 | tf_op jit(solution)/shard_map/ppermute | solution.py:225
  22.3 2.8 %collective-permute-start.5 = (bf16[256,128]{1,0:T(8,128)(2,1)S(1)}, bf16[256,128]{1,0:T(8,128)(2,1)S(1)}, u32[]{:S(2)}, u32[]{:S(2)}) collective-permute-start(bf16[256,128]{1,0:T(8,128)(2,1)S(1)} %fold.11), channel_id=1, source_target_pairs={{0,192},{16,208},{32,224},{48,240},{64,128},{80,144},{96,160},{112... | collective-permute-start | bytes 196616 | tf_op jit(solution)/shard_map/ppermute | solution.py:225
  25.2 2.7 %collective-permute-done.5.refs_5_ = bf16[256,128]{1,0:T(8,128)(2,1)S(1)} collective-permute-done((bf16[256,128]{1,0:T(8,128)(2,1)S(1)}, bf16[256,128]{1,0:T(8,128)(2,1)S(1)}, u32[]{:S(2)}, u32[]{:S(2)}) %collective-permute-start.5) | collective-permute-done | bytes 65568 | tf_op jit(solution)/shard_map/ppermute | solution.py:225
  33.8 2.4 %collective-permute-done.8.b_ref.refs_2_ = bf16[256,128]{1,0:T(8,128)(2,1)S(1)} collective-permute-done((bf16[256,128]{1,0:T(8,128)(2,1)S(1)}, bf16[256,128]{1,0:T(8,128)(2,1)S(1)}, u32[]{:S(2)}, u32[]{:S(2)}) %collective-permute-start.8) | collective-permute-done | bytes 65568 | tf_op jit(solution)/shard_map/ppermute | solution.py:225
  38.3 3.1 %cross.1 = (bf16[512,512]{1,0:T(8,128)(2,1)}, f32[512,512]{1,0:T(8,128)S(1)}) custom-call(bf16[512,512]{1,0:T(8,128)(2,1)S(1)} %copy-done.2, bf16[512,512]{1,0:T(8,128)(2,1)S(1)} %copy-done.1, bf16[512,512]{1,0:T(8,128)(2,1)S(1)} %get-tuple-element.49.v_ref, bf16[512,512]{1,0:T(8,128)(2,1)S(1)} %get-tuple-element.54.low_ref, ...), custom_call_target="tpu_custom_call" | custom-call | flops 1000 | bytes 3801088 | tf_op jit(solution)/shard_map/cross/pallas_call | solution.py:52
  42.2 4.0 %collective-permute-done.10.b_ref.refs_4_ = bf16[256,128]{1,0:T(8,128)(2,1)S(1)} collective-permute-done((bf16[256,128]{1,0:T(8,128)(2,1)S(1)}, bf16[256,128]{1,0:T(8,128)(2,1)S(1)}, u32[]{:S(2)}, u32[]{:S(2)}) %collective-permute-start.10) | collective-permute-done | bytes 65568 | tf_op jit(solution)/shard_map/ppermute | solution.py:225
  46.2 3.0 %collective-permute-start.11 = (bf16[256,128]{1,0:T(8,128)(2,1)S(1)}, bf16[256,128]{1,0:T(8,128)(2,1)S(1)}, u32[]{:S(2)}, u32[]{:S(2)}) collective-permute-start(bf16[256,128]{1,0:T(8,128)(2,1)S(1)} %fold.15), channel_id=1, source_target_pairs={{0,192},{16,208},{32,224},{48,240},{64,128},{80,144},{96,160},{112... | collective-permute-start | bytes 196616 | tf_op jit(solution)/shard_map/ppermute | solution.py:225
  49.2 2.7 %collective-permute-done.11.refs_5_ = bf16[256,128]{1,0:T(8,128)(2,1)S(1)} collective-permute-done((bf16[256,128]{1,0:T(8,128)(2,1)S(1)}, bf16[256,128]{1,0:T(8,128)(2,1)S(1)}, u32[]{:S(2)}, u32[]{:S(2)}) %collective-permute-start.11) | collective-permute-done | bytes 65568 | tf_op jit(solution)/shard_map/ppermute | solution.py:225
  57.8 3.9 %collective-permute-start.15 = (bf16[256,512]{1,0:T(8,128)(2,1)S(1)}, bf16[256,512]{1,0:T(8,128)(2,1)S(1)}, u32[]{:S(2)}, u32[]{:S(2)}) collective-permute-start(bf16[256,512]{1,0:T(8,128)(2,1)S(1)} %get-tuple-element.67), channel_id=1, source_target_pairs={{0,14},{2,0},{4,2},{6,4},{8,6},{10,8},{12,10},{14,12},{1,15},{3,1}... | collective-permute-start | bytes 786440 | tf_op jit(solution)/shard_map/ppermute | solution.py:239
  61.8 2.4 %work.1 = (bf16[2,512,512]{2,1,0:T(8,128)(2,1)S(1)}, bf16[16,512,128]{2,1,0:T(8,128)(2,1)S(1)}) custom-call(bf16[512,512]{1,0:T(8,128)(2,1)S(1)} %get-tuple-element.63.refs_0_.vg_ref, bf16[2048,512]{1,0:T(8,128)(2,1)S(1)} %copy-done, bf16[2048,512]{1,0:T(8,128)(2,1)S(1)} %collective-permute-done.w_ref.refs_5_.refs_2_.other_ref, ...), custom_call_target="tpu_custom_call" | custom-call | flops 1000 | bytes 12058624 | tf_op jit(solution)/shard_map/work/pallas_call | solution.py:52
  64.2 4.4 %collective-permute-done.14.r_ref = bf16[256,512]{1,0:T(8,128)(2,1)S(1)} collective-permute-done((bf16[256,512]{1,0:T(8,128)(2,1)S(1)}, bf16[256,512]{1,0:T(8,128)(2,1)S(1)}, u32[]{:S(2)}, u32[]{:S(2)}) %collective-permute-start.14) | collective-permute-done | bytes 262176 | tf_op jit(solution)/shard_map/ppermute | solution.py:239
  68.7 3.0 %collective-permute-start.17 = (bf16[512,512]{1,0:T(8,128)(2,1)S(1)}, bf16[512,512]{1,0:T(8,128)(2,1)S(1)}, u32[]{:S(2)}, u32[]{:S(2)}) collective-permute-start(bf16[512,512]{1,0:T(8,128)(2,1)S(1)} %get-tuple-element.72), channel_id=1, source_target_pairs={{0,14},{2,0},{4,2},{6,4},{8,6},{10,8},{12,10},{14,12},{1,15},{3,1}... | collective-permute-start | bytes 1572872 | tf_op jit(solution)/shard_map/ppermute | solution.py:239
  72.3 3.2 %collective-permute-start.19 = (bf16[2,4,256,128]{3,2,1,0:T(8,128)(2,1)S(1)}, bf16[2,4,256,128]{3,2,1,0:T(8,128)(2,1)S(1)}, u32[]{:S(2)}, u32[]{:S(2)}) collective-permute-start(bf16[2,4,256,128]{3,2,1,0:T(8,128)(2,1)S(1)} %get-tuple-element.77), channel_id=1, source_target_pairs={{0,192},{16,208},{32,224},{48,240},{64,0},{80,16},{96,32},{112,48}... | collective-permute-start | bytes 1572872 | tf_op jit(solution)/shard_map/ppermute | solution.py:229
  75.5 3.8 %key_grad.1 = (bf16[512,512]{1,0:T(8,128)(2,1)}, bf16[5,512,512]{2,1,0:T(8,128)(2,1)S(1)}) custom-call(bf16[512,512]{1,0:T(8,128)(2,1)S(1)} %get-tuple-element.49.v_ref, f32[512,512]{1,0:T(8,128)S(1)} %get-tuple-element.57._.kp_ref, bf16[512,128]{1,0:T(8,128)(2,1)S(1)} %get-tuple-element.62.state_ref, bf16[512,512]{1,0:T(8,128)(2,1)S(1)} %get-tuple-element.63.refs_0_.vg_ref, ...), custom_call_target="tpu_custom_call" | custom-call | flops 1000 | bytes 10092544 | tf_op jit(solution)/shard_map/key_grad/pallas_call | solution.py:52
  79.3 3.3 %collective-permute-done.17.l_ref = bf16[512,512]{1,0:T(8,128)(2,1)S(1)} collective-permute-done((bf16[512,512]{1,0:T(8,128)(2,1)S(1)}, bf16[512,512]{1,0:T(8,128)(2,1)S(1)}, u32[]{:S(2)}, u32[]{:S(2)}) %collective-permute-start.17) | collective-permute-done | bytes 524320 | tf_op jit(solution)/shard_map/ppermute | solution.py:239
  82.6 3.4 %collective-permute-done.16.r_ref = bf16[512,512]{1,0:T(8,128)(2,1)S(1)} collective-permute-done((bf16[512,512]{1,0:T(8,128)(2,1)S(1)}, bf16[512,512]{1,0:T(8,128)(2,1)S(1)}, u32[]{:S(2)}, u32[]{:S(2)}) %collective-permute-start.16) | collective-permute-done | bytes 524320 | tf_op jit(solution)/shard_map/ppermute | solution.py:239
  87.0 3.2 %collective-permute-start.21 = (bf16[512,512]{1,0:T(8,128)(2,1)S(1)}, bf16[512,512]{1,0:T(8,128)(2,1)S(1)}, u32[]{:S(2)}, u32[]{:S(2)}) collective-permute-start(bf16[512,512]{1,0:T(8,128)(2,1)S(1)} %get-tuple-element.79), channel_id=1, source_target_pairs={{0,14},{2,0},{4,2},{6,4},{8,6},{10,8},{12,10},{14,12},{1,15},{3,1}... | collective-permute-start | bytes 1572872 | tf_op jit(solution)/shard_map/ppermute | solution.py:239
  91.2 2.3 %collective-permute-start.23 = (bf16[4,256,128]{2,1,0:T(8,128)(2,1)S(1)}, bf16[4,256,128]{2,1,0:T(8,128)(2,1)S(1)}, u32[]{:S(2)}, u32[]{:S(2)}) collective-permute-start(bf16[4,256,128]{2,1,0:T(8,128)(2,1)S(1)} %get-tuple-element.81), channel_id=1, source_target_pairs={{0,192},{16,208},{32,224},{48,240},{64,0},{80,16},{96,32},{112,48}... | collective-permute-start | bytes 786440 | tf_op jit(solution)/shard_map/ppermute | solution.py:229
  93.5 4.3 %collective-permute-done.22.ru_ref = bf16[4,256,128]{2,1,0:T(8,128)(2,1)S(1)} collective-permute-done((bf16[4,256,128]{2,1,0:T(8,128)(2,1)S(1)}, bf16[4,256,128]{2,1,0:T(8,128)(2,1)S(1)}, u32[]{:S(2)}, u32[]{:S(2)}) %collective-permute-start.22) | collective-permute-done | bytes 262176 | tf_op jit(solution)/shard_map/ppermute | solution.py:229
  97.9 2.5 %collective-permute-done.20.r_ref = bf16[512,512]{1,0:T(8,128)(2,1)S(1)} collective-permute-done((bf16[512,512]{1,0:T(8,128)(2,1)S(1)}, bf16[512,512]{1,0:T(8,128)(2,1)S(1)}, u32[]{:S(2)}, u32[]{:S(2)}) %collective-permute-start.20) | collective-permute-done | bytes 524320 | tf_op jit(solution)/shard_map/ppermute | solution.py:239
  106.2 2.9 %collective-permute-done.24.a_ref = bf16[512,128]{1,0:T(8,128)(2,1)S(1)} collective-permute-done((bf16[512,128]{1,0:T(8,128)(2,1)S(1)}, bf16[512,128]{1,0:T(8,128)(2,1)S(1)}, u32[]{:S(2)}, u32[]{:S(2)}) %collective-permute-start.24) | collective-permute-done | bytes 131104 | tf_op jit(solution)/shard_map/ppermute | solution.py:233
  109.1 2.4 %collective-permute-done.25.b_ref = bf16[512,128]{1,0:T(8,128)(2,1)S(1)} collective-permute-done((bf16[512,128]{1,0:T(8,128)(2,1)S(1)}, bf16[512,128]{1,0:T(8,128)(2,1)S(1)}, u32[]{:S(2)}, u32[]{:S(2)}) %collective-permute-start.25) | collective-permute-done | bytes 131104 | tf_op jit(solution)/shard_map/ppermute | solution.py:233
  (66 shorter events, 38.5 us)
Async XLA Ops:
  0.6 4.5 %collective-permute-start = (bf16[2048,512]{1,0:T(8,128)(2,1)}, bf16[2048,512]{1,0:T(8,128)(2,1)S(1)}, u32[]{:S(2)}, u32[]{:S(2)}) collective-permute-start(bf16[2048,512]{1,0:T(8,128)(2,1)} %own_ref.1), channel_id=1, source_target_pairs={{0,1},{1,0},{2,3},{3,2},{4,5},{5,4},{6,7},{7,6},{8,9},{9,8},{10,11... | collective-permute-start | bytes 6291464 | tf_op jit(solution)/shard_map/ppermute | solution.py:243
  12.4 5.6 %collective-permute-start.3 = (bf16[256,128]{1,0:T(8,128)(2,1)S(1)}, bf16[256,128]{1,0:T(8,128)(2,1)S(1)}, u32[]{:S(2)}, u32[]{:S(2)}) collective-permute-start(bf16[256,128]{1,0:T(8,128)(2,1)S(1)} %fold.9.a_ref), channel_id=1, source_target_pairs={{0,48},{16,32},{32,16},{48,0},{64,112},{80,96},{96,80},{112,64},{1... | collective-permute-start | bytes 196616 | tf_op jit(solution)/shard_map/ppermute | solution.py:225
  18.0 4.4 %collective-permute-start.4 = (bf16[256,128]{1,0:T(8,128)(2,1)S(1)}, bf16[256,128]{1,0:T(8,128)(2,1)S(1)}, u32[]{:S(2)}, u32[]{:S(2)}) collective-permute-start(bf16[256,128]{1,0:T(8,128)(2,1)S(1)} %fold.10.a_ref), channel_id=1, source_target_pairs={{0,64},{16,80},{32,96},{48,112},{64,0},{80,16},{96,32},{112,48},{1... | collective-permute-start | bytes 196616 | tf_op jit(solution)/shard_map/ppermute | solution.py:225
  22.3 5.6 %collective-permute-start.5 = (bf16[256,128]{1,0:T(8,128)(2,1)S(1)}, bf16[256,128]{1,0:T(8,128)(2,1)S(1)}, u32[]{:S(2)}, u32[]{:S(2)}) collective-permute-start(bf16[256,128]{1,0:T(8,128)(2,1)S(1)} %fold.11), channel_id=1, source_target_pairs={{0,192},{16,208},{32,224},{48,240},{64,128},{80,144},{96,160},{112... | collective-permute-start | bytes 196616 | tf_op jit(solution)/shard_map/ppermute | solution.py:225
  31.9 4.4 %collective-permute-start.8 = (bf16[256,128]{1,0:T(8,128)(2,1)S(1)}, bf16[256,128]{1,0:T(8,128)(2,1)S(1)}, u32[]{:S(2)}, u32[]{:S(2)}) collective-permute-start(bf16[256,128]{1,0:T(8,128)(2,1)S(1)} %fold.12.a_ref), channel_id=1, source_target_pairs={{0,16},{16,0},{32,48},{48,32},{64,80},{80,64},{96,112},{112,96},{1... | collective-permute-start | bytes 196616 | tf_op jit(solution)/shard_map/ppermute | solution.py:225
  36.2 5.6 %collective-permute-start.9 = (bf16[256,128]{1,0:T(8,128)(2,1)S(1)}, bf16[256,128]{1,0:T(8,128)(2,1)S(1)}, u32[]{:S(2)}, u32[]{:S(2)}) collective-permute-start(bf16[256,128]{1,0:T(8,128)(2,1)S(1)} %fold.13.a_ref), channel_id=1, source_target_pairs={{0,48},{16,32},{32,16},{48,0},{64,112},{80,96},{96,80},{112,64},{1... | collective-permute-start | bytes 196616 | tf_op jit(solution)/shard_map/ppermute | solution.py:225
  41.8 4.4 %collective-permute-start.10 = (bf16[256,128]{1,0:T(8,128)(2,1)S(1)}, bf16[256,128]{1,0:T(8,128)(2,1)S(1)}, u32[]{:S(2)}, u32[]{:S(2)}) collective-permute-start(bf16[256,128]{1,0:T(8,128)(2,1)S(1)} %fold.14.a_ref), channel_id=1, source_target_pairs={{0,64},{16,80},{32,96},{48,112},{64,0},{80,16},{96,32},{112,48},{1... | collective-permute-start | bytes 196616 | tf_op jit(solution)/shard_map/ppermute | solution.py:225
  46.2 5.7 %collective-permute-start.11 = (bf16[256,128]{1,0:T(8,128)(2,1)S(1)}, bf16[256,128]{1,0:T(8,128)(2,1)S(1)}, u32[]{:S(2)}, u32[]{:S(2)}) collective-permute-start(bf16[256,128]{1,0:T(8,128)(2,1)S(1)} %fold.15), channel_id=1, source_target_pairs={{0,192},{16,208},{32,224},{48,240},{64,128},{80,144},{96,160},{112... | collective-permute-start | bytes 196616 | tf_op jit(solution)/shard_map/ppermute | solution.py:225
  55.7 16.1 %collective-permute-start.13 = (bf16[16,512,128]{2,1,0:T(8,128)(2,1)S(1)}, bf16[16,512,128]{2,1,0:T(8,128)(2,1)S(1)}, u32[]{:S(2)}, u32[]{:S(2)}) collective-permute-start(bf16[16,512,128]{2,1,0:T(8,128)(2,1)S(1)} %get-tuple-element.65), channel_id=1, source_target_pairs={{0,1},{1,0},{2,3},{3,2},{4,5},{5,4},{6,7},{7,6},{8,9},{9,8},{10,11... | collective-permute-start | bytes 6291464 | tf_op jit(solution)/shard_map/ppermute | solution.py:243
  55.9 12.7 %collective-permute-start.14 = (bf16[256,512]{1,0:T(8,128)(2,1)S(1)}, bf16[256,512]{1,0:T(8,128)(2,1)S(1)}, u32[]{:S(2)}, u32[]{:S(2)}) collective-permute-start(bf16[256,512]{1,0:T(8,128)(2,1)S(1)} %get-tuple-element.66), channel_id=1, source_target_pairs={{0,2},{2,4},{4,6},{6,8},{8,10},{10,12},{12,14},{14,0},{1,3},{3,5},... | collective-permute-start | bytes 786440 | tf_op jit(solution)/shard_map/ppermute | solution.py:239
  57.8 10.7 %collective-permute-start.15 = (bf16[256,512]{1,0:T(8,128)(2,1)S(1)}, bf16[256,512]{1,0:T(8,128)(2,1)S(1)}, u32[]{:S(2)}, u32[]{:S(2)}) collective-permute-start(bf16[256,512]{1,0:T(8,128)(2,1)S(1)} %get-tuple-element.67), channel_id=1, source_target_pairs={{0,14},{2,0},{4,2},{6,4},{8,6},{10,8},{12,10},{14,12},{1,15},{3,1}... | collective-permute-start | bytes 786440 | tf_op jit(solution)/shard_map/ppermute | solution.py:239
  68.7 13.9 %collective-permute-start.17 = (bf16[512,512]{1,0:T(8,128)(2,1)S(1)}, bf16[512,512]{1,0:T(8,128)(2,1)S(1)}, u32[]{:S(2)}, u32[]{:S(2)}) collective-permute-start(bf16[512,512]{1,0:T(8,128)(2,1)S(1)} %get-tuple-element.72), channel_id=1, source_target_pairs={{0,14},{2,0},{4,2},{6,4},{8,6},{10,8},{12,10},{14,12},{1,15},{3,1}... | collective-permute-start | bytes 1572872 | tf_op jit(solution)/shard_map/ppermute | solution.py:239
  71.7 14.3 %collective-permute-start.16 = (bf16[512,512]{1,0:T(8,128)(2,1)S(1)}, bf16[512,512]{1,0:T(8,128)(2,1)S(1)}, u32[]{:S(2)}, u32[]{:S(2)}) collective-permute-start(bf16[512,512]{1,0:T(8,128)(2,1)S(1)} %get-tuple-element.69._), channel_id=1, source_target_pairs={{0,2},{2,4},{4,6},{6,8},{8,10},{10,12},{12,14},{14,0},{1,3},{3,5},... | collective-permute-start | bytes 1572872 | tf_op jit(solution)/shard_map/ppermute | solution.py:239
  72.2 14.4 %collective-permute-start.18 = (bf16[2,4,256,128]{3,2,1,0:T(8,128)(2,1)S(1)}, bf16[2,4,256,128]{3,2,1,0:T(8,128)(2,1)S(1)}, u32[]{:S(2)}, u32[]{:S(2)}) collective-permute-start(bf16[2,4,256,128]{3,2,1,0:T(8,128)(2,1)S(1)} %get-tuple-element.75), channel_id=1, source_target_pairs={{0,64},{16,80},{32,96},{48,112},{64,128},{80,144},{96,160},{112,17... | collective-permute-start | bytes 1572872 | tf_op jit(solution)/shard_map/ppermute | solution.py:229
  72.3 14.3 %collective-permute-start.19 = (bf16[2,4,256,128]{3,2,1,0:T(8,128)(2,1)S(1)}, bf16[2,4,256,128]{3,2,1,0:T(8,128)(2,1)S(1)}, u32[]{:S(2)}, u32[]{:S(2)}) collective-permute-start(bf16[2,4,256,128]{3,2,1,0:T(8,128)(2,1)S(1)} %get-tuple-element.77), channel_id=1, source_target_pairs={{0,192},{16,208},{32,224},{48,240},{64,0},{80,16},{96,32},{112,48}... | collective-permute-start | bytes 1572872 | tf_op jit(solution)/shard_map/ppermute | solution.py:229
  87.0 13.4 %collective-permute-start.20 = (bf16[512,512]{1,0:T(8,128)(2,1)S(1)}, bf16[512,512]{1,0:T(8,128)(2,1)S(1)}, u32[]{:S(2)}, u32[]{:S(2)}) collective-permute-start(bf16[512,512]{1,0:T(8,128)(2,1)S(1)} %get-tuple-element.78), channel_id=1, source_target_pairs={{0,2},{2,4},{4,6},{6,8},{8,10},{10,12},{12,14},{14,0},{1,3},{3,5},... | collective-permute-start | bytes 1572872 | tf_op jit(solution)/shard_map/ppermute | solution.py:239
  87.0 13.4 %collective-permute-start.21 = (bf16[512,512]{1,0:T(8,128)(2,1)S(1)}, bf16[512,512]{1,0:T(8,128)(2,1)S(1)}, u32[]{:S(2)}, u32[]{:S(2)}) collective-permute-start(bf16[512,512]{1,0:T(8,128)(2,1)S(1)} %get-tuple-element.79), channel_id=1, source_target_pairs={{0,14},{2,0},{4,2},{6,4},{8,6},{10,8},{12,10},{14,12},{1,15},{3,1}... | collective-permute-start | bytes 1572872 | tf_op jit(solution)/shard_map/ppermute | solution.py:239
  90.3 7.6 %collective-permute-start.22 = (bf16[4,256,128]{2,1,0:T(8,128)(2,1)S(1)}, bf16[4,256,128]{2,1,0:T(8,128)(2,1)S(1)}, u32[]{:S(2)}, u32[]{:S(2)}) collective-permute-start(bf16[4,256,128]{2,1,0:T(8,128)(2,1)S(1)} %get-tuple-element.80), channel_id=1, source_target_pairs={{0,64},{16,80},{32,96},{48,112},{64,128},{80,144},{96,160},{112,17... | collective-permute-start | bytes 786440 | tf_op jit(solution)/shard_map/ppermute | solution.py:229
  91.2 6.6 %collective-permute-start.23 = (bf16[4,256,128]{2,1,0:T(8,128)(2,1)S(1)}, bf16[4,256,128]{2,1,0:T(8,128)(2,1)S(1)}, u32[]{:S(2)}, u32[]{:S(2)}) collective-permute-start(bf16[4,256,128]{2,1,0:T(8,128)(2,1)S(1)} %get-tuple-element.81), channel_id=1, source_target_pairs={{0,192},{16,208},{32,224},{48,240},{64,0},{80,16},{96,32},{112,48}... | collective-permute-start | bytes 786440 | tf_op jit(solution)/shard_map/ppermute | solution.py:229
  100.8 12.5 %collective-permute-start.27 = (bf16[512,512]{1,0:T(8,128)(2,1)S(1)}, bf16[512,512]{1,0:T(8,128)(2,1)S(1)}, u32[]{:S(2)}, u32[]{:S(2)}) collective-permute-start(bf16[512,512]{1,0:T(8,128)(2,1)S(1)} %get-tuple-element.86), channel_id=1, source_target_pairs={{0,2},{2,4},{4,6},{6,8},{8,10},{10,12},{12,14},{14,0},{1,3},{3,5},... | collective-permute-start | bytes 1572872 | tf_op jit(solution)/shard_map/ppermute | solution.py:239
  102.5 10.9 %collective-permute-start.28 = (bf16[512,512]{1,0:T(8,128)(2,1)S(1)}, bf16[512,512]{1,0:T(8,128)(2,1)S(1)}, u32[]{:S(2)}, u32[]{:S(2)}) collective-permute-start(bf16[512,512]{1,0:T(8,128)(2,1)S(1)} %get-tuple-element.87), channel_id=1, source_target_pairs={{0,14},{2,0},{4,2},{6,4},{8,6},{10,8},{12,10},{14,12},{1,15},{3,1}... | collective-permute-start | bytes 1572872 | tf_op jit(solution)/shard_map/ppermute | solution.py:239
  104.2 5.0 %collective-permute-start.24 = (bf16[512,128]{1,0:T(8,128)(2,1)S(1)}, bf16[512,128]{1,0:T(8,128)(2,1)S(1)}, u32[]{:S(2)}, u32[]{:S(2)}) collective-permute-start(bf16[512,128]{1,0:T(8,128)(2,1)S(1)} %get-tuple-element.83), channel_id=1, source_target_pairs={{0,16},{16,32},{32,48},{48,0},{64,80},{80,96},{96,112},{112,64},{1... | collective-permute-start | bytes 393224 | tf_op jit(solution)/shard_map/ppermute | solution.py:233
  105.0 6.6 %collective-permute-start.25 = (bf16[512,128]{1,0:T(8,128)(2,1)S(1)}, bf16[512,128]{1,0:T(8,128)(2,1)S(1)}, u32[]{:S(2)}, u32[]{:S(2)}) collective-permute-start(bf16[512,128]{1,0:T(8,128)(2,1)S(1)} %get-tuple-element.84), channel_id=1, source_target_pairs={{0,32},{16,48},{32,0},{48,16},{64,96},{80,112},{96,64},{112,80},{1... | collective-permute-start | bytes 393224 | tf_op jit(solution)/shard_map/ppermute | solution.py:233
  105.2 7.7 %collective-permute-start.26 = (bf16[512,128]{1,0:T(8,128)(2,1)S(1)}, bf16[512,128]{1,0:T(8,128)(2,1)S(1)}, u32[]{:S(2)}, u32[]{:S(2)}) collective-permute-start(bf16[512,128]{1,0:T(8,128)(2,1)S(1)} %get-tuple-element.85), channel_id=1, source_target_pairs={{0,48},{16,0},{32,16},{48,32},{64,112},{80,64},{96,80},{112,96},{1... | collective-permute-start | bytes 393224 | tf_op jit(solution)/shard_map/ppermute | solution.py:233
  (9 other events, 51.9 us)

commit v4 on v3

--- a/solution.py
+++ b/solution.py
@@ -312,7 +312,7 @@
     weight_pieces(scale, core(), vg_ref, x_ref, piece_ref)
 
 
-def open_turn_kernel(r_ref, l_ref, p_ref, ro_ref, lo_ref):
+def open_turn_kernel(r_ref, l_ref, p_ref, _, ro_ref, lo_ref):
     half = r_ref.shape[0]
     ro_ref[:half] = (wide(r_ref) + p_ref[0, :half].astype(F32)).astype(BF16)
     ro_ref[half:] = p_ref[0, half:]
@@ -349,7 +349,7 @@
             o_ref[first + p] = res[:, p * 128 : p * 128 + 128]
 
 
-def chip_kernel(a_ref, b_ref, _, right, left, cu1, cv1, own):
+def chip_kernel(a_ref, b_ref, right, left, cu1, cv1, own):
     half = own.shape[1] // 2
 
     x, _ = place()
@@ -473,25 +473,24 @@
         [sds((2, tok, 512)), pieces],
         "work",
     )
-    r, l = call(open_turn_kernel, [VMEM] * 3, [r, l, threes], [full] * 2, "turn")
-    after = r
-    r, l = along_z(r, 1), along_z(l, -1)
-
     square4 = (SIDE, SIDE) + mine.shape[1:]
     piece = sds((SIDE, cols // 2, 128))
     two_pieces = sds((2,) + piece.shape)
     right, left, cu1, cv1, own = call(
         chip_kernel,
-        [VMEM] * 2 + [ANY],
-        [mine.reshape(square4), got.reshape(square4), after],
+        [VMEM] * 2,
+        [mine.reshape(square4), got.reshape(square4)],
         [two_pieces] * 2 + [piece] * 2 + [sds((SIDE, cols, 128))],
         "chip",
     )
     right, left = along_x_ring(right, 1), along_x_ring(left, -1)
+    r, l = call(open_turn_kernel, [VMEM] * 3 + [ANY], [r, l, threes, own], [full] * 2, "turn")
+    after = r
+    r, l = along_z(r, 1), along_z(l, -1)
     key_grad, parts = call(
         key_grad_kernel,
         [VMEM] * 6 + [ANY],
-        [value, key_part, state_grad, value_grad, value_weight, w_other, own],
+        [value, key_part, state_grad, value_grad, value_weight, w_other, after],
         [square, sds((5, tok, 512))],
         "key_grad",
     )

time: 115 us -> 115 us (level)
    ppermute x8, waiting for transfers between devices: 14.1 us -> 9.71 us  [along_z(): return lax.ppermute(a, 'head', [(i, (i + k) % RING) for i in range(RING)])]
    ppermute x4, waiting for transfers between devices: 4.91 us -> 8.7 us  [along_x_ring(): return lax.ppermute(a, 'ctx', [(i, (i + SIDE * k) % 16) for i in range(16)])]
where the time goes in v4:
time: 115 us; the launch traced here: 114 us
  waiting for transfers between devices  51.6 us (45%)
  starting transfers between devices  37.9 us (33%)
  Pallas kernels  23.6 us (21%)
    pallas_call x24, Pallas kernels, call(): pl.pallas_call(body, out_shape=tuple(outs), in_specs=specs, out_specs=tup...  23.6 us
    ppermute x8, waiting for transfers between devices, along(): return lax.ppermute(a, 'ctx', [(i, other(i)) for i in range(SIDE * SIDE)])  20.5 us
    ppermute x8, starting transfers between devices, along_z(): return lax.ppermute(a, 'head', [(i, (i + k) % RING) for i in range(RING)])  15.5 us
    ppermute x8, starting transfers between devices, along(): return lax.ppermute(a, 'ctx', [(i, other(i)) for i in range(SIDE * SIDE)])  12.8 us
    ppermute x8, waiting for transfers between devices, along_z(): return lax.ppermute(a, 'head', [(i, (i + k) % RING) for i in range(RING)])  9.71 us
    ppermute x4, waiting for transfers between devices, along_x_ring(): return lax.ppermute(a, 'ctx', [(i, (i + SIDE * k) % 16) for i in range(16)])  8.7 us
    ppermute x3, waiting for transfers between devices, along_y_ring(): lax.ppermute(a, 'ctx', [(i, i // SIDE * SIDE + (i + k) % SIDE) for i in r...  6.68 us
    ppermute x4, starting transfers between devices, along_x_ring(): return lax.ppermute(a, 'ctx', [(i, (i + SIDE * k) % 16) for i in range(16)])  6.54 us
  transfers between devices with their start and end apart: 29, of which 23 were waited for; matrix products, arithmetic and copies ran while one was open for 0% of the time, Pallas kernels for 14%

profile of v4, /device:TPU:24, one launch (start us, length us, event | category | flops | bytes accessed | tf_op | source)
XLA Modules:
  0.0 114.0 jit_solution(17433480248793926085)
XLA Ops:
  0.7 2.9 %value_own.1 = (bf16[512,4096]{1,0:T(8,128)(2,1)S(1)}, f32[512,512]{1,0:T(8,128)S(1)}) custom-call(bf16[512,4096]{1,0:T(8,128)(2,1)} %x_hbm.1, bf16[2048,512]{1,0:T(8,128)(2,1)} %own_ref.1), custom_call_target="tpu_custom_call" | custom-call | flops 1000 | bytes 11534336 | tf_op jit(solution)/shard_map/value_own/pallas_call | solution.py:52
  14.4 3.5 %collective-permute-done.3.b_ref.refs_3_ = bf16[256,128]{1,0:T(8,128)(2,1)S(1)} collective-permute-done((bf16[256,128]{1,0:T(8,128)(2,1)S(1)}, bf16[256,128]{1,0:T(8,128)(2,1)S(1)}, u32[]{:S(2)}, u32[]{:S(2)}) %collective-permute-start.3) | collective-permute-done | bytes 65568 | tf_op jit(solution)/shard_map/ppermute | solution.py:225
  19.5 2.8 %collective-permute-done.4.b_ref.refs_4_ = bf16[256,128]{1,0:T(8,128)(2,1)S(1)} collective-permute-done((bf16[256,128]{1,0:T(8,128)(2,1)S(1)}, bf16[256,128]{1,0:T(8,128)(2,1)S(1)}, u32[]{:S(2)}, u32[]{:S(2)}) %collective-permute-start.4) | collective-permute-done | bytes 65568 | tf_op jit(solution)/shard_map/ppermute | solution.py:225
  22.3 2.8 %collective-permute-start.5 = (bf16[256,128]{1,0:T(8,128)(2,1)S(1)}, bf16[256,128]{1,0:T(8,128)(2,1)S(1)}, u32[]{:S(2)}, u32[]{:S(2)}) collective-permute-start(bf16[256,128]{1,0:T(8,128)(2,1)S(1)} %fold.11), channel_id=1, source_target_pairs={{0,192},{16,208},{32,224},{48,240},{64,128},{80,144},{96,160},{112... | collective-permute-start | bytes 196616 | tf_op jit(solution)/shard_map/ppermute | solution.py:225
  25.2 2.7 %collective-permute-done.5.refs_5_ = bf16[256,128]{1,0:T(8,128)(2,1)S(1)} collective-permute-done((bf16[256,128]{1,0:T(8,128)(2,1)S(1)}, bf16[256,128]{1,0:T(8,128)(2,1)S(1)}, u32[]{:S(2)}, u32[]{:S(2)}) %collective-permute-start.5) | collective-permute-done | bytes 65568 | tf_op jit(solution)/shard_map/ppermute | solution.py:225
  38.3 3.1 %cross.1 = (bf16[512,512]{1,0:T(8,128)(2,1)}, f32[512,512]{1,0:T(8,128)S(1)}) custom-call(bf16[512,512]{1,0:T(8,128)(2,1)S(1)} %copy-done.2, bf16[512,512]{1,0:T(8,128)(2,1)S(1)} %copy-done.1, bf16[512,512]{1,0:T(8,128)(2,1)S(1)} %get-tuple-element.49.v_ref, bf16[512,512]{1,0:T(8,128)(2,1)S(1)} %get-tuple-element.54.low_ref, ...), custom_call_target="tpu_custom_call" | custom-call | flops 1000 | bytes 3801088 | tf_op jit(solution)/shard_map/cross/pallas_call | solution.py:52
  42.2 4.0 %collective-permute-done.10.b_ref.refs_4_ = bf16[256,128]{1,0:T(8,128)(2,1)S(1)} collective-permute-done((bf16[256,128]{1,0:T(8,128)(2,1)S(1)}, bf16[256,128]{1,0:T(8,128)(2,1)S(1)}, u32[]{:S(2)}, u32[]{:S(2)}) %collective-permute-start.10) | collective-permute-done | bytes 65568 | tf_op jit(solution)/shard_map/ppermute | solution.py:225
  46.2 3.0 %collective-permute-start.11 = (bf16[256,128]{1,0:T(8,128)(2,1)S(1)}, bf16[256,128]{1,0:T(8,128)(2,1)S(1)}, u32[]{:S(2)}, u32[]{:S(2)}) collective-permute-start(bf16[256,128]{1,0:T(8,128)(2,1)S(1)} %fold.15), channel_id=1, source_target_pairs={{0,192},{16,208},{32,224},{48,240},{64,128},{80,144},{96,160},{112... | collective-permute-start | bytes 196616 | tf_op jit(solution)/shard_map/ppermute | solution.py:225
  49.2 2.7 %collective-permute-done.11.refs_5_ = bf16[256,128]{1,0:T(8,128)(2,1)S(1)} collective-permute-done((bf16[256,128]{1,0:T(8,128)(2,1)S(1)}, bf16[256,128]{1,0:T(8,128)(2,1)S(1)}, u32[]{:S(2)}, u32[]{:S(2)}) %collective-permute-start.11) | collective-permute-done | bytes 65568 | tf_op jit(solution)/shard_map/ppermute | solution.py:225
  57.8 3.9 %collective-permute-start.14 = (bf16[256,512]{1,0:T(8,128)(2,1)S(1)}, bf16[256,512]{1,0:T(8,128)(2,1)S(1)}, u32[]{:S(2)}, u32[]{:S(2)}) collective-permute-start(bf16[256,512]{1,0:T(8,128)(2,1)S(1)} %get-tuple-element.65), channel_id=1, source_target_pairs={{0,14},{2,0},{4,2},{6,4},{8,6},{10,8},{12,10},{14,12},{1,15},{3,1}... | collective-permute-start | bytes 786440 | tf_op jit(solution)/shard_map/ppermute | solution.py:239
  61.8 2.4 %work.1 = (bf16[2,512,512]{2,1,0:T(8,128)(2,1)S(1)}, bf16[16,512,128]{2,1,0:T(8,128)(2,1)S(1)}) custom-call(bf16[512,512]{1,0:T(8,128)(2,1)S(1)} %get-tuple-element.63.refs_0_.vg_ref, bf16[2048,512]{1,0:T(8,128)(2,1)S(1)} %copy-done, bf16[2048,512]{1,0:T(8,128)(2,1)S(1)} %collective-permute-done.w_ref.refs_5_.refs_2_.other_ref, ...), custom_call_target="tpu_custom_call" | custom-call | flops 1000 | bytes 12058624 | tf_op jit(solution)/shard_map/work/pallas_call | solution.py:52
  64.8 3.2 %collective-permute-start.19 = (bf16[2,4,256,128]{3,2,1,0:T(8,128)(2,1)S(1)}, bf16[2,4,256,128]{3,2,1,0:T(8,128)(2,1)S(1)}, u32[]{:S(2)}, u32[]{:S(2)}) collective-permute-start(bf16[2,4,256,128]{3,2,1,0:T(8,128)(2,1)S(1)} %get-tuple-element.77), channel_id=1, source_target_pairs={{0,192},{16,208},{32,224},{48,240},{64,0},{80,16},{96,32},{112,48}... | collective-permute-start | bytes 1572872 | tf_op jit(solution)/shard_map/ppermute | solution.py:229
  68.7 3.0 %collective-permute-start.17 = (bf16[512,512]{1,0:T(8,128)(2,1)S(1)}, bf16[512,512]{1,0:T(8,128)(2,1)S(1)}, u32[]{:S(2)}, u32[]{:S(2)}) collective-permute-start(bf16[512,512]{1,0:T(8,128)(2,1)S(1)} %get-tuple-element.72), channel_id=1, source_target_pairs={{0,14},{2,0},{4,2},{6,4},{8,6},{10,8},{12,10},{14,12},{1,15},{3,1}... | collective-permute-start | bytes 1572872 | tf_op jit(solution)/shard_map/ppermute | solution.py:239
  71.7 3.8 %key_grad.1 = (bf16[512,512]{1,0:T(8,128)(2,1)}, bf16[5,512,512]{2,1,0:T(8,128)(2,1)S(1)}) custom-call(bf16[512,512]{1,0:T(8,128)(2,1)S(1)} %get-tuple-element.49.v_ref, f32[512,512]{1,0:T(8,128)S(1)} %get-tuple-element.57._.kp_ref, bf16[512,128]{1,0:T(8,128)(2,1)S(1)} %get-tuple-element.62.state_ref, bf16[512,512]{1,0:T(8,128)(2,1)S(1)} %get-tuple-element.63.refs_0_.vg_ref, ...), custom_call_target="tpu_custom_call" | custom-call | flops 1000 | bytes 10092544 | tf_op jit(solution)/shard_map/key_grad/pallas_call | solution.py:52
  75.5 4.3 %collective-permute-done.18.b_ref.right_ref = bf16[2,4,256,128]{3,2,1,0:T(8,128)(2,1)S(1)} collective-permute-done((bf16[2,4,256,128]{3,2,1,0:T(8,128)(2,1)S(1)}, bf16[2,4,256,128]{3,2,1,0:T(8,128)(2,1)S(1)}, u32[]{:S(2)}, u32[]{:S(2)}) %collective-permute-start.18) | collective-permute-done | bytes 524320 | tf_op jit(solution)/shard_map/ppermute | solution.py:229
  79.9 2.7 %collective-permute-done.17.l_ref = bf16[512,512]{1,0:T(8,128)(2,1)S(1)} collective-permute-done((bf16[512,512]{1,0:T(8,128)(2,1)S(1)}, bf16[512,512]{1,0:T(8,128)(2,1)S(1)}, u32[]{:S(2)}, u32[]{:S(2)}) %collective-permute-start.17) | collective-permute-done | bytes 524320 | tf_op jit(solution)/shard_map/ppermute | solution.py:239
  82.6 3.4 %collective-permute-done.16.r_ref = bf16[512,512]{1,0:T(8,128)(2,1)S(1)} collective-permute-done((bf16[512,512]{1,0:T(8,128)(2,1)S(1)}, bf16[512,512]{1,0:T(8,128)(2,1)S(1)}, u32[]{:S(2)}, u32[]{:S(2)}) %collective-permute-start.16) | collective-permute-done | bytes 524320 | tf_op jit(solution)/shard_map/ppermute | solution.py:239
  86.5 3.2 %collective-permute-start.21 = (bf16[512,512]{1,0:T(8,128)(2,1)S(1)}, bf16[512,512]{1,0:T(8,128)(2,1)S(1)}, u32[]{:S(2)}, u32[]{:S(2)}) collective-permute-start(bf16[512,512]{1,0:T(8,128)(2,1)S(1)} %get-tuple-element.79), channel_id=1, source_target_pairs={{0,14},{2,0},{4,2},{6,4},{8,6},{10,8},{12,10},{14,12},{1,15},{3,1}... | collective-permute-start | bytes 1572872 | tf_op jit(solution)/shard_map/ppermute | solution.py:239
  89.7 3.2 %collective-permute-start.23 = (bf16[4,256,128]{2,1,0:T(8,128)(2,1)S(1)}, bf16[4,256,128]{2,1,0:T(8,128)(2,1)S(1)}, u32[]{:S(2)}, u32[]{:S(2)}) collective-permute-start(bf16[4,256,128]{2,1,0:T(8,128)(2,1)S(1)} %get-tuple-element.81), channel_id=1, source_target_pairs={{0,192},{16,208},{32,224},{48,240},{64,0},{80,16},{96,32},{112,48}... | collective-permute-start | bytes 786440 | tf_op jit(solution)/shard_map/ppermute | solution.py:229
  92.9 4.3 %collective-permute-done.22.ru_ref = bf16[4,256,128]{2,1,0:T(8,128)(2,1)S(1)} collective-permute-done((bf16[4,256,128]{2,1,0:T(8,128)(2,1)S(1)}, bf16[4,256,128]{2,1,0:T(8,128)(2,1)S(1)}, u32[]{:S(2)}, u32[]{:S(2)}) %collective-permute-start.22) | collective-permute-done | bytes 262176 | tf_op jit(solution)/shard_map/ppermute | solution.py:229
  97.3 2.5 %collective-permute-done.20.r_ref = bf16[512,512]{1,0:T(8,128)(2,1)S(1)} collective-permute-done((bf16[512,512]{1,0:T(8,128)(2,1)S(1)}, bf16[512,512]{1,0:T(8,128)(2,1)S(1)}, u32[]{:S(2)}, u32[]{:S(2)}) %collective-permute-start.20) | collective-permute-done | bytes 524320 | tf_op jit(solution)/shard_map/ppermute | solution.py:239
  100.4 3.2 %collective-permute-start.28 = (bf16[512,512]{1,0:T(8,128)(2,1)S(1)}, bf16[512,512]{1,0:T(8,128)(2,1)S(1)}, u32[]{:S(2)}, u32[]{:S(2)}) collective-permute-start(bf16[512,512]{1,0:T(8,128)(2,1)S(1)} %get-tuple-element.87), channel_id=1, source_target_pairs={{0,14},{2,0},{4,2},{6,4},{8,6},{10,8},{12,10},{14,12},{1,15},{3,1}... | collective-permute-start | bytes 1572872 | tf_op jit(solution)/shard_map/ppermute | solution.py:239
  105.6 2.9 %collective-permute-done.24.a_ref = bf16[512,128]{1,0:T(8,128)(2,1)S(1)} collective-permute-done((bf16[512,128]{1,0:T(8,128)(2,1)S(1)}, bf16[512,128]{1,0:T(8,128)(2,1)S(1)}, u32[]{:S(2)}, u32[]{:S(2)}) %collective-permute-start.24) | collective-permute-done | bytes 131104 | tf_op jit(solution)/shard_map/ppermute | solution.py:233
  108.6 2.4 %collective-permute-done.25.b_ref = bf16[512,128]{1,0:T(8,128)(2,1)S(1)} collective-permute-done((bf16[512,128]{1,0:T(8,128)(2,1)S(1)}, bf16[512,128]{1,0:T(8,128)(2,1)S(1)}, u32[]{:S(2)}, u32[]{:S(2)}) %collective-permute-start.25) | collective-permute-done | bytes 131104 | tf_op jit(solution)/shard_map/ppermute | solution.py:233
  (66 shorter events, 36.7 us)
Async XLA Ops:
  0.6 4.5 %collective-permute-start = (bf16[2048,512]{1,0:T(8,128)(2,1)}, bf16[2048,512]{1,0:T(8,128)(2,1)S(1)}, u32[]{:S(2)}, u32[]{:S(2)}) collective-permute-start(bf16[2048,512]{1,0:T(8,128)(2,1)} %own_ref.1), channel_id=1, source_target_pairs={{0,1},{1,0},{2,3},{3,2},{4,5},{5,4},{6,7},{7,6},{8,9},{9,8},{10,11... | collective-permute-start | bytes 6291464 | tf_op jit(solution)/shard_map/ppermute | solution.py:243
  12.4 5.6 %collective-permute-start.3 = (bf16[256,128]{1,0:T(8,128)(2,1)S(1)}, bf16[256,128]{1,0:T(8,128)(2,1)S(1)}, u32[]{:S(2)}, u32[]{:S(2)}) collective-permute-start(bf16[256,128]{1,0:T(8,128)(2,1)S(1)} %fold.9.a_ref), channel_id=1, source_target_pairs={{0,48},{16,32},{32,16},{48,0},{64,112},{80,96},{96,80},{112,64},{1... | collective-permute-start | bytes 196616 | tf_op jit(solution)/shard_map/ppermute | solution.py:225
  18.0 4.4 %collective-permute-start.4 = (bf16[256,128]{1,0:T(8,128)(2,1)S(1)}, bf16[256,128]{1,0:T(8,128)(2,1)S(1)}, u32[]{:S(2)}, u32[]{:S(2)}) collective-permute-start(bf16[256,128]{1,0:T(8,128)(2,1)S(1)} %fold.10.a_ref), channel_id=1, source_target_pairs={{0,64},{16,80},{32,96},{48,112},{64,0},{80,16},{96,32},{112,48},{1... | collective-permute-start | bytes 196616 | tf_op jit(solution)/shard_map/ppermute | solution.py:225
  22.3 5.6 %collective-permute-start.5 = (bf16[256,128]{1,0:T(8,128)(2,1)S(1)}, bf16[256,128]{1,0:T(8,128)(2,1)S(1)}, u32[]{:S(2)}, u32[]{:S(2)}) collective-permute-start(bf16[256,128]{1,0:T(8,128)(2,1)S(1)} %fold.11), channel_id=1, source_target_pairs={{0,192},{16,208},{32,224},{48,240},{64,128},{80,144},{96,160},{112... | collective-permute-start | bytes 196616 | tf_op jit(solution)/shard_map/ppermute | solution.py:225
  31.9 4.4 %collective-permute-start.8 = (bf16[256,128]{1,0:T(8,128)(2,1)S(1)}, bf16[256,128]{1,0:T(8,128)(2,1)S(1)}, u32[]{:S(2)}, u32[]{:S(2)}) collective-permute-start(bf16[256,128]{1,0:T(8,128)(2,1)S(1)} %fold.12.a_ref), channel_id=1, source_target_pairs={{0,16},{16,0},{32,48},{48,32},{64,80},{80,64},{96,112},{112,96},{1... | collective-permute-start | bytes 196616 | tf_op jit(solution)/shard_map/ppermute | solution.py:225
  36.2 5.6 %collective-permute-start.9 = (bf16[256,128]{1,0:T(8,128)(2,1)S(1)}, bf16[256,128]{1,0:T(8,128)(2,1)S(1)}, u32[]{:S(2)}, u32[]{:S(2)}) collective-permute-start(bf16[256,128]{1,0:T(8,128)(2,1)S(1)} %fold.13.a_ref), channel_id=1, source_target_pairs={{0,48},{16,32},{32,16},{48,0},{64,112},{80,96},{96,80},{112,64},{1... | collective-permute-start | bytes 196616 | tf_op jit(solution)/shard_map/ppermute | solution.py:225
  41.8 4.4 %collective-permute-start.10 = (bf16[256,128]{1,0:T(8,128)(2,1)S(1)}, bf16[256,128]{1,0:T(8,128)(2,1)S(1)}, u32[]{:S(2)}, u32[]{:S(2)}) collective-permute-start(bf16[256,128]{1,0:T(8,128)(2,1)S(1)} %fold.14.a_ref), channel_id=1, source_target_pairs={{0,64},{16,80},{32,96},{48,112},{64,0},{80,16},{96,32},{112,48},{1... | collective-permute-start | bytes 196616 | tf_op jit(solution)/shard_map/ppermute | solution.py:225
  46.2 5.7 %collective-permute-start.11 = (bf16[256,128]{1,0:T(8,128)(2,1)S(1)}, bf16[256,128]{1,0:T(8,128)(2,1)S(1)}, u32[]{:S(2)}, u32[]{:S(2)}) collective-permute-start(bf16[256,128]{1,0:T(8,128)(2,1)S(1)} %fold.15), channel_id=1, source_target_pairs={{0,192},{16,208},{32,224},{48,240},{64,128},{80,144},{96,160},{112... | collective-permute-start | bytes 196616 | tf_op jit(solution)/shard_map/ppermute | solution.py:225
  55.7 8.6 %collective-permute-start.15 = (bf16[16,512,128]{2,1,0:T(8,128)(2,1)S(1)}, bf16[16,512,128]{2,1,0:T(8,128)(2,1)S(1)}, u32[]{:S(2)}, u32[]{:S(2)}) collective-permute-start(bf16[16,512,128]{2,1,0:T(8,128)(2,1)S(1)} %get-tuple-element.68), channel_id=1, source_target_pairs={{0,1},{1,0},{2,3},{3,2},{4,5},{5,4},{6,7},{7,6},{8,9},{9,8},{10,11... | collective-permute-start | bytes 6291464 | tf_op jit(solution)/shard_map/ppermute | solution.py:243
  55.9 12.7 %collective-permute-start.13 = (bf16[256,512]{1,0:T(8,128)(2,1)S(1)}, bf16[256,512]{1,0:T(8,128)(2,1)S(1)}, u32[]{:S(2)}, u32[]{:S(2)}) collective-permute-start(bf16[256,512]{1,0:T(8,128)(2,1)S(1)} %get-tuple-element.64), channel_id=1, source_target_pairs={{0,2},{2,4},{4,6},{6,8},{8,10},{10,12},{12,14},{14,0},{1,3},{3,5},... | collective-permute-start | bytes 786440 | tf_op jit(solution)/shard_map/ppermute | solution.py:239
  57.8 10.7 %collective-permute-start.14 = (bf16[256,512]{1,0:T(8,128)(2,1)S(1)}, bf16[256,512]{1,0:T(8,128)(2,1)S(1)}, u32[]{:S(2)}, u32[]{:S(2)}) collective-permute-start(bf16[256,512]{1,0:T(8,128)(2,1)S(1)} %get-tuple-element.65), channel_id=1, source_target_pairs={{0,14},{2,0},{4,2},{6,4},{8,6},{10,8},{12,10},{14,12},{1,15},{3,1}... | collective-permute-start | bytes 786440 | tf_op jit(solution)/shard_map/ppermute | solution.py:239
  64.7 15.2 %collective-permute-start.18 = (bf16[2,4,256,128]{3,2,1,0:T(8,128)(2,1)S(1)}, bf16[2,4,256,128]{3,2,1,0:T(8,128)(2,1)S(1)}, u32[]{:S(2)}, u32[]{:S(2)}) collective-permute-start(bf16[2,4,256,128]{3,2,1,0:T(8,128)(2,1)S(1)} %get-tuple-element.75), channel_id=1, source_target_pairs={{0,64},{16,80},{32,96},{48,112},{64,128},{80,144},{96,160},{112,17... | collective-permute-start | bytes 1572872 | tf_op jit(solution)/shard_map/ppermute | solution.py:229
  64.8 15.1 %collective-permute-start.19 = (bf16[2,4,256,128]{3,2,1,0:T(8,128)(2,1)S(1)}, bf16[2,4,256,128]{3,2,1,0:T(8,128)(2,1)S(1)}, u32[]{:S(2)}, u32[]{:S(2)}) collective-permute-start(bf16[2,4,256,128]{3,2,1,0:T(8,128)(2,1)S(1)} %get-tuple-element.77), channel_id=1, source_target_pairs={{0,192},{16,208},{32,224},{48,240},{64,0},{80,16},{96,32},{112,48}... | collective-permute-start | bytes 1572872 | tf_op jit(solution)/shard_map/ppermute | solution.py:229
  68.7 13.9 %collective-permute-start.17 = (bf16[512,512]{1,0:T(8,128)(2,1)S(1)}, bf16[512,512]{1,0:T(8,128)(2,1)S(1)}, u32[]{:S(2)}, u32[]{:S(2)}) collective-permute-start(bf16[512,512]{1,0:T(8,128)(2,1)S(1)} %get-tuple-element.72), channel_id=1, source_target_pairs={{0,14},{2,0},{4,2},{6,4},{8,6},{10,8},{12,10},{14,12},{1,15},{3,1}... | collective-permute-start | bytes 1572872 | tf_op jit(solution)/shard_map/ppermute | solution.py:239
  71.7 14.3 %collective-permute-start.16 = (bf16[512,512]{1,0:T(8,128)(2,1)S(1)}, bf16[512,512]{1,0:T(8,128)(2,1)S(1)}, u32[]{:S(2)}, u32[]{:S(2)}) collective-permute-start(bf16[512,512]{1,0:T(8,128)(2,1)S(1)} %get-tuple-element.70._), channel_id=1, source_target_pairs={{0,2},{2,4},{4,6},{6,8},{8,10},{10,12},{12,14},{14,0},{1,3},{3,5},... | collective-permute-start | bytes 1572872 | tf_op jit(solution)/shard_map/ppermute | solution.py:239
  86.4 13.4 %collective-permute-start.20 = (bf16[512,512]{1,0:T(8,128)(2,1)S(1)}, bf16[512,512]{1,0:T(8,128)(2,1)S(1)}, u32[]{:S(2)}, u32[]{:S(2)}) collective-permute-start(bf16[512,512]{1,0:T(8,128)(2,1)S(1)} %get-tuple-element.78), channel_id=1, source_target_pairs={{0,2},{2,4},{4,6},{6,8},{8,10},{10,12},{12,14},{14,0},{1,3},{3,5},... | collective-permute-start | bytes 1572872 | tf_op jit(solution)/shard_map/ppermute | solution.py:239
  86.5 13.4 %collective-permute-start.21 = (bf16[512,512]{1,0:T(8,128)(2,1)S(1)}, bf16[512,512]{1,0:T(8,128)(2,1)S(1)}, u32[]{:S(2)}, u32[]{:S(2)}) collective-permute-start(bf16[512,512]{1,0:T(8,128)(2,1)S(1)} %get-tuple-element.79), channel_id=1, source_target_pairs={{0,14},{2,0},{4,2},{6,4},{8,6},{10,8},{12,10},{14,12},{1,15},{3,1}... | collective-permute-start | bytes 1572872 | tf_op jit(solution)/shard_map/ppermute | solution.py:239
  89.7 7.6 %collective-permute-start.22 = (bf16[4,256,128]{2,1,0:T(8,128)(2,1)S(1)}, bf16[4,256,128]{2,1,0:T(8,128)(2,1)S(1)}, u32[]{:S(2)}, u32[]{:S(2)}) collective-permute-start(bf16[4,256,128]{2,1,0:T(8,128)(2,1)S(1)} %get-tuple-element.80), channel_id=1, source_target_pairs={{0,64},{16,80},{32,96},{48,112},{64,128},{80,144},{96,160},{112,17... | collective-permute-start | bytes 786440 | tf_op jit(solution)/shard_map/ppermute | solution.py:229
  89.7 7.6 %collective-permute-start.23 = (bf16[4,256,128]{2,1,0:T(8,128)(2,1)S(1)}, bf16[4,256,128]{2,1,0:T(8,128)(2,1)S(1)}, u32[]{:S(2)}, u32[]{:S(2)}) collective-permute-start(bf16[4,256,128]{2,1,0:T(8,128)(2,1)S(1)} %get-tuple-element.81), channel_id=1, source_target_pairs={{0,192},{16,208},{32,224},{48,240},{64,0},{80,16},{96,32},{112,48}... | collective-permute-start | bytes 786440 | tf_op jit(solution)/shard_map/ppermute | solution.py:229
  100.3 12.5 %collective-permute-start.27 = (bf16[512,512]{1,0:T(8,128)(2,1)S(1)}, bf16[512,512]{1,0:T(8,128)(2,1)S(1)}, u32[]{:S(2)}, u32[]{:S(2)}) collective-permute-start(bf16[512,512]{1,0:T(8,128)(2,1)S(1)} %get-tuple-element.86), channel_id=1, source_target_pairs={{0,2},{2,4},{4,6},{6,8},{8,10},{10,12},{12,14},{14,0},{1,3},{3,5},... | collective-permute-start | bytes 1572872 | tf_op jit(solution)/shard_map/ppermute | solution.py:239
  100.4 12.4 %collective-permute-start.28 = (bf16[512,512]{1,0:T(8,128)(2,1)S(1)}, bf16[512,512]{1,0:T(8,128)(2,1)S(1)}, u32[]{:S(2)}, u32[]{:S(2)}) collective-permute-start(bf16[512,512]{1,0:T(8,128)(2,1)S(1)} %get-tuple-element.87), channel_id=1, source_target_pairs={{0,14},{2,0},{4,2},{6,4},{8,6},{10,8},{12,10},{14,12},{1,15},{3,1}... | collective-permute-start | bytes 1572872 | tf_op jit(solution)/shard_map/ppermute | solution.py:239
  103.6 5.0 %collective-permute-start.24 = (bf16[512,128]{1,0:T(8,128)(2,1)S(1)}, bf16[512,128]{1,0:T(8,128)(2,1)S(1)}, u32[]{:S(2)}, u32[]{:S(2)}) collective-permute-start(bf16[512,128]{1,0:T(8,128)(2,1)S(1)} %get-tuple-element.83), channel_id=1, source_target_pairs={{0,16},{16,32},{32,48},{48,0},{64,80},{80,96},{96,112},{112,64},{1... | collective-permute-start | bytes 393224 | tf_op jit(solution)/shard_map/ppermute | solution.py:233
  104.4 6.6 %collective-permute-start.25 = (bf16[512,128]{1,0:T(8,128)(2,1)S(1)}, bf16[512,128]{1,0:T(8,128)(2,1)S(1)}, u32[]{:S(2)}, u32[]{:S(2)}) collective-permute-start(bf16[512,128]{1,0:T(8,128)(2,1)S(1)} %get-tuple-element.84), channel_id=1, source_target_pairs={{0,32},{16,48},{32,0},{48,16},{64,96},{80,112},{96,64},{112,80},{1... | collective-permute-start | bytes 393224 | tf_op jit(solution)/shard_map/ppermute | solution.py:233
  104.6 7.7 %collective-permute-start.26 = (bf16[512,128]{1,0:T(8,128)(2,1)S(1)}, bf16[512,128]{1,0:T(8,128)(2,1)S(1)}, u32[]{:S(2)}, u32[]{:S(2)}) collective-permute-start(bf16[512,128]{1,0:T(8,128)(2,1)S(1)} %get-tuple-element.85), channel_id=1, source_target_pairs={{0,48},{16,0},{32,16},{48,32},{64,112},{80,64},{96,80},{112,96},{1... | collective-permute-start | bytes 393224 | tf_op jit(solution)/shard_map/ppermute | solution.py:233
  (9 other events, 51.9 us)

commit v5 on v4

--- a/solution.py
+++ b/solution.py
@@ -188,7 +188,8 @@
         qg_ref[:, c] = (dot(cross, k_ref[:, c]) + dot(low, state_ref[c, :], NT)).astype(BF16)
         kp_ref[:, c] = dot(cross, q_ref[:, c], TN)
 
-    each_head(q_ref, head)
+    for c in heads_of(q_ref):
+        head(c)
 
 
 def chip_sum_kernel(keep_ref, got_ref, _, t_ref):
@@ -389,9 +390,12 @@
         ref[half:] = v.astype(ref.dtype)
 
 
-def last_kernel(keep_ref, a_ref, b_ref, c_ref, r_ref, l_ref, p_ref, o_ref, i_ref):
+def owner_kernel(keep_ref, a_ref, b_ref, c_ref, o_ref):
+    o_ref[...] = (keep_ref[...] + wide(a_ref) + wide(b_ref) + wide(c_ref)).T
+
+
+def last_kernel(r_ref, l_ref, p_ref, i_ref):
     i_ref[...] = (p_ref[p_ref.shape[0] - 1].astype(F32) + wide(r_ref) + wide(l_ref)).astype(BF16)
-    o_ref[...] = (keep_ref[...] + wide(a_ref) + wide(b_ref) + wide(c_ref)).T
 
 
 def local(layer_input, query_act, key_act, out_grad, value_weight):
@@ -512,13 +516,10 @@
     )
     r, l = along_z(r, 1), along_z(l, -1)
     got = [along_y_ring(m, k) for m, k in zip((m1, m2, m3), (1, 2, 3))]
-    weight_grad, input_grad = call(
-        last_kernel,
-        [VMEM] * 7,
-        [keep, *got, r, l, parts],
-        [sds((128, cols), F32), full],
-        "last",
-    )
+    (weight_grad,) = call(
+        owner_kernel, [VMEM] * 4, [keep, *got], [sds((128, cols), F32)], "owner"
+    )
+    (input_grad,) = call(last_kernel, [VMEM] * 3, [r, l, parts], [full], "last")
     return (query_grad, key_grad, input_grad, weight_grad)
 
 

time: 115 us -> 115 us (level)
    pallas_call x24 -> x25, Pallas kernels: 23.6 us -> 23.9 us  [call(): pl.pallas_call(body, out_shape=tuple(outs), in_specs=specs, out_specs=tup...]
  transfers between devices with their start and end apart: 29 -> 29, of which waited for: 23 -> 22; matrix products, arithmetic and copies ran while one was open for 0% -> 0% of each run, Pallas kernels for 14% -> 15%
where the time goes in v5:
time: 115 us; the launch traced here: 114 us
  waiting for transfers between devices  51.2 us (45%)
  starting transfers between devices  38.1 us (33%)
  Pallas kernels  23.9 us (21%)
    pallas_call x25, Pallas kernels, call(): pl.pallas_call(body, out_shape=tuple(outs), in_specs=specs, out_specs=tup...  23.9 us
    ppermute x8, waiting for transfers between devices, along(): return lax.ppermute(a, 'ctx', [(i, other(i)) for i in range(SIDE * SIDE)])  20.8 us
    ppermute x8, starting transfers between devices, along_z(): return lax.ppermute(a, 'head', [(i, (i + k) % RING) for i in range(RING)])  15.7 us
    ppermute x8, starting transfers between devices, along(): return lax.ppermute(a, 'ctx', [(i, other(i)) for i in range(SIDE * SIDE)])  12.8 us
    ppermute x8, waiting for transfers between devices, along_z(): return lax.ppermute(a, 'head', [(i, (i + k) % RING) for i in range(RING)])  9.22 us
    ppermute x4, waiting for transfers between devices, along_x_ring(): return lax.ppermute(a, 'ctx', [(i, (i + SIDE * k) % 16) for i in range(16)])  8.7 us
    ppermute x4, starting transfers between devices, along_x_ring(): return lax.ppermute(a, 'ctx', [(i, (i + SIDE * k) % 16) for i in range(16)])  6.54 us
    ppermute x3, waiting for transfers between devices, along_y_ring(): lax.ppermute(a, 'ctx', [(i, i // SIDE * SIDE + (i + k) % SIDE) for i in r...  6.34 us
  transfers between devices with their start and end apart: 29, of which 22 were waited for; matrix products, arithmetic and copies ran while one was open for 0% of the time, Pallas kernels for 15%

profile of v5, /device:TPU:24, one launch (start us, length us, event | category | flops | bytes accessed | tf_op | source)
XLA Modules:
  0.0 114.0 jit_solution(2205076588466371879)
XLA Ops:
  0.7 2.9 %value_own.1 = (bf16[512,4096]{1,0:T(8,128)(2,1)S(1)}, f32[512,512]{1,0:T(8,128)S(1)}) custom-call(bf16[512,4096]{1,0:T(8,128)(2,1)} %x_hbm.1, bf16[2048,512]{1,0:T(8,128)(2,1)} %own_ref.1), custom_call_target="tpu_custom_call" | custom-call | flops 1000 | bytes 11534336 | tf_op jit(solution)/shard_map/value_own/pallas_call | solution.py:52
  14.4 3.5 %collective-permute-done.3.b_ref.refs_3_ = bf16[256,128]{1,0:T(8,128)(2,1)S(1)} collective-permute-done((bf16[256,128]{1,0:T(8,128)(2,1)S(1)}, bf16[256,128]{1,0:T(8,128)(2,1)S(1)}, u32[]{:S(2)}, u32[]{:S(2)}) %collective-permute-start.3) | collective-permute-done | bytes 65568 | tf_op jit(solution)/shard_map/ppermute | solution.py:226
  19.5 2.8 %collective-permute-done.4.b_ref.refs_4_ = bf16[256,128]{1,0:T(8,128)(2,1)S(1)} collective-permute-done((bf16[256,128]{1,0:T(8,128)(2,1)S(1)}, bf16[256,128]{1,0:T(8,128)(2,1)S(1)}, u32[]{:S(2)}, u32[]{:S(2)}) %collective-permute-start.4) | collective-permute-done | bytes 65568 | tf_op jit(solution)/shard_map/ppermute | solution.py:226
  22.3 2.8 %collective-permute-start.5 = (bf16[256,128]{1,0:T(8,128)(2,1)S(1)}, bf16[256,128]{1,0:T(8,128)(2,1)S(1)}, u32[]{:S(2)}, u32[]{:S(2)}) collective-permute-start(bf16[256,128]{1,0:T(8,128)(2,1)S(1)} %fold.11), channel_id=1, source_target_pairs={{0,192},{16,208},{32,224},{48,240},{64,128},{80,144},{96,160},{112... | collective-permute-start | bytes 196616 | tf_op jit(solution)/shard_map/ppermute | solution.py:226
  25.2 2.7 %collective-permute-done.5.refs_5_ = bf16[256,128]{1,0:T(8,128)(2,1)S(1)} collective-permute-done((bf16[256,128]{1,0:T(8,128)(2,1)S(1)}, bf16[256,128]{1,0:T(8,128)(2,1)S(1)}, u32[]{:S(2)}, u32[]{:S(2)}) %collective-permute-start.5) | collective-permute-done | bytes 65568 | tf_op jit(solution)/shard_map/ppermute | solution.py:226
  33.8 2.4 %collective-permute-done.8.b_ref.refs_2_ = bf16[256,128]{1,0:T(8,128)(2,1)S(1)} collective-permute-done((bf16[256,128]{1,0:T(8,128)(2,1)S(1)}, bf16[256,128]{1,0:T(8,128)(2,1)S(1)}, u32[]{:S(2)}, u32[]{:S(2)}) %collective-permute-start.8) | collective-permute-done | bytes 65568 | tf_op jit(solution)/shard_map/ppermute | solution.py:226
  38.3 2.7 %cross.1 = (bf16[512,512]{1,0:T(8,128)(2,1)}, f32[512,512]{1,0:T(8,128)S(1)}) custom-call(bf16[512,512]{1,0:T(8,128)(2,1)S(1)} %copy-done.2, bf16[512,512]{1,0:T(8,128)(2,1)S(1)} %copy-done.1, bf16[512,512]{1,0:T(8,128)(2,1)S(1)} %get-tuple-element.47.v_ref, bf16[512,512]{1,0:T(8,128)(2,1)S(1)} %get-tuple-element.52.low_ref, ...), custom_call_target="tpu_custom_call" | custom-call | flops 1000 | bytes 3801088 | tf_op jit(solution)/shard_map/cross/pallas_call | solution.py:52
  42.4 4.0 %collective-permute-done.10.b_ref.refs_4_ = bf16[256,128]{1,0:T(8,128)(2,1)S(1)} collective-permute-done((bf16[256,128]{1,0:T(8,128)(2,1)S(1)}, bf16[256,128]{1,0:T(8,128)(2,1)S(1)}, u32[]{:S(2)}, u32[]{:S(2)}) %collective-permute-start.10) | collective-permute-done | bytes 65568 | tf_op jit(solution)/shard_map/ppermute | solution.py:226
  46.4 2.8 %collective-permute-start.11 = (bf16[256,128]{1,0:T(8,128)(2,1)S(1)}, bf16[256,128]{1,0:T(8,128)(2,1)S(1)}, u32[]{:S(2)}, u32[]{:S(2)}) collective-permute-start(bf16[256,128]{1,0:T(8,128)(2,1)S(1)} %fold.15), channel_id=1, source_target_pairs={{0,192},{16,208},{32,224},{48,240},{64,128},{80,144},{96,160},{112... | collective-permute-start | bytes 196616 | tf_op jit(solution)/shard_map/ppermute | solution.py:226
  49.2 2.7 %collective-permute-done.11.refs_5_ = bf16[256,128]{1,0:T(8,128)(2,1)S(1)} collective-permute-done((bf16[256,128]{1,0:T(8,128)(2,1)S(1)}, bf16[256,128]{1,0:T(8,128)(2,1)S(1)}, u32[]{:S(2)}, u32[]{:S(2)}) %collective-permute-start.11) | collective-permute-done | bytes 65568 | tf_op jit(solution)/shard_map/ppermute | solution.py:226
  57.8 3.9 %collective-permute-start.14 = (bf16[256,512]{1,0:T(8,128)(2,1)S(1)}, bf16[256,512]{1,0:T(8,128)(2,1)S(1)}, u32[]{:S(2)}, u32[]{:S(2)}) collective-permute-start(bf16[256,512]{1,0:T(8,128)(2,1)S(1)} %get-tuple-element.63), channel_id=1, source_target_pairs={{0,14},{2,0},{4,2},{6,4},{8,6},{10,8},{12,10},{14,12},{1,15},{3,1}... | collective-permute-start | bytes 786440 | tf_op jit(solution)/shard_map/ppermute | solution.py:240
  61.8 2.4 %work.1 = (bf16[2,512,512]{2,1,0:T(8,128)(2,1)S(1)}, bf16[16,512,128]{2,1,0:T(8,128)(2,1)S(1)}) custom-call(bf16[512,512]{1,0:T(8,128)(2,1)S(1)} %get-tuple-element.61.refs_0_.vg_ref, bf16[2048,512]{1,0:T(8,128)(2,1)S(1)} %copy-done, bf16[2048,512]{1,0:T(8,128)(2,1)S(1)} %collective-permute-done.w_ref.refs_5_.refs_2_.other_ref, ...), custom_call_target="tpu_custom_call" | custom-call | flops 1000 | bytes 12058624 | tf_op jit(solution)/shard_map/work/pallas_call | solution.py:52
  64.8 3.2 %collective-permute-start.19 = (bf16[2,4,256,128]{3,2,1,0:T(8,128)(2,1)S(1)}, bf16[2,4,256,128]{3,2,1,0:T(8,128)(2,1)S(1)}, u32[]{:S(2)}, u32[]{:S(2)}) collective-permute-start(bf16[2,4,256,128]{3,2,1,0:T(8,128)(2,1)S(1)} %get-tuple-element.75), channel_id=1, source_target_pairs={{0,192},{16,208},{32,224},{48,240},{64,0},{80,16},{96,32},{112,48}... | collective-permute-start | bytes 1572872 | tf_op jit(solution)/shard_map/ppermute | solution.py:230
  68.7 3.0 %collective-permute-start.17 = (bf16[512,512]{1,0:T(8,128)(2,1)S(1)}, bf16[512,512]{1,0:T(8,128)(2,1)S(1)}, u32[]{:S(2)}, u32[]{:S(2)}) collective-permute-start(bf16[512,512]{1,0:T(8,128)(2,1)S(1)} %get-tuple-element.70), channel_id=1, source_target_pairs={{0,14},{2,0},{4,2},{6,4},{8,6},{10,8},{12,10},{14,12},{1,15},{3,1}... | collective-permute-start | bytes 1572872 | tf_op jit(solution)/shard_map/ppermute | solution.py:240
  71.7 3.8 %key_grad.1 = (bf16[512,512]{1,0:T(8,128)(2,1)}, bf16[5,512,512]{2,1,0:T(8,128)(2,1)S(1)}) custom-call(bf16[512,512]{1,0:T(8,128)(2,1)S(1)} %get-tuple-element.47.v_ref, f32[512,512]{1,0:T(8,128)S(1)} %get-tuple-element.55._.kp_ref, bf16[512,128]{1,0:T(8,128)(2,1)S(1)} %get-tuple-element.60.state_ref, bf16[512,512]{1,0:T(8,128)(2,1)S(1)} %get-tuple-element.61.refs_0_.vg_ref, ...), custom_call_target="tpu_custom_call" | custom-call | flops 1000 | bytes 10092544 | tf_op jit(solution)/shard_map/key_grad/pallas_call | solution.py:52
  75.5 4.3 %collective-permute-done.18.b_ref.right_ref = bf16[2,4,256,128]{3,2,1,0:T(8,128)(2,1)S(1)} collective-permute-done((bf16[2,4,256,128]{3,2,1,0:T(8,128)(2,1)S(1)}, bf16[2,4,256,128]{3,2,1,0:T(8,128)(2,1)S(1)}, u32[]{:S(2)}, u32[]{:S(2)}) %collective-permute-start.18) | collective-permute-done | bytes 524320 | tf_op jit(solution)/shard_map/ppermute | solution.py:230
  79.9 2.7 %collective-permute-done.17.l_ref = bf16[512,512]{1,0:T(8,128)(2,1)S(1)} collective-permute-done((bf16[512,512]{1,0:T(8,128)(2,1)S(1)}, bf16[512,512]{1,0:T(8,128)(2,1)S(1)}, u32[]{:S(2)}, u32[]{:S(2)}) %collective-permute-start.17) | collective-permute-done | bytes 524320 | tf_op jit(solution)/shard_map/ppermute | solution.py:240
  82.6 3.4 %collective-permute-done.16.r_ref = bf16[512,512]{1,0:T(8,128)(2,1)S(1)} collective-permute-done((bf16[512,512]{1,0:T(8,128)(2,1)S(1)}, bf16[512,512]{1,0:T(8,128)(2,1)S(1)}, u32[]{:S(2)}, u32[]{:S(2)}) %collective-permute-start.16) | collective-permute-done | bytes 524320 | tf_op jit(solution)/shard_map/ppermute | solution.py:240
  86.7 3.2 %collective-permute-start.21 = (bf16[512,512]{1,0:T(8,128)(2,1)S(1)}, bf16[512,512]{1,0:T(8,128)(2,1)S(1)}, u32[]{:S(2)}, u32[]{:S(2)}) collective-permute-start(bf16[512,512]{1,0:T(8,128)(2,1)S(1)} %get-tuple-element.77), channel_id=1, source_target_pairs={{0,14},{2,0},{4,2},{6,4},{8,6},{10,8},{12,10},{14,12},{1,15},{3,1}... | collective-permute-start | bytes 1572872 | tf_op jit(solution)/shard_map/ppermute | solution.py:240
  89.9 3.2 %collective-permute-start.23 = (bf16[4,256,128]{2,1,0:T(8,128)(2,1)S(1)}, bf16[4,256,128]{2,1,0:T(8,128)(2,1)S(1)}, u32[]{:S(2)}, u32[]{:S(2)}) collective-permute-start(bf16[4,256,128]{2,1,0:T(8,128)(2,1)S(1)} %get-tuple-element.79), channel_id=1, source_target_pairs={{0,192},{16,208},{32,224},{48,240},{64,0},{80,16},{96,32},{112,48}... | collective-permute-start | bytes 786440 | tf_op jit(solution)/shard_map/ppermute | solution.py:230
  93.2 4.3 %collective-permute-done.22.ru_ref = bf16[4,256,128]{2,1,0:T(8,128)(2,1)S(1)} collective-permute-done((bf16[4,256,128]{2,1,0:T(8,128)(2,1)S(1)}, bf16[4,256,128]{2,1,0:T(8,128)(2,1)S(1)}, u32[]{:S(2)}, u32[]{:S(2)}) %collective-permute-start.22) | collective-permute-done | bytes 262176 | tf_op jit(solution)/shard_map/ppermute | solution.py:230
  97.5 2.5 %collective-permute-done.20.r_ref = bf16[512,512]{1,0:T(8,128)(2,1)S(1)} collective-permute-done((bf16[512,512]{1,0:T(8,128)(2,1)S(1)}, bf16[512,512]{1,0:T(8,128)(2,1)S(1)}, u32[]{:S(2)}, u32[]{:S(2)}) %collective-permute-start.20) | collective-permute-done | bytes 524320 | tf_op jit(solution)/shard_map/ppermute | solution.py:240
  100.6 3.2 %collective-permute-start.25 = (bf16[512,512]{1,0:T(8,128)(2,1)S(1)}, bf16[512,512]{1,0:T(8,128)(2,1)S(1)}, u32[]{:S(2)}, u32[]{:S(2)}) collective-permute-start(bf16[512,512]{1,0:T(8,128)(2,1)S(1)} %get-tuple-element.81), channel_id=1, source_target_pairs={{0,14},{2,0},{4,2},{6,4},{8,6},{10,8},{12,10},{14,12},{1,15},{3,1}... | collective-permute-start | bytes 1572872 | tf_op jit(solution)/shard_map/ppermute | solution.py:240
  105.8 2.9 %collective-permute-done.26.a_ref = bf16[512,128]{1,0:T(8,128)(2,1)S(1)} collective-permute-done((bf16[512,128]{1,0:T(8,128)(2,1)S(1)}, bf16[512,128]{1,0:T(8,128)(2,1)S(1)}, u32[]{:S(2)}, u32[]{:S(2)}) %collective-permute-start.26) | collective-permute-done | bytes 131104 | tf_op jit(solution)/shard_map/ppermute | solution.py:234
  (67 shorter events, 37.2 us)
Async XLA Ops:
  0.6 4.5 %collective-permute-start = (bf16[2048,512]{1,0:T(8,128)(2,1)}, bf16[2048,512]{1,0:T(8,128)(2,1)S(1)}, u32[]{:S(2)}, u32[]{:S(2)}) collective-permute-start(bf16[2048,512]{1,0:T(8,128)(2,1)} %own_ref.1), channel_id=1, source_target_pairs={{0,1},{1,0},{2,3},{3,2},{4,5},{5,4},{6,7},{7,6},{8,9},{9,8},{10,11... | collective-permute-start | bytes 6291464 | tf_op jit(solution)/shard_map/ppermute | solution.py:244
  12.4 5.6 %collective-permute-start.3 = (bf16[256,128]{1,0:T(8,128)(2,1)S(1)}, bf16[256,128]{1,0:T(8,128)(2,1)S(1)}, u32[]{:S(2)}, u32[]{:S(2)}) collective-permute-start(bf16[256,128]{1,0:T(8,128)(2,1)S(1)} %fold.9.a_ref), channel_id=1, source_target_pairs={{0,48},{16,32},{32,16},{48,0},{64,112},{80,96},{96,80},{112,64},{1... | collective-permute-start | bytes 196616 | tf_op jit(solution)/shard_map/ppermute | solution.py:226
  18.0 4.4 %collective-permute-start.4 = (bf16[256,128]{1,0:T(8,128)(2,1)S(1)}, bf16[256,128]{1,0:T(8,128)(2,1)S(1)}, u32[]{:S(2)}, u32[]{:S(2)}) collective-permute-start(bf16[256,128]{1,0:T(8,128)(2,1)S(1)} %fold.10.a_ref), channel_id=1, source_target_pairs={{0,64},{16,80},{32,96},{48,112},{64,0},{80,16},{96,32},{112,48},{1... | collective-permute-start | bytes 196616 | tf_op jit(solution)/shard_map/ppermute | solution.py:226
  22.3 5.6 %collective-permute-start.5 = (bf16[256,128]{1,0:T(8,128)(2,1)S(1)}, bf16[256,128]{1,0:T(8,128)(2,1)S(1)}, u32[]{:S(2)}, u32[]{:S(2)}) collective-permute-start(bf16[256,128]{1,0:T(8,128)(2,1)S(1)} %fold.11), channel_id=1, source_target_pairs={{0,192},{16,208},{32,224},{48,240},{64,128},{80,144},{96,160},{112... | collective-permute-start | bytes 196616 | tf_op jit(solution)/shard_map/ppermute | solution.py:226
  31.9 4.4 %collective-permute-start.8 = (bf16[256,128]{1,0:T(8,128)(2,1)S(1)}, bf16[256,128]{1,0:T(8,128)(2,1)S(1)}, u32[]{:S(2)}, u32[]{:S(2)}) collective-permute-start(bf16[256,128]{1,0:T(8,128)(2,1)S(1)} %fold.12.a_ref), channel_id=1, source_target_pairs={{0,16},{16,0},{32,48},{48,32},{64,80},{80,64},{96,112},{112,96},{1... | collective-permute-start | bytes 196616 | tf_op jit(solution)/shard_map/ppermute | solution.py:226
  36.2 5.6 %collective-permute-start.9 = (bf16[256,128]{1,0:T(8,128)(2,1)S(1)}, bf16[256,128]{1,0:T(8,128)(2,1)S(1)}, u32[]{:S(2)}, u32[]{:S(2)}) collective-permute-start(bf16[256,128]{1,0:T(8,128)(2,1)S(1)} %fold.13.a_ref), channel_id=1, source_target_pairs={{0,48},{16,32},{32,16},{48,0},{64,112},{80,96},{96,80},{112,64},{1... | collective-permute-start | bytes 196616 | tf_op jit(solution)/shard_map/ppermute | solution.py:226
  41.8 4.5 %collective-permute-start.10 = (bf16[256,128]{1,0:T(8,128)(2,1)S(1)}, bf16[256,128]{1,0:T(8,128)(2,1)S(1)}, u32[]{:S(2)}, u32[]{:S(2)}) collective-permute-start(bf16[256,128]{1,0:T(8,128)(2,1)S(1)} %fold.14.a_ref), channel_id=1, source_target_pairs={{0,64},{16,80},{32,96},{48,112},{64,0},{80,16},{96,32},{112,48},{1... | collective-permute-start | bytes 196616 | tf_op jit(solution)/shard_map/ppermute | solution.py:226
  46.4 5.6 %collective-permute-start.11 = (bf16[256,128]{1,0:T(8,128)(2,1)S(1)}, bf16[256,128]{1,0:T(8,128)(2,1)S(1)}, u32[]{:S(2)}, u32[]{:S(2)}) collective-permute-start(bf16[256,128]{1,0:T(8,128)(2,1)S(1)} %fold.15), channel_id=1, source_target_pairs={{0,192},{16,208},{32,224},{48,240},{64,128},{80,144},{96,160},{112... | collective-permute-start | bytes 196616 | tf_op jit(solution)/shard_map/ppermute | solution.py:226
  55.7 8.6 %collective-permute-start.15 = (bf16[16,512,128]{2,1,0:T(8,128)(2,1)S(1)}, bf16[16,512,128]{2,1,0:T(8,128)(2,1)S(1)}, u32[]{:S(2)}, u32[]{:S(2)}) collective-permute-start(bf16[16,512,128]{2,1,0:T(8,128)(2,1)S(1)} %get-tuple-element.66), channel_id=1, source_target_pairs={{0,1},{1,0},{2,3},{3,2},{4,5},{5,4},{6,7},{7,6},{8,9},{9,8},{10,11... | collective-permute-start | bytes 6291464 | tf_op jit(solution)/shard_map/ppermute | solution.py:244
  55.9 12.7 %collective-permute-start.13 = (bf16[256,512]{1,0:T(8,128)(2,1)S(1)}, bf16[256,512]{1,0:T(8,128)(2,1)S(1)}, u32[]{:S(2)}, u32[]{:S(2)}) collective-permute-start(bf16[256,512]{1,0:T(8,128)(2,1)S(1)} %get-tuple-element.62), channel_id=1, source_target_pairs={{0,2},{2,4},{4,6},{6,8},{8,10},{10,12},{12,14},{14,0},{1,3},{3,5},... | collective-permute-start | bytes 786440 | tf_op jit(solution)/shard_map/ppermute | solution.py:240
  57.8 10.7 %collective-permute-start.14 = (bf16[256,512]{1,0:T(8,128)(2,1)S(1)}, bf16[256,512]{1,0:T(8,128)(2,1)S(1)}, u32[]{:S(2)}, u32[]{:S(2)}) collective-permute-start(bf16[256,512]{1,0:T(8,128)(2,1)S(1)} %get-tuple-element.63), channel_id=1, source_target_pairs={{0,14},{2,0},{4,2},{6,4},{8,6},{10,8},{12,10},{14,12},{1,15},{3,1}... | collective-permute-start | bytes 786440 | tf_op jit(solution)/shard_map/ppermute | solution.py:240
  64.7 15.2 %collective-permute-start.18 = (bf16[2,4,256,128]{3,2,1,0:T(8,128)(2,1)S(1)}, bf16[2,4,256,128]{3,2,1,0:T(8,128)(2,1)S(1)}, u32[]{:S(2)}, u32[]{:S(2)}) collective-permute-start(bf16[2,4,256,128]{3,2,1,0:T(8,128)(2,1)S(1)} %get-tuple-element.73), channel_id=1, source_target_pairs={{0,64},{16,80},{32,96},{48,112},{64,128},{80,144},{96,160},{112,17... | collective-permute-start | bytes 1572872 | tf_op jit(solution)/shard_map/ppermute | solution.py:230
  64.8 15.1 %collective-permute-start.19 = (bf16[2,4,256,128]{3,2,1,0:T(8,128)(2,1)S(1)}, bf16[2,4,256,128]{3,2,1,0:T(8,128)(2,1)S(1)}, u32[]{:S(2)}, u32[]{:S(2)}) collective-permute-start(bf16[2,4,256,128]{3,2,1,0:T(8,128)(2,1)S(1)} %get-tuple-element.75), channel_id=1, source_target_pairs={{0,192},{16,208},{32,224},{48,240},{64,0},{80,16},{96,32},{112,48}... | collective-permute-start | bytes 1572872 | tf_op jit(solution)/shard_map/ppermute | solution.py:230
  68.7 13.9 %collective-permute-start.17 = (bf16[512,512]{1,0:T(8,128)(2,1)S(1)}, bf16[512,512]{1,0:T(8,128)(2,1)S(1)}, u32[]{:S(2)}, u32[]{:S(2)}) collective-permute-start(bf16[512,512]{1,0:T(8,128)(2,1)S(1)} %get-tuple-element.70), channel_id=1, source_target_pairs={{0,14},{2,0},{4,2},{6,4},{8,6},{10,8},{12,10},{14,12},{1,15},{3,1}... | collective-permute-start | bytes 1572872 | tf_op jit(solution)/shard_map/ppermute | solution.py:240
  71.7 14.3 %collective-permute-start.16 = (bf16[512,512]{1,0:T(8,128)(2,1)S(1)}, bf16[512,512]{1,0:T(8,128)(2,1)S(1)}, u32[]{:S(2)}, u32[]{:S(2)}) collective-permute-start(bf16[512,512]{1,0:T(8,128)(2,1)S(1)} %get-tuple-element.68._), channel_id=1, source_target_pairs={{0,2},{2,4},{4,6},{6,8},{8,10},{10,12},{12,14},{14,0},{1,3},{3,5},... | collective-permute-start | bytes 1572872 | tf_op jit(solution)/shard_map/ppermute | solution.py:240
  86.4 13.7 %collective-permute-start.20 = (bf16[512,512]{1,0:T(8,128)(2,1)S(1)}, bf16[512,512]{1,0:T(8,128)(2,1)S(1)}, u32[]{:S(2)}, u32[]{:S(2)}) collective-permute-start(bf16[512,512]{1,0:T(8,128)(2,1)S(1)} %get-tuple-element.76), channel_id=1, source_target_pairs={{0,2},{2,4},{4,6},{6,8},{8,10},{10,12},{12,14},{14,0},{1,3},{3,5},... | collective-permute-start | bytes 1572872 | tf_op jit(solution)/shard_map/ppermute | solution.py:240
  86.7 13.4 %collective-permute-start.21 = (bf16[512,512]{1,0:T(8,128)(2,1)S(1)}, bf16[512,512]{1,0:T(8,128)(2,1)S(1)}, u32[]{:S(2)}, u32[]{:S(2)}) collective-permute-start(bf16[512,512]{1,0:T(8,128)(2,1)S(1)} %get-tuple-element.77), channel_id=1, source_target_pairs={{0,14},{2,0},{4,2},{6,4},{8,6},{10,8},{12,10},{14,12},{1,15},{3,1}... | collective-permute-start | bytes 1572872 | tf_op jit(solution)/shard_map/ppermute | solution.py:240
  89.9 7.6 %collective-permute-start.22 = (bf16[4,256,128]{2,1,0:T(8,128)(2,1)S(1)}, bf16[4,256,128]{2,1,0:T(8,128)(2,1)S(1)}, u32[]{:S(2)}, u32[]{:S(2)}) collective-permute-start(bf16[4,256,128]{2,1,0:T(8,128)(2,1)S(1)} %get-tuple-element.78), channel_id=1, source_target_pairs={{0,64},{16,80},{32,96},{48,112},{64,128},{80,144},{96,160},{112,17... | collective-permute-start | bytes 786440 | tf_op jit(solution)/shard_map/ppermute | solution.py:230
  89.9 7.6 %collective-permute-start.23 = (bf16[4,256,128]{2,1,0:T(8,128)(2,1)S(1)}, bf16[4,256,128]{2,1,0:T(8,128)(2,1)S(1)}, u32[]{:S(2)}, u32[]{:S(2)}) collective-permute-start(bf16[4,256,128]{2,1,0:T(8,128)(2,1)S(1)} %get-tuple-element.79), channel_id=1, source_target_pairs={{0,192},{16,208},{32,224},{48,240},{64,0},{80,16},{96,32},{112,48}... | collective-permute-start | bytes 786440 | tf_op jit(solution)/shard_map/ppermute | solution.py:230
  100.5 12.5 %collective-permute-start.24 = (bf16[512,512]{1,0:T(8,128)(2,1)S(1)}, bf16[512,512]{1,0:T(8,128)(2,1)S(1)}, u32[]{:S(2)}, u32[]{:S(2)}) collective-permute-start(bf16[512,512]{1,0:T(8,128)(2,1)S(1)} %get-tuple-element.80), channel_id=1, source_target_pairs={{0,2},{2,4},{4,6},{6,8},{8,10},{10,12},{12,14},{14,0},{1,3},{3,5},... | collective-permute-start | bytes 1572872 | tf_op jit(solution)/shard_map/ppermute | solution.py:240
  100.6 12.4 %collective-permute-start.25 = (bf16[512,512]{1,0:T(8,128)(2,1)S(1)}, bf16[512,512]{1,0:T(8,128)(2,1)S(1)}, u32[]{:S(2)}, u32[]{:S(2)}) collective-permute-start(bf16[512,512]{1,0:T(8,128)(2,1)S(1)} %get-tuple-element.81), channel_id=1, source_target_pairs={{0,14},{2,0},{4,2},{6,4},{8,6},{10,8},{12,10},{14,12},{1,15},{3,1}... | collective-permute-start | bytes 1572872 | tf_op jit(solution)/shard_map/ppermute | solution.py:240
  103.8 5.0 %collective-permute-start.26 = (bf16[512,128]{1,0:T(8,128)(2,1)S(1)}, bf16[512,128]{1,0:T(8,128)(2,1)S(1)}, u32[]{:S(2)}, u32[]{:S(2)}) collective-permute-start(bf16[512,128]{1,0:T(8,128)(2,1)S(1)} %get-tuple-element.83), channel_id=1, source_target_pairs={{0,16},{16,32},{32,48},{48,0},{64,80},{80,96},{96,112},{112,64},{1... | collective-permute-start | bytes 393224 | tf_op jit(solution)/shard_map/ppermute | solution.py:234
  104.3 6.5 %collective-permute-start.27 = (bf16[512,128]{1,0:T(8,128)(2,1)S(1)}, bf16[512,128]{1,0:T(8,128)(2,1)S(1)}, u32[]{:S(2)}, u32[]{:S(2)}) collective-permute-start(bf16[512,128]{1,0:T(8,128)(2,1)S(1)} %get-tuple-element.84), channel_id=1, source_target_pairs={{0,32},{16,48},{32,0},{48,16},{64,96},{80,112},{96,64},{112,80},{1... | collective-permute-start | bytes 393224 | tf_op jit(solution)/shard_map/ppermute | solution.py:234
  104.8 7.3 %collective-permute-start.28 = (bf16[512,128]{1,0:T(8,128)(2,1)S(1)}, bf16[512,128]{1,0:T(8,128)(2,1)S(1)}, u32[]{:S(2)}, u32[]{:S(2)}) collective-permute-start(bf16[512,128]{1,0:T(8,128)(2,1)S(1)} %get-tuple-element.85), channel_id=1, source_target_pairs={{0,48},{16,0},{32,16},{48,32},{64,112},{80,64},{96,80},{112,96},{1... | collective-permute-start | bytes 393224 | tf_op jit(solution)/shard_map/ppermute | solution.py:234
  (9 other events, 51.9 us)
